TPU v7x, 256 devices: a whole 4x4x8 slice. The times are simulated.
256 devices in a mesh: stream: 32 (over z, y_lo, core), slab: 8 (over y_hi, x).
Axes of the slice: x: 4, y: 4 (y_hi: 2, y_lo: 2; y = y_hi * 2 + y_lo), z: 8, core: 2. Of those that a mesh axis runs over, the one named last changes fastest.
Arguments:
- conc: float32 [2, 64, 64, 4096], P(None, 'slab', None, 'stream'), may hold values from -6 to 6
- kappa: float32 [2, 64, 64, 4096], P(None, 'slab', None, 'stream'), may hold values from 0.01 to 0.1
- velocity: float32 [64, 64, 4096], P('slab', None, 'stream'), may hold values from 0.02 to 0.2
- cell_type: int32 [64, 64, 4096], P('slab', None, 'stream'), may hold values 0 or 1
- target_row: int32 [2, 64, 4096], P(None, None, 'stream'), may hold values from 0 to 63, as said below
- target_col: int32 [2, 64, 4096], P(None, None, 'stream'), may hold values from 0 to 4095, as said below
- mortar_weight: float32 [2, 64, 4096], P(None, None, 'stream'), may hold values from 0.3 to 1
Outputs:
- final: float32 [2, 64, 64, 4096], P(None, 'slab', None, 'stream')
Inputs may be any that keep to these rules, and one draw needn't show every extreme that they name: target_row lies within one cell of the face's lateral index. target_col lies within one cell of the face's streamwise index.
All inputs are finite; a program needn't handle non-finite values. No bound on the sum of `cell_type` on one device may be relied on, other than what follows from the above.
Results may differ from a plain program's by a relative error of at most 0.0001.
Values sent between devices are 32-bit elements; how exact they have to be, the bound alone decides.
No kernel may reach another device: no remote copies, remote signals or barrier semaphores. Data moves between devices by JAX's collectives and lax.ppermute only.
A program may use at most 128 MiB of HBM per device.

v0:
```python
import jax
import jax.numpy as jnp
from jax import lax
from jax.sharding import PartitionSpec as P

STEPS = 3


def extended(cells, sides, width):
    for axis, dim in sides:
        count = lax.axis_size(axis)
        ends = count - 1
        head = lax.slice_in_dim(cells, 0, width, axis=dim)
        tail = lax.slice_in_dim(cells, cells.shape[dim] - width, cells.shape[dim], axis=dim)
        cells = jnp.concatenate(
            [
                lax.ppermute(tail, axis, [(i, (i + 1) % count) for i in range(ends)]),
                cells,
                lax.ppermute(head, axis, [((i + 1) % count, i) for i in range(ends)]),
            ],
            axis=dim,
        )
    return cells


def from_behind(value, axis, steps):
    count = lax.axis_size(axis)
    leading, last = (max(0, -steps), min(count, count - steps))
    return lax.ppermute(value, axis, [(source, source + steps) for source in range(leading, last)])


def transport(pc, pk, pu):
    cx = pc[:, 1:-1]
    kx = pk[:, 1:-1]
    fx = 0.5 * (kx[..., 1:] + kx[..., :-1]) * (cx[..., 1:] - cx[..., :-1])
    diff_x = fx[..., 1:] - fx[..., :-1]
    cz = pc[..., 1:-1]
    kz = pk[..., 1:-1]
    fz = 0.5 * (kz[:, 1:] + kz[:, :-1]) * (cz[:, 1:] - cz[:, :-1])
    diff_z = fz[:, 1:] - fz[:, :-1]
    cell = pc[:, 1:-1, :, 1:-1]
    kcell = pk[:, 1:-1, :, 1:-1]
    fy = 0.5 * (kcell[:, :, 1:] + kcell[:, :, :-1]) * (cell[:, :, 1:] - cell[:, :, :-1])
    zero_row = jnp.zeros_like(fy[:, :, :1])
    diff_y = jnp.concatenate([fy, zero_row], 2) - jnp.concatenate([zero_row, fy], 2)
    carried = pu[None, 1:-1] * pc[:, 1:-1]
    advect = carried[..., :-2] - carried[..., 1:-1]
    return diff_x + diff_y + diff_z + advect


def face_flux(water, bed_wide, offsets, weights, rates):
    rows = water.shape[-2]
    count = water.shape[-1]
    lead = [(0, 0)] * (water.ndim - 2)
    padded = jnp.pad(bed_wide, lead + [(1, 1), (0, 0)])
    totals = [jnp.zeros_like(water), jnp.zeros_like(water)]
    for shift_a in (-1, 0, 1):
        for shift_b in (-1, 0, 1):
            moved = padded[..., 1 + shift_a : 1 + shift_a + rows, 1 + shift_b : 1 + shift_b + count]
            for intersection in range(2):
                hit = (
                    (offsets[intersection] == shift_a) & (offsets[2 + intersection] == shift_b)
                ).astype(water.dtype)
                totals[intersection] = totals[intersection] + hit * moved
    scale = rates.reshape((rates.shape[0],) + (1,) * (water.ndim - 1))
    parts = [
        scale * weights[intersection] * (water - totals[intersection]) for intersection in range(2)
    ]
    return jnp.stack(parts, 1)


def spread(flux, offsets):
    rows = flux.shape[-2]
    count = flux.shape[-1]
    lead = [(0, 0)] * (flux.ndim - 3)
    wide = jnp.zeros(flux.shape[:1] + flux.shape[2:-1] + (count + 2,), flux.dtype)
    for shift_a in (-1, 0, 1):
        for shift_b in (-1, 0, 1):
            part = jnp.zeros_like(flux[:, 0])
            for intersection in range(2):
                hit = (
                    (offsets[intersection] == shift_a) & (offsets[2 + intersection] == shift_b)
                ).astype(flux.dtype)
                part = part + hit * flux[:, intersection]
            moved = jnp.pad(part, lead + [(1, 1), (0, 0)])[..., 1 - shift_a : 1 - shift_a + rows, :]
            wide = wide + jnp.pad(moved, lead + [(0, 0), (1 + shift_b, 1 - shift_b)])
    return wide


def per_device(conc, kappa, velocity, cell_type, target_row, target_col, mortar_weight):
    rates = jnp.array([0.08, 0.12], jnp.float32)
    active = cell_type.astype(jnp.float32)
    depth = conc.shape[1]
    lateral = conc.shape[2]
    width = conc.shape[3]
    slab_pos = lax.axis_index("slab")
    slab_count = lax.axis_size("slab")
    water_flag = (slab_pos < slab_count - 1).astype(jnp.float32)
    bed_flag = (slab_pos > 0).astype(jnp.float32)
    start_col = lax.axis_index("stream") * width
    row_off = (target_row - jnp.arange(lateral, dtype=jnp.int32)[None, :, None]).astype(jnp.float32)
    col_off = (target_col - start_col - jnp.arange(width, dtype=jnp.int32)[None, None, :]).astype(
        jnp.float32
    )
    faces = jnp.concatenate([row_off, col_off, mortar_weight], 0)
    coef_pad = extended(
        jnp.concatenate([kappa, velocity[None]], 0), (("stream", 3), ("slab", 1)), 1
    )
    pk = coef_pad[0:2]
    pu = coef_pad[2]
    for step in range(STEPS):
        pc = extended(conc, (("stream", 3), ("slab", 1)), 1)
        delta = transport(pc, pk, pu)
        water = conc[:, depth - 1]
        flux = face_flux(water, pc[:, depth + 1], faces[0:4], faces[4:6], rates)
        loss = jnp.sum(flux, axis=1) * water_flag
        wide = spread(flux, faces[0:4]) * water_flag
        arrived = from_behind(wide, "slab", 1)
        from_left = from_behind(arrived[:, :, width + 1], "stream", 1)
        from_right = from_behind(arrived[:, :, 0], "stream", -1)
        gain = arrived[:, :, 1 : width + 1]
        gain = gain.at[:, :, 0].add(from_left).at[:, :, width - 1].add(from_right)
        gain = gain * bed_flag
        delta = delta.at[:, depth - 1].add(-loss).at[:, 0].add(gain)
        conc = conc + active[None] * delta
    return conc


def solution(mesh):
    return jax.shard_map(
        per_device,
        mesh=mesh,
        in_specs=(
            P(None, "slab", None, "stream"),
            P(None, "slab", None, "stream"),
            P("slab", None, "stream"),
            P("slab", None, "stream"),
            P(None, None, "stream"),
            P(None, None, "stream"),
            P(None, None, "stream"),
        ),
        out_specs=P(None, "slab", None, "stream"),
        check_vma=False,
    )
```

profile of v0, /device:TPU:121, one launch (start us, length us, event | category | flops | bytes accessed | tf_op | source)
XLA Modules:
  0.0 195.5 jit_solution(6207632736299081237)
XLA Ops:
  0.0 1.7 fusion.6
  2.0 2.7 %collective-permute-start = (f32[3,8,64,1]{2,1,3,0:T(8,128)S(1)}, f32[3,8,64,1]{2,1,3,0:T(8,128)S(1)}, u32[]{:S(2)}, u32[]{:S(2)}) collective-permute-start(f32[3,8,64,1]{2,1,3,0:T(8,128)S(1)} %copy.125), channel_id=1, source_target_pairs={{8,0},{16,8},{24,16},{32,24},{40,32},{48,40},{56,48},{64,56},{72,6... | collective-permute-start | bytes 18440 | tf_op jit(solution)/shard_map/ppermute | solution.py:19
  5.0 5.2 %collective-permute-start.1 = (f32[3,8,64,1]{2,1,3,0:T(8,128)S(1)}, f32[3,8,64,1]{2,1,3,0:T(8,128)}, u32[]{:S(2)}, u32[]{:S(2)}) collective-permute-start(f32[3,8,64,1]{2,1,3,0:T(8,128)S(1)} %copy.127), channel_id=1, source_target_pairs={{0,8},{8,16},{16,24},{24,32},{32,40},{40,48},{48,56},{56,64},{64,7... | collective-permute-start | bytes 18440 | tf_op jit(solution)/shard_map/ppermute | solution.py:17
  10.3 1.1 fusion.44
  11.4 1.9 collective-permute-start.2
  13.3 5.8 %collective-permute-start.3 = (f32[2,8,64,1]{3,2,0,1:T(8,128)}, f32[2,8,64,1]{3,2,0,1:T(8,128)}, u32[]{:S(2)}, u32[]{:S(2)}) collective-permute-start(f32[2,8,64,1]{3,2,0,1:T(8,128)} %get-tuple-element.208), channel_id=1, source_target_pairs={{0,8},{8,16},{16,24},{24,32},{32,40},{40,48},{48,56},{56,64},{64,7... | collective-permute-start | bytes 12296 | tf_op jit(solution)/shard_map/ppermute | solution.py:17
  19.1 0.9 pad_maximum_fusion
  20.2 0.7 copy-done.64
  20.9 0.8 copy-done.65
  22.4 0.7 convert_bitcast_fusion.14
  24.7 0.7 convert_element_type.90
  25.7 1.0 copy.137
  27.0 1.0 pad_maximum_fusion.35
  28.0 2.7 %broadcast_multiply_fusion.2 = (f32[2,8,64,130]{3,2,0,1:T(8,128)}, f32[2,8,64,130]{3,2,0,1:T(8,128)S(1)}) fusion(f32[8,64,130]{2,1,0:T(8,128)S(1)} %fusion.23, f32[2,8,64,1]{3,2,0,1:T(8,128)} %collective-permute-done.2, f32[2,8,64,1]{3,2,0,1:T(8,128)} %collective-permute-done.3, f32[2,8,64,128]{3,2,1,0:T(8,128)S(1)} %copy-done.1), kind=kLoop, calls=%fused_computation.88 | loop fusion | flops 399360 | bytes 1863680 | tf_op jit(solution)/shard_map/mul | solution.py:46
  30.7 0.7 fusion.41
  31.4 3.1 %collective-permute-start.7 = (f32[2,1,64,130]{3,2,0,1:T(8,128)}, f32[2,1,64,130]{3,2,0,1:T(8,128)}, u32[]{:S(2)}, u32[]{:S(2)}) collective-permute-start(f32[2,1,64,130]{3,2,0,1:T(8,128)} %get-tuple-element.201), channel_id=1, source_target_pairs={{0,1},{1,2},{2,3},{3,4},{4,5},{5,6},{6,7},{8,9},{9,10},{10,11},{11... | collective-permute-start | bytes 199688 | tf_op jit(solution)/shard_map/ppermute | solution.py:17
  34.5 5.8 %collective-permute-start.6 = (f32[2,1,64,130]{3,2,0,1:T(8,128)}, f32[2,1,64,130]{3,2,0,1:T(8,128)}, u32[]{:S(2)}, u32[]{:S(2)}) collective-permute-start(f32[2,1,64,130]{3,2,0,1:T(8,128)} %get-tuple-element.200), channel_id=1, source_target_pairs={{1,0},{2,1},{3,2},{4,3},{5,4},{6,5},{7,6},{9,8},{10,9},{11,10},{12... | collective-permute-start | bytes 199688 | tf_op jit(solution)/shard_map/ppermute | solution.py:19
  40.3 1.9 collective-permute-start.5
  42.2 7.0 %collective-permute-start.4 = (f32[3,1,64,130]{3,2,1,0:T(8,128)}, f32[3,1,64,130]{3,2,1,0:T(8,128)}, u32[]{:S(2)}, u32[]{:S(2)}) collective-permute-start(f32[3,1,64,130]{3,2,1,0:T(8,128)} %get-tuple-element.194), channel_id=1, source_target_pairs={{1,0},{2,1},{3,2},{4,3},{5,4},{6,5},{7,6},{9,8},{10,9},{11,10},{12... | collective-permute-start | bytes 299528 | tf_op jit(solution)/shard_map/ppermute | solution.py:19
  49.2 1.9 copy.128
  51.1 1.2 copy.126
  52.5 3.2 %fusion.2 = (f32[2,8,64,129]{3,2,0,1:T(8,128)S(1)}, f32[2,8,64,129]{3,2,0,1:T(8,128)}) fusion(f32[2,8,64,1]{3,2,0,1:T(8,128)} %collective-permute-done.2, f32[2,8,64,1]{3,2,0,1:T(8,128)} %collective-permute-done.3, f32[1,8,64,128]{3,2,0,1:T(8,128)S(1)} %bitcast.116, f32[3,8,64,1]{3,2,0,1:T(8,128)} %copy.128, f32[3,8,64,1]{3,2,0,1:T(8,128)} %copy.126, ...), kind=kLoop, calls=%fused_computation.10 | loop fusion | flops 1320960 | bytes 2387968 | tf_op jit(solution)/shard_map/mul | solution.py:35
  56.5 2.7 %multiply_add_fusion.28 = (f32[2,64,128]{2,1,0:T(8,128)S(1)}, f32[2,64,128]{2,1,0:T(8,128)S(1)}, f32[2,64,128]{2,1,0:T(8,128)S(1)}) fusion(f32[64,128]{1,0:T(8,128)S(1)} %copy-done.52, f32[64,128]{1,0:T(8,128)S(1)} %copy-done.49, f32[64,128]{1,0:T(8,128)S(1)} %get-tuple-element.261, f32[64,128]{1,0:T(8,128)S(1)} %get-tuple-element.260, ...), kind=kLoop, calls=%fused_computation.194 | loop fusion | flops 704512 | bytes 1245696 | tf_op jit(solution)/shard_map/add | solution.py:84
  59.7 2.1 %collective-permute-start.8 = (f32[2,64,130]{2,1,0:T(8,128)S(1)}, f32[2,64,130]{2,1,0:T(8,128)S(1)}, u32[]{:S(2)}, u32[]{:S(2)}) collective-permute-start(f32[2,64,130]{2,1,0:T(8,128)S(1)} %add_multiply_fusion.2), channel_id=1, source_target_pairs={{0,1},{1,2},{2,3},{3,4},{4,5},{5,6},{6,7},{8,9},{9,10},{10,11},{11... | collective-permute-start | bytes 199688 | tf_op jit(solution)/shard_map/ppermute | solution.py:29
  61.8 2.1 %fusion.11 = f32[2,9,64,128]{3,2,0,1:T(8,128)S(1)} fusion(f32[2,1,64,130]{3,2,0,1:T(8,128)} %collective-permute-done.7, f32[2,8,64,1]{3,2,0,1:T(8,128)} %collective-permute-done.2, f32[2,8,64,1]{3,2,0,1:T(8,128)} %collective-permute-done.3, f32[2,1,64,130]{3,2,0,1:T(8,128)} %collective-permute-done.6, f32[3,1,64,130]{3,2,1,0:T(8,128)} %collective-permute-done.5, ...), kind=kLoop, calls=%fused_computation.39 | loop fusion | flops 2359296 | bytes 2253824 | tf_op jit(solution)/shard_map/mul | solution.py:39
  63.8 1.2 fusion.22
  65.0 4.1 %collective-permute-done.8 = f32[2,64,130]{2,1,0:T(8,128)S(1)} collective-permute-done((f32[2,64,130]{2,1,0:T(8,128)S(1)}, f32[2,64,130]{2,1,0:T(8,128)S(1)}, u32[]{:S(2)}, u32[]{:S(2)}) %collective-permute-start.8) | collective-permute-done | bytes 66592 | tf_op jit(solution)/shard_map/ppermute | solution.py:29
  69.3 6.2 %collective-permute-start.9 = (f32[2,64]{1,0:T(2,128)S(1)}, f32[2,64]{1,0:T(2,128)S(1)}, u32[]{:S(2)}, u32[]{:S(2)}) collective-permute-start(f32[2,64]{1,0:T(2,128)S(1)} %get-tuple-element.154), channel_id=1, source_target_pairs={{0,8},{8,16},{16,24},{24,32},{32,40},{40,48},{48,56},{56,64},{64,7... | collective-permute-start | bytes 1544 | tf_op jit(solution)/shard_map/ppermute | solution.py:29
  75.5 1.9 collective-permute-start.10
  77.4 1.5 fusion.37
  79.1 3.4 %collective-permute-done.10 = f32[2,64]{1,0:T(2,128)S(1)} collective-permute-done((f32[2,64]{1,0:T(2,128)S(1)}, f32[2,64]{1,0:T(2,128)S(1)}, u32[]{:S(2)}, u32[]{:S(2)}) %collective-permute-start.10) | collective-permute-done | bytes 544 | tf_op jit(solution)/shard_map/ppermute | solution.py:29
  83.3 1.5 fusion.36
  84.8 1.1 multiply_add_fusion.1
  86.1 1.9 collective-permute-start.11
  88.1 5.9 %collective-permute-start.12 = (f32[2,8,64,1]{3,2,0,1:T(8,128)S(1)}, f32[2,8,64,1]{3,2,0,1:T(8,128)S(1)}, u32[]{:S(2)}, u32[]{:S(2)}) collective-permute-start(f32[2,8,64,1]{3,2,0,1:T(8,128)S(1)} %get-tuple-element.206), channel_id=1, source_target_pairs={{0,8},{8,16},{16,24},{24,32},{32,40},{40,48},{48,56},{56,64},{64,7... | collective-permute-start | bytes 12296 | tf_op jit(solution)/shard_map/ppermute | solution.py:17
  94.1 4.7 %collective-permute-done.11 = f32[2,8,64,1]{3,2,0,1:T(8,128)S(1)} collective-permute-done((f32[2,8,64,1]{3,2,0,1:T(8,128)S(1)}, f32[2,8,64,1]{3,2,0,1:T(8,128)S(1)}, u32[]{:S(2)}, u32[]{:S(2)}) %collective-permute-start.11) | collective-permute-done | bytes 4128 | tf_op jit(solution)/shard_map/ppermute | solution.py:19
  98.8 1.2 collective-permute-done.12
  100.6 1.9 collective-permute-start.14
  102.5 7.0 %collective-permute-start.13 = (f32[2,1,64,130]{3,2,0,1:T(8,128)S(1)}, f32[2,1,64,130]{3,2,0,1:T(8,128)S(1)}, u32[]{:S(2)}, u32[]{:S(2)}) collective-permute-start(f32[2,1,64,130]{3,2,0,1:T(8,128)S(1)} %get-tuple-element.198), channel_id=1, source_target_pairs={{1,0},{2,1},{3,2},{4,3},{5,4},{6,5},{7,6},{9,8},{10,9},{11,10},{12... | collective-permute-start | bytes 199688 | tf_op jit(solution)/shard_map/ppermute | solution.py:19
  110.1 1.4 collective-permute-done.13
  112.3 1.9 collective-permute-start.15
  114.2 1.7 fusion.9
  115.9 1.1 fusion.18
  117.0 5.0 %collective-permute-done.15 = f32[2,64,130]{2,1,0:T(8,128)S(1)} collective-permute-done((f32[2,64,130]{2,1,0:T(8,128)S(1)}, f32[2,64,130]{2,1,0:T(8,128)S(1)}, u32[]{:S(2)}, u32[]{:S(2)}) %collective-permute-start.15) | collective-permute-done | bytes 66592 | tf_op jit(solution)/shard_map/ppermute | solution.py:29
  122.2 8.8 %collective-permute-start.16 = (f32[2,64]{1,0:T(2,128)S(1)}, f32[2,64]{1,0:T(2,128)S(1)}, u32[]{:S(2)}, u32[]{:S(2)}) collective-permute-start(f32[2,64]{1,0:T(2,128)S(1)} %get-tuple-element.152), channel_id=1, source_target_pairs={{0,8},{8,16},{16,24},{24,32},{32,40},{40,48},{48,56},{56,64},{64,7... | collective-permute-start | bytes 1544 | tf_op jit(solution)/shard_map/ppermute | solution.py:29
  131.0 1.9 collective-permute-start.17
  132.9 1.5 fusion.35
  134.6 3.4 %collective-permute-done.17 = f32[2,64]{1,0:T(2,128)S(1)} collective-permute-done((f32[2,64]{1,0:T(2,128)S(1)}, f32[2,64]{1,0:T(2,128)S(1)}, u32[]{:S(2)}, u32[]{:S(2)}) %collective-permute-start.17) | collective-permute-done | bytes 544 | tf_op jit(solution)/shard_map/ppermute | solution.py:29
  138.8 1.5 fusion.34
  140.3 1.1 copy_add_fusion
  141.6 1.9 collective-permute-start.18
  143.6 6.1 %collective-permute-start.19 = (f32[2,8,64,1]{3,2,0,1:T(8,128)S(1)}, f32[2,8,64,1]{3,2,0,1:T(8,128)S(1)}, u32[]{:S(2)}, u32[]{:S(2)}) collective-permute-start(f32[2,8,64,1]{3,2,0,1:T(8,128)S(1)} %get-tuple-element.204), channel_id=1, source_target_pairs={{0,8},{8,16},{16,24},{24,32},{32,40},{40,48},{48,56},{56,64},{64,7... | collective-permute-start | bytes 12296 | tf_op jit(solution)/shard_map/ppermute | solution.py:17
  149.8 4.6 %collective-permute-done.18 = f32[2,8,64,1]{3,2,0,1:T(8,128)S(1)} collective-permute-done((f32[2,8,64,1]{3,2,0,1:T(8,128)S(1)}, f32[2,8,64,1]{3,2,0,1:T(8,128)S(1)}, u32[]{:S(2)}, u32[]{:S(2)}) %collective-permute-start.18) | collective-permute-done | bytes 4128 | tf_op jit(solution)/shard_map/ppermute | solution.py:19
  154.3 1.2 collective-permute-done.19
  156.1 1.9 collective-permute-start.21
  158.2 7.1 %collective-permute-start.20 = (f32[2,1,64,130]{3,2,0,1:T(8,128)S(1)}, f32[2,1,64,130]{3,2,0,1:T(8,128)S(1)}, u32[]{:S(2)}, u32[]{:S(2)}) collective-permute-start(f32[2,1,64,130]{3,2,0,1:T(8,128)S(1)} %get-tuple-element.196), channel_id=1, source_target_pairs={{1,0},{2,1},{3,2},{4,3},{5,4},{6,5},{7,6},{9,8},{10,9},{11,10},{12... | collective-permute-start | bytes 199688 | tf_op jit(solution)/shard_map/ppermute | solution.py:19
  165.7 1.5 collective-permute-done.20
  168.1 1.9 collective-permute-start.22
  170.0 1.7 copy_multiply_fusion
  172.0 5.8 %collective-permute-done.22 = f32[2,64,130]{2,1,0:T(8,128)S(1)} collective-permute-done((f32[2,64,130]{2,1,0:T(8,128)S(1)}, f32[2,64,130]{2,1,0:T(8,128)S(1)}, u32[]{:S(2)}, u32[]{:S(2)}) %collective-permute-start.22) | collective-permute-done | bytes 66592 | tf_op jit(solution)/shard_map/ppermute | solution.py:29
  178.0 8.8 %collective-permute-start.23 = (f32[2,64]{1,0:T(2,128)S(1)}, f32[2,64]{1,0:T(2,128)S(1)}, u32[]{:S(2)}, u32[]{:S(2)}) collective-permute-start(f32[2,64]{1,0:T(2,128)S(1)} %get-tuple-element.150), channel_id=1, source_target_pairs={{0,8},{8,16},{16,24},{24,32},{32,40},{40,48},{48,56},{56,64},{64,7... | collective-permute-start | bytes 1544 | tf_op jit(solution)/shard_map/ppermute | solution.py:29
  186.8 1.9 collective-permute-start.24
  188.9 4.8 %collective-permute-done.24 = f32[2,64]{1,0:T(2,128)S(1)} collective-permute-done((f32[2,64]{1,0:T(2,128)S(1)}, f32[2,64]{1,0:T(2,128)S(1)}, u32[]{:S(2)}, u32[]{:S(2)}) %collective-permute-start.24) | collective-permute-done | bytes 544 | tf_op jit(solution)/shard_map/ppermute | solution.py:29
  194.6 0.9 multiply_add_fusion
  (221 shorter events, 12.3 us)
Async XLA Ops:
  2.0 8.3 %copy-start.1 = (f32[2,8,64,128]{3,2,1,0:T(8,128)S(1)}, f32[2,8,64,128]{3,2,1,0:T(8,128)}, u32[]{:S(2)}) copy-start(f32[2,8,64,128]{3,2,1,0:T(8,128)} %param.32) | copy-start | bytes 1572868
  2.0 23.4 %collective-permute-start = (f32[3,8,64,1]{2,1,3,0:T(8,128)S(1)}, f32[3,8,64,1]{2,1,3,0:T(8,128)S(1)}, u32[]{:S(2)}, u32[]{:S(2)}) collective-permute-start(f32[3,8,64,1]{2,1,3,0:T(8,128)S(1)} %copy.125), channel_id=1, source_target_pairs={{8,0},{16,8},{24,16},{32,24},{40,32},{48,40},{56,48},{64,56},{72,6... | collective-permute-start | bytes 18440 | tf_op jit(solution)/shard_map/ppermute | solution.py:19
  5.0 14.0 %copy-start = (f32[2,8,64,128]{3,2,1,0:T(8,128)S(1)}, f32[2,8,64,128]{3,2,1,0:T(8,128)}, u32[]{:S(2)}) copy-start(f32[2,8,64,128]{3,2,1,0:T(8,128)} %param.33) | copy-start | bytes 1572868
  5.0 14.1 %copy-start.10 = (f32[8,64,128]{2,1,0:T(8,128)S(1)}, f32[8,64,128]{2,1,0:T(8,128)}, u32[]{:S(2)}) copy-start(f32[8,64,128]{2,1,0:T(8,128)} %param.34) | copy-start | bytes 786436
  5.0 20.7 %collective-permute-start.1 = (f32[3,8,64,1]{2,1,3,0:T(8,128)S(1)}, f32[3,8,64,1]{2,1,3,0:T(8,128)}, u32[]{:S(2)}, u32[]{:S(2)}) collective-permute-start(f32[3,8,64,1]{2,1,3,0:T(8,128)S(1)} %copy.127), channel_id=1, source_target_pairs={{0,8},{8,16},{16,24},{24,32},{32,40},{40,48},{48,56},{56,64},{64,7... | collective-permute-start | bytes 18440 | tf_op jit(solution)/shard_map/ppermute | solution.py:17
  11.4 16.7 %collective-permute-start.2 = (f32[2,8,64,1]{3,2,0,1:T(8,128)}, f32[2,8,64,1]{3,2,0,1:T(8,128)}, u32[]{:S(2)}, u32[]{:S(2)}) collective-permute-start(f32[2,8,64,1]{3,2,0,1:T(8,128)} %get-tuple-element.209), channel_id=1, source_target_pairs={{8,0},{16,8},{24,16},{32,24},{40,32},{48,40},{56,48},{64,56},{72,6... | collective-permute-start | bytes 12296 | tf_op jit(solution)/shard_map/ppermute | solution.py:19
  13.3 14.7 %collective-permute-start.3 = (f32[2,8,64,1]{3,2,0,1:T(8,128)}, f32[2,8,64,1]{3,2,0,1:T(8,128)}, u32[]{:S(2)}, u32[]{:S(2)}) collective-permute-start(f32[2,8,64,1]{3,2,0,1:T(8,128)} %get-tuple-element.208), channel_id=1, source_target_pairs={{0,8},{8,16},{16,24},{24,32},{32,40},{40,48},{48,56},{56,64},{64,7... | collective-permute-start | bytes 12296 | tf_op jit(solution)/shard_map/ppermute | solution.py:17
  31.4 30.3 %collective-permute-start.7 = (f32[2,1,64,130]{3,2,0,1:T(8,128)}, f32[2,1,64,130]{3,2,0,1:T(8,128)}, u32[]{:S(2)}, u32[]{:S(2)}) collective-permute-start(f32[2,1,64,130]{3,2,0,1:T(8,128)} %get-tuple-element.201), channel_id=1, source_target_pairs={{0,1},{1,2},{2,3},{3,4},{4,5},{5,6},{6,7},{8,9},{9,10},{10,11},{11... | collective-permute-start | bytes 199688 | tf_op jit(solution)/shard_map/ppermute | solution.py:17
  34.5 21.2 %collective-permute-start.6 = (f32[2,1,64,130]{3,2,0,1:T(8,128)}, f32[2,1,64,130]{3,2,0,1:T(8,128)}, u32[]{:S(2)}, u32[]{:S(2)}) collective-permute-start(f32[2,1,64,130]{3,2,0,1:T(8,128)} %get-tuple-element.200), channel_id=1, source_target_pairs={{1,0},{2,1},{3,2},{4,3},{5,4},{6,5},{7,6},{9,8},{10,9},{11,10},{12... | collective-permute-start | bytes 199688 | tf_op jit(solution)/shard_map/ppermute | solution.py:19
  40.3 21.4 %collective-permute-start.5 = (f32[3,1,64,130]{3,2,1,0:T(8,128)}, f32[3,1,64,130]{3,2,1,0:T(8,128)}, u32[]{:S(2)}, u32[]{:S(2)}) collective-permute-start(f32[3,1,64,130]{3,2,1,0:T(8,128)} %get-tuple-element.195), channel_id=1, source_target_pairs={{0,1},{1,2},{2,3},{3,4},{4,5},{5,6},{6,7},{8,9},{9,10},{10,11},{11... | collective-permute-start | bytes 299528 | tf_op jit(solution)/shard_map/ppermute | solution.py:17
  42.2 19.5 %collective-permute-start.4 = (f32[3,1,64,130]{3,2,1,0:T(8,128)}, f32[3,1,64,130]{3,2,1,0:T(8,128)}, u32[]{:S(2)}, u32[]{:S(2)}) collective-permute-start(f32[3,1,64,130]{3,2,1,0:T(8,128)} %get-tuple-element.194), channel_id=1, source_target_pairs={{1,0},{2,1},{3,2},{4,3},{5,4},{6,5},{7,6},{9,8},{10,9},{11,10},{12... | collective-permute-start | bytes 299528 | tf_op jit(solution)/shard_map/ppermute | solution.py:19
  52.4 3.4 %copy-start.22 = (f32[64,128]{1,0:T(8,128)S(1)}, f32[64,128]{1,0:T(8,128)}, u32[]{:S(2)}) copy-start(f32[64,128]{1,0:T(8,128)} %get-tuple-element.258) | copy-start | bytes 98308
  52.4 3.4 %copy-start.25 = (f32[64,128]{1,0:T(8,128)S(1)}, f32[64,128]{1,0:T(8,128)}, u32[]{:S(2)}) copy-start(f32[64,128]{1,0:T(8,128)} %get-tuple-element.186) | copy-start | bytes 98308
  52.4 3.4 %copy-start.28 = (f32[64,128]{1,0:T(8,128)S(1)}, f32[64,128]{1,0:T(8,128)}, u32[]{:S(2)}) copy-start(f32[64,128]{1,0:T(8,128)} %get-tuple-element.237) | copy-start | bytes 98308
  52.4 3.4 %copy-start.31 = (f32[64,128]{1,0:T(8,128)S(1)}, f32[64,128]{1,0:T(8,128)}, u32[]{:S(2)}) copy-start(f32[64,128]{1,0:T(8,128)} %get-tuple-element.247) | copy-start | bytes 98308
  52.4 3.4 %copy-start.34 = (f32[64,128]{1,0:T(8,128)S(1)}, f32[64,128]{1,0:T(8,128)}, u32[]{:S(2)}) copy-start(f32[64,128]{1,0:T(8,128)} %get-tuple-element.249) | copy-start | bytes 98308
  52.4 3.4 %copy-start.37 = (f32[64,128]{1,0:T(8,128)S(1)}, f32[64,128]{1,0:T(8,128)}, u32[]{:S(2)}) copy-start(f32[64,128]{1,0:T(8,128)} %get-tuple-element.263) | copy-start | bytes 98308
  52.4 3.4 %copy-start.40 = (f32[64,128]{1,0:T(8,128)S(1)}, f32[64,128]{1,0:T(8,128)}, u32[]{:S(2)}) copy-start(f32[64,128]{1,0:T(8,128)} %get-tuple-element.265) | copy-start | bytes 98308
  52.5 3.4 %copy-start.43 = (f32[64,128]{1,0:T(8,128)S(1)}, f32[64,128]{1,0:T(8,128)}, u32[]{:S(2)}) copy-start(f32[64,128]{1,0:T(8,128)} %get-tuple-element.267) | copy-start | bytes 98308
  52.5 3.4 %copy-start.46 = (f32[64,128]{1,0:T(8,128)S(1)}, f32[64,128]{1,0:T(8,128)}, u32[]{:S(2)}) copy-start(f32[64,128]{1,0:T(8,128)} %get-tuple-element.269) | copy-start | bytes 98308
  52.5 3.4 %copy-start.49 = (f32[64,128]{1,0:T(8,128)S(1)}, f32[64,128]{1,0:T(8,128)}, u32[]{:S(2)}) copy-start(f32[64,128]{1,0:T(8,128)} %get-tuple-element.179) | copy-start | bytes 98308
  52.5 3.4 %copy-start.52 = (f32[64,128]{1,0:T(8,128)S(1)}, f32[64,128]{1,0:T(8,128)}, u32[]{:S(2)}) copy-start(f32[64,128]{1,0:T(8,128)} %get-tuple-element.234) | copy-start | bytes 98308
  52.5 3.4 %copy-start.55 = (f32[64,128]{1,0:T(8,128)S(1)}, f32[64,128]{1,0:T(8,128)}, u32[]{:S(2)}) copy-start(f32[64,128]{1,0:T(8,128)} %get-tuple-element.245) | copy-start | bytes 98308
  52.5 3.4 %copy-start.58 = (f32[64,128]{1,0:T(8,128)S(1)}, f32[64,128]{1,0:T(8,128)}, u32[]{:S(2)}) copy-start(f32[64,128]{1,0:T(8,128)} %get-tuple-element.246) | copy-start | bytes 98308
  59.6 4.2 %copy-start.12 = (f32[2,8,64,130]{3,2,0,1:T(8,128)S(1)}, f32[2,8,64,130]{3,2,0,1:T(8,128)}, u32[]{:S(2)}) copy-start(f32[2,8,64,130]{3,2,0,1:T(8,128)} %get-tuple-element.192) | copy-start | bytes 1597444
  59.7 9.5 %collective-permute-start.8 = (f32[2,64,130]{2,1,0:T(8,128)S(1)}, f32[2,64,130]{2,1,0:T(8,128)S(1)}, u32[]{:S(2)}, u32[]{:S(2)}) collective-permute-start(f32[2,64,130]{2,1,0:T(8,128)S(1)} %add_multiply_fusion.2), channel_id=1, source_target_pairs={{0,1},{1,2},{2,3},{3,4},{4,5},{5,6},{6,7},{8,9},{9,10},{10,11},{11... | collective-permute-start | bytes 199688 | tf_op jit(solution)/shard_map/ppermute | solution.py:29
  69.1 9.8 %copy-start.61 = (f32[2,64,130]{2,1,0:T(8,128)}, f32[2,64,130]{2,1,0:T(8,128)S(1)}, u32[]{:S(2)}) copy-start(f32[2,64,130]{2,1,0:T(8,128)S(1)} %collective-permute-done.8) | copy-start | bytes 199684
  69.3 9.7 %collective-permute-start.9 = (f32[2,64]{1,0:T(2,128)S(1)}, f32[2,64]{1,0:T(2,128)S(1)}, u32[]{:S(2)}, u32[]{:S(2)}) collective-permute-start(f32[2,64]{1,0:T(2,128)S(1)} %get-tuple-element.154), channel_id=1, source_target_pairs={{0,8},{8,16},{16,24},{24,32},{32,40},{40,48},{48,56},{56,64},{64,7... | collective-permute-start | bytes 1544 | tf_op jit(solution)/shard_map/ppermute | solution.py:29
  75.5 7.0 %collective-permute-start.10 = (f32[2,64]{1,0:T(2,128)S(1)}, f32[2,64]{1,0:T(2,128)S(1)}, u32[]{:S(2)}, u32[]{:S(2)}) collective-permute-start(f32[2,64]{1,0:T(2,128)S(1)} %get-tuple-element.153), channel_id=1, source_target_pairs={{8,0},{16,8},{24,16},{32,24},{40,32},{48,40},{56,48},{64,56},{72,6... | collective-permute-start | bytes 1544 | tf_op jit(solution)/shard_map/ppermute | solution.py:29
  79.0 3.6 %copy-start.62 = (f32[2,64,130]{2,1,0:T(8,128)S(1)}, f32[2,64,130]{2,1,0:T(8,128)}, u32[]{:S(2)}) copy-start(f32[2,64,130]{2,1,0:T(8,128)} %copy-done.61) | copy-start | bytes 199684
  86.1 12.7 %collective-permute-start.11 = (f32[2,8,64,1]{3,2,0,1:T(8,128)S(1)}, f32[2,8,64,1]{3,2,0,1:T(8,128)S(1)}, u32[]{:S(2)}, u32[]{:S(2)}) collective-permute-start(f32[2,8,64,1]{3,2,0,1:T(8,128)S(1)} %get-tuple-element.207), channel_id=1, source_target_pairs={{8,0},{16,8},{24,16},{32,24},{40,32},{48,40},{56,48},{64,56},{72,6... | collective-permute-start | bytes 12296 | tf_op jit(solution)/shard_map/ppermute | solution.py:19
  88.1 12.0 %copy-start.8 = (f32[8,64,130]{2,1,0:T(8,128)S(1)}, f32[8,64,130]{2,1,0:T(8,128)}, u32[]{:S(2)}) copy-start(f32[8,64,130]{2,1,0:T(8,128)} %copy-done.7) | copy-start | bytes 798724
  88.1 12.0 %collective-permute-start.12 = (f32[2,8,64,1]{3,2,0,1:T(8,128)S(1)}, f32[2,8,64,1]{3,2,0,1:T(8,128)S(1)}, u32[]{:S(2)}, u32[]{:S(2)}) collective-permute-start(f32[2,8,64,1]{3,2,0,1:T(8,128)S(1)} %get-tuple-element.206), channel_id=1, source_target_pairs={{0,8},{8,16},{16,24},{24,32},{32,40},{40,48},{48,56},{56,64},{64,7... | collective-permute-start | bytes 12296 | tf_op jit(solution)/shard_map/ppermute | solution.py:17
  100.1 9.4 %copy-start.5 = (f32[2,8,64,129]{3,2,0,1:T(8,128)S(1)}, f32[2,8,64,129]{3,2,0,1:T(8,128)}, u32[]{:S(2)}) copy-start(f32[2,8,64,129]{3,2,0,1:T(8,128)} %get-tuple-element.191) | copy-start | bytes 1585156
  100.6 13.6 %collective-permute-start.14 = (f32[2,1,64,130]{3,2,0,1:T(8,128)S(1)}, f32[2,1,64,130]{3,2,0,1:T(8,128)S(1)}, u32[]{:S(2)}, u32[]{:S(2)}) collective-permute-start(f32[2,1,64,130]{3,2,0,1:T(8,128)S(1)} %get-tuple-element.199), channel_id=1, source_target_pairs={{0,1},{1,2},{2,3},{3,4},{4,5},{5,6},{6,7},{8,9},{9,10},{10,11},{11... | collective-permute-start | bytes 199688 | tf_op jit(solution)/shard_map/ppermute | solution.py:17
  102.5 8.9 %collective-permute-start.13 = (f32[2,1,64,130]{3,2,0,1:T(8,128)S(1)}, f32[2,1,64,130]{3,2,0,1:T(8,128)S(1)}, u32[]{:S(2)}, u32[]{:S(2)}) collective-permute-start(f32[2,1,64,130]{3,2,0,1:T(8,128)S(1)} %get-tuple-element.198), channel_id=1, source_target_pairs={{1,0},{2,1},{3,2},{4,3},{5,4},{6,5},{7,6},{9,8},{10,9},{11,10},{12... | collective-permute-start | bytes 199688 | tf_op jit(solution)/shard_map/ppermute | solution.py:19
  112.3 9.7 %collective-permute-start.15 = (f32[2,64,130]{2,1,0:T(8,128)S(1)}, f32[2,64,130]{2,1,0:T(8,128)S(1)}, u32[]{:S(2)}, u32[]{:S(2)}) collective-permute-start(f32[2,64,130]{2,1,0:T(8,128)S(1)} %add_multiply_fusion.1), channel_id=1, source_target_pairs={{0,1},{1,2},{2,3},{3,4},{4,5},{5,6},{6,7},{8,9},{9,10},{10,11},{11... | collective-permute-start | bytes 199688 | tf_op jit(solution)/shard_map/ppermute | solution.py:29
  122.2 12.3 %collective-permute-start.16 = (f32[2,64]{1,0:T(2,128)S(1)}, f32[2,64]{1,0:T(2,128)S(1)}, u32[]{:S(2)}, u32[]{:S(2)}) collective-permute-start(f32[2,64]{1,0:T(2,128)S(1)} %get-tuple-element.152), channel_id=1, source_target_pairs={{0,8},{8,16},{16,24},{24,32},{32,40},{40,48},{48,56},{56,64},{64,7... | collective-permute-start | bytes 1544 | tf_op jit(solution)/shard_map/ppermute | solution.py:29
  131.0 7.0 %collective-permute-start.17 = (f32[2,64]{1,0:T(2,128)S(1)}, f32[2,64]{1,0:T(2,128)S(1)}, u32[]{:S(2)}, u32[]{:S(2)}) collective-permute-start(f32[2,64]{1,0:T(2,128)S(1)} %get-tuple-element.151), channel_id=1, source_target_pairs={{8,0},{16,8},{24,16},{32,24},{40,32},{48,40},{56,48},{64,56},{72,6... | collective-permute-start | bytes 1544 | tf_op jit(solution)/shard_map/ppermute | solution.py:29
  141.6 12.7 %collective-permute-start.18 = (f32[2,8,64,1]{3,2,0,1:T(8,128)S(1)}, f32[2,8,64,1]{3,2,0,1:T(8,128)S(1)}, u32[]{:S(2)}, u32[]{:S(2)}) collective-permute-start(f32[2,8,64,1]{3,2,0,1:T(8,128)S(1)} %get-tuple-element.205), channel_id=1, source_target_pairs={{8,0},{16,8},{24,16},{32,24},{40,32},{48,40},{56,48},{64,56},{72,6... | collective-permute-start | bytes 12296 | tf_op jit(solution)/shard_map/ppermute | solution.py:19
  143.5 12.0 %copy-start.9 = (f32[8,64,130]{2,1,0:T(8,128)S(1)}, f32[8,64,130]{2,1,0:T(8,128)}, u32[]{:S(2)}) copy-start(f32[8,64,130]{2,1,0:T(8,128)} %copy-done.7) | copy-start | bytes 798724
  143.6 12.0 %collective-permute-start.19 = (f32[2,8,64,1]{3,2,0,1:T(8,128)S(1)}, f32[2,8,64,1]{3,2,0,1:T(8,128)S(1)}, u32[]{:S(2)}, u32[]{:S(2)}) collective-permute-start(f32[2,8,64,1]{3,2,0,1:T(8,128)S(1)} %get-tuple-element.204), channel_id=1, source_target_pairs={{0,8},{8,16},{16,24},{24,32},{32,40},{40,48},{48,56},{56,64},{64,7... | collective-permute-start | bytes 12296 | tf_op jit(solution)/shard_map/ppermute | solution.py:17
  155.6 9.7 %copy-start.6 = (f32[2,8,64,129]{3,2,0,1:T(8,128)S(1)}, f32[2,8,64,129]{3,2,0,1:T(8,128)}, u32[]{:S(2)}) copy-start(f32[2,8,64,129]{3,2,0,1:T(8,128)} %get-tuple-element.191) | copy-start | bytes 1585156
  156.1 13.9 %collective-permute-start.21 = (f32[2,1,64,130]{3,2,0,1:T(8,128)S(1)}, f32[2,1,64,130]{3,2,0,1:T(8,128)S(1)}, u32[]{:S(2)}, u32[]{:S(2)}) collective-permute-start(f32[2,1,64,130]{3,2,0,1:T(8,128)S(1)} %get-tuple-element.197), channel_id=1, source_target_pairs={{0,1},{1,2},{2,3},{3,4},{4,5},{5,6},{6,7},{8,9},{9,10},{10,11},{11... | collective-permute-start | bytes 199688 | tf_op jit(solution)/shard_map/ppermute | solution.py:17
  158.0 9.2 %copy-start.15 = (f32[64,128]{1,0:T(8,128)S(1)}, f32[64,128]{1,0:T(8,128)}, u32[]{:S(2)}) copy-start(f32[64,128]{1,0:T(8,128)} %get-tuple-element.255) | copy-start | bytes 98308
  158.0 9.2 %copy-start.18 = (f32[64,128]{1,0:T(8,128)S(1)}, f32[64,128]{1,0:T(8,128)}, u32[]{:S(2)}) copy-start(f32[64,128]{1,0:T(8,128)} %get-tuple-element.256) | copy-start | bytes 98308
  158.0 9.2 %copy-start.21 = (f32[64,128]{1,0:T(8,128)S(1)}, f32[64,128]{1,0:T(8,128)}, u32[]{:S(2)}) copy-start(f32[64,128]{1,0:T(8,128)} %get-tuple-element.257) | copy-start | bytes 98308
  158.0 9.2 %copy-start.24 = (f32[64,128]{1,0:T(8,128)S(1)}, f32[64,128]{1,0:T(8,128)}, u32[]{:S(2)}) copy-start(f32[64,128]{1,0:T(8,128)} %get-tuple-element.258) | copy-start | bytes 98308
  158.0 9.2 %copy-start.27 = (f32[64,128]{1,0:T(8,128)S(1)}, f32[64,128]{1,0:T(8,128)}, u32[]{:S(2)}) copy-start(f32[64,128]{1,0:T(8,128)} %get-tuple-element.186) | copy-start | bytes 98308
  158.1 9.2 %copy-start.30 = (f32[64,128]{1,0:T(8,128)S(1)}, f32[64,128]{1,0:T(8,128)}, u32[]{:S(2)}) copy-start(f32[64,128]{1,0:T(8,128)} %get-tuple-element.237) | copy-start | bytes 98308
  158.1 9.2 %copy-start.33 = (f32[64,128]{1,0:T(8,128)S(1)}, f32[64,128]{1,0:T(8,128)}, u32[]{:S(2)}) copy-start(f32[64,128]{1,0:T(8,128)} %get-tuple-element.247) | copy-start | bytes 98308
  158.1 9.2 %copy-start.36 = (f32[64,128]{1,0:T(8,128)S(1)}, f32[64,128]{1,0:T(8,128)}, u32[]{:S(2)}) copy-start(f32[64,128]{1,0:T(8,128)} %get-tuple-element.249) | copy-start | bytes 98308
  158.1 9.2 %copy-start.39 = (f32[64,128]{1,0:T(8,128)S(1)}, f32[64,128]{1,0:T(8,128)}, u32[]{:S(2)}) copy-start(f32[64,128]{1,0:T(8,128)} %get-tuple-element.263) | copy-start | bytes 98308
  158.1 9.2 %copy-start.42 = (f32[64,128]{1,0:T(8,128)S(1)}, f32[64,128]{1,0:T(8,128)}, u32[]{:S(2)}) copy-start(f32[64,128]{1,0:T(8,128)} %get-tuple-element.265) | copy-start | bytes 98308
  158.1 9.2 %copy-start.45 = (f32[64,128]{1,0:T(8,128)S(1)}, f32[64,128]{1,0:T(8,128)}, u32[]{:S(2)}) copy-start(f32[64,128]{1,0:T(8,128)} %get-tuple-element.267) | copy-start | bytes 98308
  158.1 9.2 %copy-start.48 = (f32[64,128]{1,0:T(8,128)S(1)}, f32[64,128]{1,0:T(8,128)}, u32[]{:S(2)}) copy-start(f32[64,128]{1,0:T(8,128)} %get-tuple-element.269) | copy-start | bytes 98308
  158.1 9.2 %copy-start.51 = (f32[64,128]{1,0:T(8,128)S(1)}, f32[64,128]{1,0:T(8,128)}, u32[]{:S(2)}) copy-start(f32[64,128]{1,0:T(8,128)} %get-tuple-element.179) | copy-start | bytes 98308
  158.1 9.2 %copy-start.54 = (f32[64,128]{1,0:T(8,128)S(1)}, f32[64,128]{1,0:T(8,128)}, u32[]{:S(2)}) copy-start(f32[64,128]{1,0:T(8,128)} %get-tuple-element.234) | copy-start | bytes 98308
  158.1 9.2 %copy-start.57 = (f32[64,128]{1,0:T(8,128)S(1)}, f32[64,128]{1,0:T(8,128)}, u32[]{:S(2)}) copy-start(f32[64,128]{1,0:T(8,128)} %get-tuple-element.245) | copy-start | bytes 98308
  158.2 9.2 %copy-start.60 = (f32[64,128]{1,0:T(8,128)S(1)}, f32[64,128]{1,0:T(8,128)}, u32[]{:S(2)}) copy-start(f32[64,128]{1,0:T(8,128)} %get-tuple-element.246) | copy-start | bytes 98308
  158.2 9.0 %collective-permute-start.20 = (f32[2,1,64,130]{3,2,0,1:T(8,128)S(1)}, f32[2,1,64,130]{3,2,0,1:T(8,128)S(1)}, u32[]{:S(2)}, u32[]{:S(2)}) collective-permute-start(f32[2,1,64,130]{3,2,0,1:T(8,128)S(1)} %get-tuple-element.196), channel_id=1, source_target_pairs={{1,0},{2,1},{3,2},{4,3},{5,4},{6,5},{7,6},{9,8},{10,9},{11,10},{12... | collective-permute-start | bytes 199688 | tf_op jit(solution)/shard_map/ppermute | solution.py:19
  168.1 9.7 %collective-permute-start.22 = (f32[2,64,130]{2,1,0:T(8,128)S(1)}, f32[2,64,130]{2,1,0:T(8,128)S(1)}, u32[]{:S(2)}, u32[]{:S(2)}) collective-permute-start(f32[2,64,130]{2,1,0:T(8,128)S(1)} %add_multiply_fusion), channel_id=1, source_target_pairs={{0,1},{1,2},{2,3},{3,4},{4,5},{5,6},{6,7},{8,9},{9,10},{10,11},{11... | collective-permute-start | bytes 199688 | tf_op jit(solution)/shard_map/ppermute | solution.py:29
  178.0 10.8 %collective-permute-start.23 = (f32[2,64]{1,0:T(2,128)S(1)}, f32[2,64]{1,0:T(2,128)S(1)}, u32[]{:S(2)}, u32[]{:S(2)}) collective-permute-start(f32[2,64]{1,0:T(2,128)S(1)} %get-tuple-element.150), channel_id=1, source_target_pairs={{0,8},{8,16},{16,24},{24,32},{32,40},{40,48},{48,56},{56,64},{64,7... | collective-permute-start | bytes 1544 | tf_op jit(solution)/shard_map/ppermute | solution.py:29
  186.8 7.0 %collective-permute-start.24 = (f32[2,64]{1,0:T(2,128)S(1)}, f32[2,64]{1,0:T(2,128)S(1)}, u32[]{:S(2)}, u32[]{:S(2)}) collective-permute-start(f32[2,64]{1,0:T(2,128)S(1)} %get-tuple-element.149), channel_id=1, source_target_pairs={{8,0},{16,8},{24,16},{32,24},{40,32},{48,40},{56,48},{64,56},{72,6... | collective-permute-start | bytes 1544 | tf_op jit(solution)/shard_map/ppermute | solution.py:29
  (29 other events, 52.8 us)
where the time goes:
time: 197 us; the launch traced here: 195 us
  starting transfers between devices  103 us (52%)
  waiting for transfers between devices  41.1 us (21%)
  other arithmetic  36.6 us (19%)
  local copies, waits for them, and re-layouts  13.6 us (7%)
    ppermute x9, starting transfers between devices, from_behind(): lax.ppermute(value, axis, [(source, source + steps) for source in range(l...  35.5 us
    ppermute x8, starting transfers between devices, extended(): lax.ppermute(head, axis, [((i + 1) % count, i) for i in range(ends)])  35.3 us
    ppermute x8, starting transfers between devices, extended(): lax.ppermute(tail, axis, [(i, (i + 1) % count) for i in range(ends)])  31.8 us
    ppermute x9, waiting for transfers between devices, from_behind(): lax.ppermute(value, axis, [(source, source + steps) for source in range(l...  26.5 us
    ppermute x8, waiting for transfers between devices, extended(): lax.ppermute(head, axis, [((i + 1) % count, i) for i in range(ends)])  12.2 us
    scatter-add x6, other arithmetic, per_device(): delta = delta.at[:, depth - 1].add(-loss).at[:, 0].add(gain)  5.98 us
    mul x3, other arithmetic, transport(): fz = 0.5 * (kz[:, 1:] + kz[:, :-1]) * (cz[:, 1:] - cz[:, :-1])  5.39 us
    mul x3, other arithmetic, transport(): fx = 0.5 * (kx[..., 1:] + kx[..., :-1]) * (cx[..., 1:] - cx[..., :-1])  3.99 us
  transfers between devices with their start and end apart: 25, of which 12 were waited for; matrix products, arithmetic and copies ran while one was open for 16% of the time, Pallas kernels for 0%

commit v1 on v0

v1 whole, which is shorter than its diff:
```python
import jax
import jax.numpy as jnp
from jax import lax
from jax.experimental import pallas as pl
from jax.experimental.pallas import tpu as pltpu
from jax.sharding import PartitionSpec as P

RATES = (0.08, 0.12)
DEPTH, ROWS, COLS = 8, 64, 128
WIDE = 2 * COLS
HALO = 3
GROUP = 2 * HALO
SLOTS = COLS // GROUP
PLANES = 12
G_CONC, G_KAPPA, G_VEL, G_TYPE, G_FACE, GROUPS = 0, 16, 32, 40, 48, 54
TILES = -(-GROUPS // SLOTS)


def lanes_of(shape):
    return lax.broadcasted_iota(jnp.int32, shape, len(shape) - 1)


def edge_mask():
    lane = lanes_of((ROWS, COLS))
    return (lane < HALO) | (lane >= COLS - HALO)


def place_group(tile, plane, slot):
    lane = lanes_of(tile.shape)
    start = slot * GROUP
    moved = pltpu.roll(plane, (start + HALO) % COLS, 1)
    return jnp.where((lane >= start) & (lane < start + GROUP), moved, tile)


def take_group(tile, slot):
    moved = pltpu.roll(tile, (COLS - slot * GROUP - HALO) % COLS, 1)
    return jnp.where(edge_mask(), moved, 0.0)


def wide(main, halo):
    return jnp.concatenate([main, halo], axis=1)


def shift_cols(x, by):
    return pltpu.roll(x, (-by) % x.shape[1], 1)


def shift_rows(x, by):
    return pltpu.roll(x, (-by) % x.shape[0], 0)


def in_plane(c, kx, ky, v):
    s = kx * (shift_cols(c, 1) - c) - v * c
    f = ky * (shift_rows(c, 1) - c)
    return (s - shift_cols(s, -1)) + (f - shift_rows(f, -1))


def face_x(k):
    return 0.5 * (k + shift_cols(k, 1))


def face_y(k):
    row = lax.broadcasted_iota(jnp.int32, k.shape, 0)
    return jnp.where(row < ROWS - 1, 0.5 * (k + shift_rows(k, 1)), 0.0)


def gather(m_ref, bed):
    total = None
    for b in (-1, 0, 1):
        at_b = shift_cols(bed, b) if b else bed
        for a in (-1, 0, 1):
            term = m_ref[3 * (a + 1) + b + 1] * (shift_rows(at_b, a) if a else at_b)
            total = term if total is None else total + term
    return total


def scatter(m_ref, water):
    total = None
    for b in (-1, 0, 1):
        part = None
        for a in (-1, 0, 1):
            term = m_ref[3 * (a + 1) + b + 1]
            if water is not None:
                term = term * water
            term = shift_rows(term, -a) if a else term
            part = term if part is None else part + term
        part = shift_cols(part, -b) if b else part
        total = part if total is None else total + part
    return total


def face_planes(row_ref, col_ref, w_ref):
    start = lax.axis_index("stream") * COLS
    row = lax.broadcasted_iota(jnp.int32, (ROWS, COLS), 0)
    col = lanes_of((ROWS, COLS)) + start
    out = [(row_ref[k] - row).astype(jnp.float32) for k in range(2)]
    out += [(col_ref[k] - col).astype(jnp.float32) for k in range(2)]
    return out + [w_ref[k] for k in range(2)]


def pack_kernel(conc, kappa, vel, kind, row_ref, col_ref, w_ref, msg):
    tiles = [jnp.zeros((ROWS, COLS), jnp.float32) for _ in range(TILES)]

    def put(group, plane):
        t, slot = divmod(group, SLOTS)
        tiles[t] = place_group(tiles[t], plane, slot)

    for q in range(2):
        for z in range(DEPTH):
            put(G_CONC + q * DEPTH + z, conc[q, z])
            put(G_KAPPA + q * DEPTH + z, kappa[q, z])
    for z in range(DEPTH):
        put(G_VEL + z, vel[z])
        put(G_TYPE + z, kind[z].astype(jnp.float32))
    for i, plane in enumerate(face_planes(row_ref, col_ref, w_ref)):
        put(G_FACE + i, plane)
    for t in range(TILES):
        msg[t] = tiles[t]


def block_kernel(
    conc, kappa, vel, kind, row_ref, col_ref, w_ref, got_a, got_b,
    u3, msg_a, msg_b, halo, edge_u, m_out,
    cells, kx, ky, kz, own,
):
    even = lax.axis_index("stream") % 2 == 0
    lane = lanes_of((ROWS, COLS))
    low = lax.rem(lane, GROUP) < HALO
    from_b = low == even
    for t in range(TILES):
        both = jnp.where(from_b, got_b[t], got_a[t])
        for slot in range(min(SLOTS, GROUPS - t * SLOTS)):
            halo[t * SLOTS + slot] = take_group(both, slot)

    planes = [wide(p, halo[G_FACE + i]) for i, p in enumerate(face_planes(row_ref, col_ref, w_ref))]
    for a in (-1, 0, 1):
        for b in (-1, 0, 1):
            total = None
            for k in range(2):
                term = jnp.where((planes[k] == a) & (planes[2 + k] == b), planes[4 + k], 0.0)
                total = term if total is None else total + term
            m_out[3 * (a + 1) + b + 1] = total
    slab = lax.axis_index("slab")
    upper = (slab > 0).astype(jnp.float32)
    lower = (slab < lax.axis_size("slab") - 1).astype(jnp.float32)
    m_out[9] = scatter(m_out, None)
    m_out[10] = planes[4] + planes[5]

    own[...] = jnp.zeros(own.shape, jnp.float32)
    own[0] = m_out[9] * upper
    own[DEPTH - 1] = m_out[10] * lower

    def prepare(z, _):
        for q in range(2):
            k = wide(kappa[q, z], halo[G_KAPPA + q * DEPTH + z])
            kx[q, z] = face_x(k)
            ky[q, z] = face_y(k)
            cells[0, q, z + 1] = wide(conc[q, z], halo[G_CONC + q * DEPTH + z])
        return 0

    lax.fori_loop(0, DEPTH, prepare, 0)

    def prepare_z(z, _):
        for q in range(2):
            k = wide(kappa[q, z], halo[G_KAPPA + q * DEPTH + z])
            below = wide(kappa[q, z + 1], halo[G_KAPPA + q * DEPTH + z + 1])
            kz[q, z + 1] = 0.5 * (k + below)
        return 0

    lax.fori_loop(0, DEPTH - 1, prepare_z, 0)
    zeros = jnp.zeros((ROWS, WIDE), jnp.float32)
    for q in range(2):
        kz[q, 0] = zeros
        kz[q, DEPTH] = zeros
        for t in range(2):
            cells[t, q, 0] = zeros
            cells[t, q, DEPTH + 1] = zeros

    for step in range(3):
        now, later = step % 2, (step + 1) % 2

        def advance(z, _):
            a = wide(kind[z].astype(jnp.float32), halo[G_TYPE + z])
            v = wide(vel[z], halo[G_VEL + z])
            for q in range(2):
                c = cells[now, q, z + 1]
                r = in_plane(c, kx[q, z], ky[q, z], v)
                r += kz[q, z + 1] * (cells[now, q, z + 2] - c)
                r -= kz[q, z] * (c - cells[now, q, z])
                r -= RATES[q] * own[z] * c
                new = c + a * r
                if step == 2:
                    u3[q, z] = new[:, :COLS]
                else:
                    cells[later, q, z + 1] = new
            return 0

        lax.fori_loop(0, DEPTH, advance, 0)
        if step < 2:
            for q in range(2):
                edge_u[0, step, q] = cells[later, q, 1]
                edge_u[1, step, q] = cells[later, q, DEPTH]

    slab_even = slab % 2 == 0

    def sides(layers):
        first, second = layers
        out = []
        for q in range(2):
            out.append((conc[q, first], halo[G_CONC + q * DEPTH + first]))
        side = 0 if first == 0 else 1
        for t in range(2):
            for q in range(2):
                u = edge_u[side, t, q]
                out.append((u[:, :COLS], u[:, COLS:]))
        for z in (first, second):
            for q in range(2):
                out.append((kappa[q, z], halo[G_KAPPA + q * DEPTH + z]))
        out.append((vel[first], halo[G_VEL + first]))
        out.append((kind[first].astype(jnp.float32), halo[G_TYPE + first]))
        return out

    strip_a = jnp.zeros((ROWS, COLS), jnp.float32)
    strip_b = strip_a
    for i, (top, bottom) in enumerate(zip(sides((0, 1)), sides((DEPTH - 1, DEPTH - 2)))):
        msg_a[i] = jnp.where(slab_even, bottom[0], top[0])
        msg_b[i] = jnp.where(slab_even, top[0], bottom[0])
        strip_a = place_group(strip_a, jnp.where(slab_even, bottom[1], top[1]), i)
        strip_b = place_group(strip_b, jnp.where(slab_even, top[1], bottom[1]), i)
    msg_a[PLANES] = strip_a
    msg_b[PLANES] = strip_b


def join_kernel(conc, kappa, vel, kind, halo, edge_u, m_ref, u3, got_a, got_b, out, ghost):
    slab = lax.axis_index("slab")
    slab_even = slab % 2 == 0
    upper = (slab > 0).astype(jnp.float32)
    lower = (slab < lax.axis_size("slab") - 1).astype(jnp.float32)
    for side in range(2):
        first = slab_even if side == 1 else jnp.logical_not(slab_even)
        strip = jnp.where(first, got_a[PLANES], got_b[PLANES])
        for i in range(PLANES):
            ghost[side, i] = wide(jnp.where(first, got_a[i], got_b[i]), take_group(strip, i))

    for z in range(3, DEPTH - 3):
        for q in range(2):
            out[q, z] = u3[q, z]

    for side in range(2):
        z0, z1, z2 = (0, 1, 2) if side == 0 else (DEPTH - 1, DEPTH - 2, DEPTH - 3)
        a0, a1, a2 = [wide(kind[z].astype(jnp.float32), halo[G_TYPE + z]) for z in (z0, z1, z2)]
        v0, v1 = [wide(vel[z], halo[G_VEL + z]) for z in (z0, z1)]
        vg, ag = ghost[side, 10], ghost[side, 11]
        own_self = m_ref[9] * upper if side == 0 else m_ref[10] * lower
        for q in range(2):
            h = RATES[q]
            k0, k1, k2 = [wide(kappa[q, z], halo[G_KAPPA + q * DEPTH + z]) for z in (z0, z1, z2)]
            kg, kgg = ghost[side, 6 + q], ghost[side, 8 + q]
            k_face = 0.5 * (kg + k0)
            k01, k12, kg2 = 0.5 * (k0 + k1), 0.5 * (k1 + k2), 0.5 * (kg + kgg)
            c0 = [wide(conc[q, z0], halo[G_CONC + q * DEPTH + z0])]
            c0 += [edge_u[side, t, q] for t in range(2)]
            cg = [ghost[side, 2 * t + q] for t in range(3)]

            def drive(e, g, both):
                if side == 0:
                    to_e = scatter(m_ref, g)
                    to_g = gather(m_ref, e) if both else None
                else:
                    to_e = gather(m_ref, g)
                    to_g = scatter(m_ref, e) if both else None
                flow = k_face * (g - e)
                return a0 * (flow + h * to_e), (ag * (h * to_g - flow) if both else None)

            kx0, ky0 = face_x(k0), face_y(k0)
            e1, d1 = drive(c0[0], cg[0], True)
            f1, g1 = drive(c0[1] + e1, cg[1] + d1, True)
            ghost_self = m_ref[10] if side == 0 else m_ref[9]
            d2 = d1 + g1 + ag * (
                in_plane(d1, face_x(kg), face_y(kg), vg) - (kg2 + h * ghost_self) * d1
            )
            hold = k01 + h * own_self
            e2 = e1 + f1 + a0 * (in_plane(e1, kx0, ky0, v0) - hold * e1)
            n2 = a1 * (k01 * e1)
            f2, _ = drive(c0[2] + e2, cg[2] + d2, False)
            e3 = e2 + f2 + a0 * (in_plane(e2, kx0, ky0, v0) - hold * e2 + k01 * n2)
            n3 = n2 + a1 * (
                in_plane(n2, face_x(k1), face_y(k1), v1) - (k01 + k12) * n2 + k01 * e2
            )
            m3 = a2 * (k12 * n2)
            out[q, z0] = u3[q, z0] + e3[:, :COLS]
            out[q, z1] = u3[q, z1] + n3[:, :COLS]
            out[q, z2] = u3[q, z2] + m3[:, :COLS]


def swap(value, axis, parity):
    count = lax.axis_size(axis)
    pairs = []
    for i in range(parity, count - 1, 2):
        pairs += [(i, i + 1), (i + 1, i)]
    return lax.ppermute(value, axis, pairs)


def shape(*dims):
    return jax.ShapeDtypeStruct(dims, jnp.float32)


def call(kernel, outs, scratch=(), cost=2_000_000):
    return pl.pallas_call(
        kernel,
        out_shape=outs,
        scratch_shapes=list(scratch),
        cost_estimate=pl.CostEstimate(flops=cost, bytes_accessed=2_000_000, transcendentals=0),
        compiler_params=pltpu.CompilerParams(vmem_limit_bytes=40 * 2**20),
    )


def per_device(conc, kappa, velocity, cell_type, target_row, target_col, mortar_weight):
    faces = (target_row, target_col, mortar_weight)
    fields = (conc, kappa, velocity, cell_type)
    tile = (ROWS, COLS)
    wide_tile = (ROWS, WIDE)
    msg = call(pack_kernel, shape(TILES, *tile))(*fields, *faces)
    got_b = swap(msg, "stream", 1)
    got_a = swap(msg, "stream", 0)
    u3, msg_a, msg_b, halo, edge_u, m = call(
        block_kernel,
        (
            shape(2, DEPTH, *tile),
            shape(PLANES + 1, *tile),
            shape(PLANES + 1, *tile),
            shape(GROUPS, *tile),
            shape(2, 2, 2, *wide_tile),
            shape(11, *wide_tile),
        ),
        (
            pltpu.VMEM((2, 2, DEPTH + 2) + wide_tile, jnp.float32),
            pltpu.VMEM((2, DEPTH) + wide_tile, jnp.float32),
            pltpu.VMEM((2, DEPTH) + wide_tile, jnp.float32),
            pltpu.VMEM((2, DEPTH + 1) + wide_tile, jnp.float32),
            pltpu.VMEM((DEPTH,) + wide_tile, jnp.float32),
        ),
    )(*fields, *faces, got_a, got_b)
    side_b = swap(msg_b, "slab", 1)
    side_a = swap(msg_a, "slab", 0)
    return call(
        join_kernel,
        shape(2, DEPTH, *tile),
        (pltpu.VMEM((2, PLANES) + wide_tile, jnp.float32),),
    )(*fields, halo, edge_u, m, u3, side_a, side_b)


def solution(mesh):
    return jax.shard_map(
        per_device,
        mesh=mesh,
        in_specs=(
            P(None, "slab", None, "stream"),
            P(None, "slab", None, "stream"),
            P("slab", None, "stream"),
            P("slab", None, "stream"),
            P(None, None, "stream"),
            P(None, None, "stream"),
            P(None, None, "stream"),
        ),
        out_specs=P(None, "slab", None, "stream"),
        check_vma=False,
    )
```

time: 197 us -> 44.9 us (0.23)
  starting transfers between devices: 103 us -> 11.3 us
  other arithmetic: 36.6 us -> 0 us
  waiting for transfers between devices: 41.1 us -> 14.8 us
  Pallas kernels: 0 us -> 11.8 us
  local copies, waits for them, and re-layouts: 13.6 us -> 6.5 us
    ppermute x25 -> x4, starting transfers between devices: 103 us -> 11.3 us  [swap(): return lax.ppermute(value, axis, pairs)]
    ppermute x25 -> x4, waiting for transfers between devices: 41.1 us -> 14.8 us  [swap(): return lax.ppermute(value, axis, pairs)]
    mul x20 -> x0, other arithmetic: 16.6 us -> none  [the longest x3 5.39 us: transport(): fz = 0.5 * (kz[:, 1:] + kz[:, :-1]) * (cz[:, 1:] - cz[:, :-1])]
    pallas_call x0 -> x3, Pallas kernels: none -> 11.8 us  [the longest x1 7.09 us: per_device(): call(block_kernel, (shape(2, DEPTH, *tile), shape(PLANES + 1, *tile), sha...]
    add x18 -> x0, other arithmetic: 9.69 us -> none  [the longest x6 3.42 us: spread(): part = part + hit * flux[:, intersection]]
    scatter-add x6 -> x0, other arithmetic: 5.98 us -> none  [per_device(): delta = delta.at[:, depth - 1].add(-loss).at[:, 0].add(gain)]
    ppermute x4 -> x0, local copies, waits for them, and re-layouts: 4.51 us -> none  [the longest x2 2.94 us: extended(): lax.ppermute(tail, axis, [(i, (i + 1) % count) for i in range(ends)])]
    unnamed x136 -> x14, local copies, waits for them, and re-layouts: 2.63 us -> 6.5 us
  transfers between devices with their start and end apart: 25 -> 4, of which waited for: 12 -> 3; matrix products, arithmetic and copies ran while one was open for 16% -> 0% of each run, Pallas kernels for 0% -> 0%
where the time goes in v1:
time: 44.9 us; the launch traced here: 44.5 us
  waiting for transfers between devices  14.8 us (33%)
  Pallas kernels  11.8 us (26%)
  starting transfers between devices  11.3 us (25%)
  local copies, waits for them, and re-layouts  6.5 us (14%)
    ppermute x4, waiting for transfers between devices, swap(): return lax.ppermute(value, axis, pairs)  14.8 us
    ppermute x4, starting transfers between devices, swap(): return lax.ppermute(value, axis, pairs)  11.3 us
    pallas_call x1, Pallas kernels, per_device(): call(block_kernel, (shape(2, DEPTH, *tile), shape(PLANES + 1, *tile), sha...  7.09 us
    unnamed x14, local copies, waits for them, and re-layouts  6.5 us
    pallas_call x1, Pallas kernels, per_device(): call(join_kernel, shape(2, DEPTH, *tile), (pltpu.VMEM((2, PLANES) + wide_...  4.21 us
  transfers between devices with their start and end apart: 4, of which 3 were waited for; matrix products, arithmetic and copies ran while one was open for 0% of the time, Pallas kernels for 0%

profile of v1, /device:TPU:121, one launch (start us, length us, event | category | flops | bytes accessed | tf_op | source)
XLA Modules:
  0.0 44.5 jit_solution(4748485679818554459)
XLA Ops:
  0.0 0.0 copy-start
  0.0 1.0 %copy-done = f32[2,8,64,128]{3,2,1,0:T(8,128)S(1)} copy-done((f32[2,8,64,128]{3,2,1,0:T(8,128)S(1)}, f32[2,8,64,128]{3,2,1,0:T(8,128)}, u32[]{:S(2)}) %copy-start) | copy-done | bytes 524312
  1.0 0.0 copy-start.1
  1.0 1.0 %copy-done.1 = f32[2,8,64,128]{3,2,1,0:T(8,128)S(1)} copy-done((f32[2,8,64,128]{3,2,1,0:T(8,128)S(1)}, f32[2,8,64,128]{3,2,1,0:T(8,128)}, u32[]{:S(2)}) %copy-start.1) | copy-done | bytes 524312
  2.1 0.0 copy-start.2
  2.1 0.9 %copy-done.2 = f32[8,64,128]{2,1,0:T(8,128)S(1)} copy-done((f32[8,64,128]{2,1,0:T(8,128)S(1)}, f32[8,64,128]{2,1,0:T(8,128)}, u32[]{:S(2)}) %copy-start.2) | copy-done | bytes 262168
  3.0 0.0 copy-start.3
  3.0 0.9 %copy-done.3 = s32[8,64,128]{2,1,0:T(8,128)S(1)} copy-done((s32[8,64,128]{2,1,0:T(8,128)S(1)}, s32[8,64,128]{2,1,0:T(8,128)}, u32[]{:S(2)}) %copy-start.3) | copy-done | bytes 262168
  4.0 0.0 copy-start.4
  4.0 0.8 %copy-done.4 = s32[2,64,128]{2,1,0:T(8,128)S(1)} copy-done((s32[2,64,128]{2,1,0:T(8,128)S(1)}, s32[2,64,128]{2,1,0:T(8,128)}, u32[]{:S(2)}) %copy-start.4) | copy-done | bytes 65560
  4.8 0.0 copy-start.5
  4.8 0.8 %copy-done.5 = s32[2,64,128]{2,1,0:T(8,128)S(1)} copy-done((s32[2,64,128]{2,1,0:T(8,128)S(1)}, s32[2,64,128]{2,1,0:T(8,128)}, u32[]{:S(2)}) %copy-start.5) | copy-done | bytes 65560
  5.7 0.0 copy-start.6
  5.7 0.8 %copy-done.6 = f32[2,64,128]{2,1,0:T(8,128)S(1)} copy-done((f32[2,64,128]{2,1,0:T(8,128)S(1)}, f32[2,64,128]{2,1,0:T(8,128)}, u32[]{:S(2)}) %copy-start.6) | copy-done | bytes 65560
  6.5 0.5 %shard_map.73 = f32[3,64,128]{2,1,0:T(8,128)S(1)} custom-call(f32[2,8,64,128]{3,2,1,0:T(8,128)S(1)} %copy-done, f32[2,8,64,128]{3,2,1,0:T(8,128)S(1)} %copy-done.1, f32[8,64,128]{2,1,0:T(8,128)S(1)} %copy-done.2, s32[8,64,128]{2,1,0:T(8,128)S(1)} %copy-done.3, s32[2,64,128]{2,1,0:T(8,128)S(1)} %copy-done.4, s32[2,64,128]{2,1,0:T(8,128)S(1)} %copy-done.5, ...), custom_call_target="tpu_custom_call" | custom-call | flops 2000000 | bytes 2000000 | tf_op jit(solution)/shard_map/pallas_call | solution.py:323
  7.0 5.5 %collective-permute-start.1 = (f32[3,64,128]{2,1,0:T(8,128)S(1)}, f32[3,64,128]{2,1,0:T(8,128)S(1)}, u32[]{:S(2)}, u32[]{:S(2)}) collective-permute-start(f32[3,64,128]{2,1,0:T(8,128)S(1)} %shard_map.73), channel_id=1, source_target_pairs={{8,16},{16,8},{24,32},{32,24},{40,48},{48,40},{56,64},{64,56},{72,... | collective-permute-start | bytes 294920 | tf_op jit(solution)/shard_map/ppermute | solution.py:301
  12.5 0.1 collective-permute-start
  12.6 2.4 %collective-permute-done.1.got_b = f32[3,64,128]{2,1,0:T(8,128)S(1)} collective-permute-done((f32[3,64,128]{2,1,0:T(8,128)S(1)}, f32[3,64,128]{2,1,0:T(8,128)S(1)}, u32[]{:S(2)}, u32[]{:S(2)}) %collective-permute-start.1) | collective-permute-done | bytes 98336 | tf_op jit(solution)/shard_map/ppermute | solution.py:301
  15.1 0.0 collective-permute-done.got_a
  15.1 7.1 %shard_map.74 = (f32[2,8,64,128]{3,2,1,0:T(8,128)S(1)}, f32[13,64,128]{2,1,0:T(8,128)S(1)}, f32[13,64,128]{2,1,0:T(8,128)S(1)}, f32[54,64,128]{2,1,0:T(8,128)S(1...) custom-call(f32[2,8,64,128]{3,2,1,0:T(8,128)S(1)} %copy-done, f32[2,8,64,128]{3,2,1,0:T(8,128)S(1)} %copy-done.1, ...), custom_call_target="tpu_custom_call" | custom-call | flops 2000000 | bytes 2000000 | tf_op jit(solution)/shard_map/pallas_call | solution.py:326
  22.2 1.3 %collective-permute-start.2 = (f32[13,64,128]{2,1,0:T(8,128)S(1)}, f32[13,64,128]{2,1,0:T(8,128)S(1)}, u32[]{:S(2)}, u32[]{:S(2)}) collective-permute-start(f32[13,64,128]{2,1,0:T(8,128)S(1)} %get-tuple-element.15), channel_id=1, source_target_pairs={{0,1},{1,0},{2,3},{3,2},{4,5},{5,4},{6,7},{7,6},{8,9},{9,8},{10,11... | collective-permute-start | bytes 1277960 | tf_op jit(solution)/shard_map/ppermute | solution.py:301
  23.5 4.4 %collective-permute-start.3 = (f32[13,64,128]{2,1,0:T(8,128)S(1)}, f32[13,64,128]{2,1,0:T(8,128)S(1)}, u32[]{:S(2)}, u32[]{:S(2)}) collective-permute-start(f32[13,64,128]{2,1,0:T(8,128)S(1)} %get-tuple-element.16), channel_id=1, source_target_pairs={{1,2},{2,1},{3,4},{4,3},{5,6},{6,5},{9,10},{10,9},{11,12},{12,11},... | collective-permute-start | bytes 1277960 | tf_op jit(solution)/shard_map/ppermute | solution.py:301
  27.9 5.7 %collective-permute-done.2.got_a = f32[13,64,128]{2,1,0:T(8,128)S(1)} collective-permute-done((f32[13,64,128]{2,1,0:T(8,128)S(1)}, f32[13,64,128]{2,1,0:T(8,128)S(1)}, u32[]{:S(2)}, u32[]{:S(2)}) %collective-permute-start.2) | collective-permute-done | bytes 426016 | tf_op jit(solution)/shard_map/ppermute | solution.py:301
  33.6 6.7 %collective-permute-done.3.got_b = f32[13,64,128]{2,1,0:T(8,128)S(1)} collective-permute-done((f32[13,64,128]{2,1,0:T(8,128)S(1)}, f32[13,64,128]{2,1,0:T(8,128)S(1)}, u32[]{:S(2)}, u32[]{:S(2)}) %collective-permute-start.3) | collective-permute-done | bytes 426016 | tf_op jit(solution)/shard_map/ppermute | solution.py:301
  40.3 4.2 %shard_map.75 = f32[2,8,64,128]{3,2,1,0:T(8,128)} custom-call(f32[2,8,64,128]{3,2,1,0:T(8,128)S(1)} %copy-done, f32[2,8,64,128]{3,2,1,0:T(8,128)S(1)} %copy-done.1, f32[8,64,128]{2,1,0:T(8,128)S(1)} %copy-done.2, s32[8,64,128]{2,1,0:T(8,128)S(1)} %copy-done.3, f32[54,64,128]{2,1,0:T(8,128)S(1)} %get-tuple-element.11.halo, ...), custom_call_target="tpu_custom_call" | custom-call | flops 2000000 | bytes 2000000 | tf_op jit(solution)/shard_map/pallas_call | solution.py:346
Async XLA Ops:
  0.0 1.0 %copy-start = (f32[2,8,64,128]{3,2,1,0:T(8,128)S(1)}, f32[2,8,64,128]{3,2,1,0:T(8,128)}, u32[]{:S(2)}) copy-start(f32[2,8,64,128]{3,2,1,0:T(8,128)} %conc.5) | copy-start | bytes 1572868
  1.0 1.0 %copy-start.1 = (f32[2,8,64,128]{3,2,1,0:T(8,128)S(1)}, f32[2,8,64,128]{3,2,1,0:T(8,128)}, u32[]{:S(2)}) copy-start(f32[2,8,64,128]{3,2,1,0:T(8,128)} %kappa.5) | copy-start | bytes 1572868
  2.1 0.9 %copy-start.2 = (f32[8,64,128]{2,1,0:T(8,128)S(1)}, f32[8,64,128]{2,1,0:T(8,128)}, u32[]{:S(2)}) copy-start(f32[8,64,128]{2,1,0:T(8,128)} %vel.5) | copy-start | bytes 786436
  3.0 0.9 %copy-start.3 = (s32[8,64,128]{2,1,0:T(8,128)S(1)}, s32[8,64,128]{2,1,0:T(8,128)}, u32[]{:S(2)}) copy-start(s32[8,64,128]{2,1,0:T(8,128)} %kind.5) | copy-start | bytes 786436
  4.0 0.8 %copy-start.4 = (s32[2,64,128]{2,1,0:T(8,128)S(1)}, s32[2,64,128]{2,1,0:T(8,128)}, u32[]{:S(2)}) copy-start(s32[2,64,128]{2,1,0:T(8,128)} %row_ref.3) | copy-start | bytes 196612
  4.8 0.8 %copy-start.5 = (s32[2,64,128]{2,1,0:T(8,128)S(1)}, s32[2,64,128]{2,1,0:T(8,128)}, u32[]{:S(2)}) copy-start(s32[2,64,128]{2,1,0:T(8,128)} %col_ref.3) | copy-start | bytes 196612
  5.7 0.8 %copy-start.6 = (f32[2,64,128]{2,1,0:T(8,128)S(1)}, f32[2,64,128]{2,1,0:T(8,128)}, u32[]{:S(2)}) copy-start(f32[2,64,128]{2,1,0:T(8,128)} %w_ref.3) | copy-start | bytes 196612
  7.0 8.0 %collective-permute-start.1 = (f32[3,64,128]{2,1,0:T(8,128)S(1)}, f32[3,64,128]{2,1,0:T(8,128)S(1)}, u32[]{:S(2)}, u32[]{:S(2)}) collective-permute-start(f32[3,64,128]{2,1,0:T(8,128)S(1)} %shard_map.73), channel_id=1, source_target_pairs={{8,16},{16,8},{24,32},{32,24},{40,48},{48,40},{56,64},{64,56},{72,... | collective-permute-start | bytes 294920 | tf_op jit(solution)/shard_map/ppermute | solution.py:301
  12.5 2.5 %collective-permute-start = (f32[3,64,128]{2,1,0:T(8,128)S(1)}, f32[3,64,128]{2,1,0:T(8,128)S(1)}, u32[]{:S(2)}, u32[]{:S(2)}) collective-permute-start(f32[3,64,128]{2,1,0:T(8,128)S(1)} %shard_map.73), channel_id=1, source_target_pairs={{0,8},{8,0},{16,24},{24,16},{32,40},{40,32},{48,56},{56,48},{64,72... | collective-permute-start | bytes 294920 | tf_op jit(solution)/shard_map/ppermute | solution.py:301
  22.2 11.4 %collective-permute-start.2 = (f32[13,64,128]{2,1,0:T(8,128)S(1)}, f32[13,64,128]{2,1,0:T(8,128)S(1)}, u32[]{:S(2)}, u32[]{:S(2)}) collective-permute-start(f32[13,64,128]{2,1,0:T(8,128)S(1)} %get-tuple-element.15), channel_id=1, source_target_pairs={{0,1},{1,0},{2,3},{3,2},{4,5},{5,4},{6,7},{7,6},{8,9},{9,8},{10,11... | collective-permute-start | bytes 1277960 | tf_op jit(solution)/shard_map/ppermute | solution.py:301
  23.5 16.8 %collective-permute-start.3 = (f32[13,64,128]{2,1,0:T(8,128)S(1)}, f32[13,64,128]{2,1,0:T(8,128)S(1)}, u32[]{:S(2)}, u32[]{:S(2)}) collective-permute-start(f32[13,64,128]{2,1,0:T(8,128)S(1)} %get-tuple-element.16), channel_id=1, source_target_pairs={{1,2},{2,1},{3,4},{4,3},{5,6},{6,5},{9,10},{10,9},{11,12},{12,11},... | collective-permute-start | bytes 1277960 | tf_op jit(solution)/shard_map/ppermute | solution.py:301

commit v2 on v1

v2 whole, which is shorter than its diff:
```python
import jax
import jax.numpy as jnp
from jax import lax
from jax.experimental import pallas as pl
from jax.experimental.pallas import tpu as pltpu
from jax.sharding import PartitionSpec as P

RATES = (0.08, 0.12)
DEPTH, ROWS, COLS = 8, 64, 128
WIDE = 2 * COLS
HALO = 3
GROUP = 2 * HALO
SLOTS = COLS // GROUP
PLANES = 12
G_CONC, G_KAPPA, G_VEL, G_TYPE, G_FACE, GROUPS = 0, 16, 32, 40, 48, 54
TILES = -(-GROUPS // SLOTS)


def lanes_of(shape):
    return lax.broadcasted_iota(jnp.int32, shape, len(shape) - 1)


def edge_mask():
    lane = lanes_of((ROWS, COLS))
    return (lane < HALO) | (lane >= COLS - HALO)


def place_group(tile, plane, slot):
    lane = lanes_of(tile.shape)
    start = slot * GROUP
    moved = pltpu.roll(plane, (start + HALO) % COLS, 1)
    return jnp.where((lane >= start) & (lane < start + GROUP), moved, tile)


def take_group(tile, slot):
    moved = pltpu.roll(tile, (COLS - slot * GROUP - HALO) % COLS, 1)
    return jnp.where(edge_mask(), moved, 0.0)


def wide(main, halo):
    return jnp.concatenate([main, halo], axis=1)


def shift_cols(x, by):
    return pltpu.roll(x, (-by) % x.shape[1], 1)


def shift_rows(x, by):
    return pltpu.roll(x, (-by) % x.shape[0], 0)


def in_plane(c, kx, ky, v):
    s = kx * (shift_cols(c, 1) - c) - v * c
    f = ky * (shift_rows(c, 1) - c)
    return (s - shift_cols(s, -1)) + (f - shift_rows(f, -1))


def face_x(k):
    return 0.5 * (k + shift_cols(k, 1))


def face_y(k):
    row = lax.broadcasted_iota(jnp.int32, k.shape, 0)
    return jnp.where(row < ROWS - 1, 0.5 * (k + shift_rows(k, 1)), 0.0)


def gather(m_ref, bed):
    total = None
    for b in (-1, 0, 1):
        at_b = shift_cols(bed, b) if b else bed
        for a in (-1, 0, 1):
            term = m_ref[3 * (a + 1) + b + 1] * (shift_rows(at_b, a) if a else at_b)
            total = term if total is None else total + term
    return total


def scatter(m_ref, water):
    total = None
    for b in (-1, 0, 1):
        part = None
        for a in (-1, 0, 1):
            term = m_ref[3 * (a + 1) + b + 1]
            if water is not None:
                term = term * water
            term = shift_rows(term, -a) if a else term
            part = term if part is None else part + term
        part = shift_cols(part, -b) if b else part
        total = part if total is None else total + part
    return total


def face_planes(row_ref, col_ref, w_ref):
    start = lax.axis_index("stream") * COLS
    row = lax.broadcasted_iota(jnp.int32, (ROWS, COLS), 0)
    col = lanes_of((ROWS, COLS)) + start
    out = [(row_ref[k] - row).astype(jnp.float32) for k in range(2)]
    out += [(col_ref[k] - col).astype(jnp.float32) for k in range(2)]
    return out + [w_ref[k] for k in range(2)]


def pack_kernel(
    conc_in, kappa_in, vel_in, kind_in, row_in, col_in, w_in,
    msg, conc, kappa, vel, active, faces,
    kind, row, col, w, sems,
):
    moves = [(conc_in, conc), (kappa_in, kappa), (vel_in, vel), (kind_in, kind)]
    moves += [(row_in, row), (col_in, col), (w_in, w)]
    copies = [pltpu.make_async_copy(*move, sems.at[i]) for i, move in enumerate(moves)]
    for copy in copies:
        copy.start()
    tiles = [jnp.zeros((ROWS, COLS), jnp.float32) for _ in range(TILES)]

    def put(group, plane):
        t, slot = divmod(group, SLOTS)
        tiles[t] = place_group(tiles[t], plane, slot)

    for q in range(2):
        if q == 0:
            copies[0].wait()
        for z in range(DEPTH):
            put(G_CONC + q * DEPTH + z, conc[q, z])
    copies[1].wait()
    for q in range(2):
        for z in range(DEPTH):
            put(G_KAPPA + q * DEPTH + z, kappa[q, z])
    copies[2].wait()
    copies[3].wait()
    for z in range(DEPTH):
        put(G_VEL + z, vel[z])
        on = kind[z].astype(jnp.float32)
        active[z] = on
        put(G_TYPE + z, on)
    for copy in copies[4:]:
        copy.wait()
    for i, plane in enumerate(face_planes(row, col, w)):
        faces[i] = plane
        put(G_FACE + i, plane)
    for t in range(TILES):
        msg[t] = tiles[t]


def merged(got_a, got_b):
    even = lax.axis_index("stream") % 2 == 0
    low = lax.rem(lanes_of((ROWS, COLS)), GROUP) < HALO
    return [jnp.where(low == even, got_b[t], got_a[t]) for t in range(TILES)]


def slab_flags():
    slab = lax.axis_index("slab")
    upper = (slab > 0).astype(jnp.float32)
    lower = (slab < lax.axis_size("slab") - 1).astype(jnp.float32)
    return slab % 2 == 0, upper, lower


def layers_of(side):
    return (0, 1, 2) if side == 0 else (DEPTH - 1, DEPTH - 2, DEPTH - 3)


def edge_kernel(conc, kappa, vel, active, faces, got_a, got_b, msg_a, msg_b, edge_u, m_out):
    tiles = merged(got_a, got_b)

    def halo(group):
        t, slot = divmod(group, SLOTS)
        return take_group(tiles[t], slot)

    planes = [wide(faces[i], halo(G_FACE + i)) for i in range(6)]
    rows_hit = [[planes[k] == a for a in (-1, 0, 1)] for k in range(2)]
    for b in (-1, 0, 1):
        parts = [jnp.where(planes[2 + k] == b, planes[4 + k], 0.0) for k in range(2)]
        for a in (-1, 0, 1):
            m_out[3 * (a + 1) + b + 1] = jnp.where(rows_hit[0][a + 1], parts[0], 0.0) + jnp.where(
                rows_hit[1][a + 1], parts[1], 0.0
            )
    m_out[9] = scatter(m_out, None)
    m_out[10] = planes[4] + planes[5]
    slab_even, upper, lower = slab_flags()

    sent = []
    for side in range(2):
        z0, z1, z2 = layers_of(side)
        own = m_out[9] * upper if side == 0 else m_out[10] * lower
        a0, a1 = [wide(active[z], halo(G_TYPE + z)) for z in (z0, z1)]
        v0, v1 = [wide(vel[z], halo(G_VEL + z)) for z in (z0, z1)]
        rows = [None] * PLANES
        for q in range(2):
            k0, k1, k2 = [wide(kappa[q, z], halo(G_KAPPA + q * DEPTH + z)) for z in (z0, z1, z2)]
            c0, c1, c2 = [wide(conc[q, z], halo(G_CONC + q * DEPTH + z)) for z in (z0, z1, z2)]
            kx0, ky0 = face_x(k0), face_y(k0)
            k01, k12 = 0.5 * (k0 + k1), 0.5 * (k1 + k2)
            hold = RATES[q] * own
            u0 = c0 + a0 * (in_plane(c0, kx0, ky0, v0) + k01 * (c1 - c0) - hold * c0)
            edge_u[side, 0, q] = u0
            u1 = c1 + a1 * (
                in_plane(c1, face_x(k1), face_y(k1), v1) + k12 * (c2 - c1) - k01 * (c1 - c0)
            )
            w0 = u0 + a0 * (in_plane(u0, kx0, ky0, v0) + k01 * (u1 - u0) - hold * u0)
            edge_u[side, 1, q] = w0
            rows[q], rows[2 + q], rows[4 + q] = c0, u0, w0
            rows[6 + q], rows[8 + q] = k0, k1
        rows[10], rows[11] = v0, a0
        sent.append(rows)

    strip_a = jnp.zeros((ROWS, COLS), jnp.float32)
    strip_b = strip_a
    for i, (top, bottom) in enumerate(zip(*sent)):
        to_a, to_b = jnp.where(slab_even, bottom, top), jnp.where(slab_even, top, bottom)
        msg_a[i] = to_a[:, :COLS]
        msg_b[i] = to_b[:, :COLS]
        strip_a = place_group(strip_a, to_a[:, COLS:], i)
        strip_b = place_group(strip_b, to_b[:, COLS:], i)
    msg_a[PLANES] = strip_a
    msg_b[PLANES] = strip_b


def block_kernel(
    conc, kappa, vel, active, m_ref, got_a, got_b,
    u3, coef, av,
    halo, cells, kx, ky, kz, own,
):
    for t, tile in enumerate(merged(got_a, got_b)):
        for slot in range(min(SLOTS, G_FACE - t * SLOTS)):
            halo[t * SLOTS + slot] = take_group(tile, slot)
    _, upper, lower = slab_flags()
    own[...] = jnp.zeros(own.shape, jnp.float32)
    own[0] = m_ref[9] * upper
    own[DEPTH - 1] = m_ref[10] * lower

    def prepare(z, _):
        for q in range(2):
            k = wide(kappa[q, z], halo[G_KAPPA + q * DEPTH + z])
            kx[q, z] = face_x(k)
            ky[q, z] = face_y(k)
            cells[0, q, z + 1] = wide(conc[q, z], halo[G_CONC + q * DEPTH + z])
        return 0

    lax.fori_loop(0, DEPTH, prepare, 0)

    def prepare_z(z, _):
        for q in range(2):
            k = wide(kappa[q, z], halo[G_KAPPA + q * DEPTH + z])
            below = wide(kappa[q, z + 1], halo[G_KAPPA + q * DEPTH + z + 1])
            kz[q, z + 1] = 0.5 * (k + below)
        return 0

    lax.fori_loop(0, DEPTH - 1, prepare_z, 0)
    zeros = jnp.zeros((ROWS, WIDE), jnp.float32)
    for q in range(2):
        kz[q, 0] = zeros
        kz[q, DEPTH] = zeros
        for t in range(2):
            cells[t, q, 0] = zeros
            cells[t, q, DEPTH + 1] = zeros

    for side in range(2):
        z0, z1, z2 = layers_of(side)
        f01, f12 = (1, 2) if side == 0 else (DEPTH - 1, DEPTH - 2)
        for i, z in enumerate((z0, z1, z2)):
            av[side, i] = wide(active[z], halo[G_TYPE + z])
        for i, z in enumerate((z0, z1)):
            av[side, 3 + i] = wide(vel[z], halo[G_VEL + z])
        for q in range(2):
            c0 = cells[0, q, z0 + 1]
            items = [kx[q, z0], ky[q, z0], kx[q, z1], ky[q, z1], kz[q, f01], kz[q, f12]]
            items.append(kz[q, f01] + RATES[q] * own[z0])
            items.append(RATES[q] * (gather(m_ref, c0) if side == 0 else scatter(m_ref, c0)))
            items.append(wide(kappa[q, z0], halo[G_KAPPA + q * DEPTH + z0]))
            items.append(c0)
            for i, item in enumerate(items):
                coef[side, q, i] = item

    for step in range(3):
        now, later = step % 2, (step + 1) % 2

        def advance(z, _):
            a = wide(active[z], halo[G_TYPE + z])
            v = wide(vel[z], halo[G_VEL + z])
            for q in range(2):
                c = cells[now, q, z + 1]
                r = in_plane(c, kx[q, z], ky[q, z], v)
                r += kz[q, z + 1] * (cells[now, q, z + 2] - c)
                r -= kz[q, z] * (c - cells[now, q, z])
                r -= RATES[q] * own[z] * c
                new = c + a * r
                if step == 2:
                    u3[q, z] = new[:, :COLS]
                else:
                    cells[later, q, z + 1] = new
            return 0

        lax.fori_loop(0, DEPTH, advance, 0)


def join_kernel(coef, av, edge_u, m_ref, u3, got_a, got_b, out, ghost, result, sems):
    copies = []

    def send(q, z, count):
        part = pl.ds(z, count)
        copy = pltpu.make_async_copy(result.at[q, part], out.at[q, part], sems.at[len(copies)])
        copy.start()
        copies.append(copy)

    for q in range(2):
        for z in range(3, DEPTH - 3):
            result[q, z] = u3[q, z]
        send(q, 3, DEPTH - 6)
    slab_even, _, _ = slab_flags()
    for side in range(2):
        first = slab_even if side == 1 else jnp.logical_not(slab_even)
        strip = jnp.where(first, got_a[PLANES], got_b[PLANES])
        for i in range(PLANES):
            ghost[side, i] = wide(jnp.where(first, got_a[i], got_b[i]), take_group(strip, i))

    for side in range(2):
        z0, z1, z2 = layers_of(side)
        a0, a1, a2, v0, v1 = [av[side, i] for i in range(5)]
        vg, ag = ghost[side, 10], ghost[side, 11]
        for q in range(2):
            h = RATES[q]
            kx0, ky0, kx1, ky1, k01, k12, hold, first_to_g, k0, first_c = [
                coef[side, q, i] for i in range(10)
            ]
            kg, kgg = ghost[side, 6 + q], ghost[side, 8 + q]
            k_face, kg2 = 0.5 * (kg + k0), 0.5 * (kg + kgg)
            own_c = [first_c, edge_u[side, 0, q], edge_u[side, 1, q]]
            ghost_c = [ghost[side, 2 * t + q] for t in range(3)]
            to_lower, to_upper = (gather, scatter) if side == 0 else (scatter, gather)

            g, e = ghost_c[0], own_c[0]
            flow = k_face * (g - e)
            e1 = a0 * (flow + h * to_upper(m_ref, g))
            d1 = ag * (first_to_g - flow)
            g, e = ghost_c[1] + d1, own_c[1] + e1
            flow = k_face * (g - e)
            ghost_self = m_ref[10] if side == 0 else m_ref[9]
            d2 = d1 + ag * (
                in_plane(d1, face_x(kg), face_y(kg), vg)
                - (kg2 + h * ghost_self) * d1
                + (h * to_lower(m_ref, e) - flow)
            )
            e2 = e1 + a0 * (
                in_plane(e1, kx0, ky0, v0) - hold * e1 + (flow + h * to_upper(m_ref, g))
            )
            n2 = a1 * (k01 * e1)
            g, e = ghost_c[2] + d2, own_c[2] + e2
            flow = k_face * (g - e)
            e3 = e2 + a0 * (
                in_plane(e2, kx0, ky0, v0) - hold * e2 + k01 * n2
                + (flow + h * to_upper(m_ref, g))
            )
            n3 = n2 + a1 * (in_plane(n2, kx1, ky1, v1) - (k01 + k12) * n2 + k01 * e2)
            m3 = a2 * (k12 * n2)
            result[q, z0] = u3[q, z0] + e3[:, :COLS]
            result[q, z1] = u3[q, z1] + n3[:, :COLS]
            result[q, z2] = u3[q, z2] + m3[:, :COLS]
            send(q, min(z0, z2), 3)
    for copy in copies:
        copy.wait()


def swap(value, axis, parity):
    count = lax.axis_size(axis)
    pairs = []
    for i in range(parity, count - 1, 2):
        pairs += [(i, i + 1), (i + 1, i)]
    return lax.ppermute(value, axis, pairs)


def shape(*dims):
    return jax.ShapeDtypeStruct(dims, jnp.float32)


def call(kernel, outs, scratch=(), **specs):
    return pl.pallas_call(
        kernel,
        out_shape=outs,
        scratch_shapes=list(scratch),
        cost_estimate=pl.CostEstimate(flops=2**21, bytes_accessed=2**21, transcendentals=0),
        compiler_params=pltpu.CompilerParams(vmem_limit_bytes=40 * 2**20),
        **specs,
    )


def per_device(conc, kappa, velocity, cell_type, target_row, target_col, mortar_weight):
    tile = (ROWS, COLS)
    wide_tile = (ROWS, WIDE)
    faces = (2,) + tile
    msg, *fields, offsets = call(
        pack_kernel,
        (
            shape(TILES, *tile),
            shape(2, DEPTH, *tile),
            shape(2, DEPTH, *tile),
            shape(DEPTH, *tile),
            shape(DEPTH, *tile),
            shape(6, *tile),
        ),
        (
            pltpu.VMEM((DEPTH,) + tile, jnp.int32),
            pltpu.VMEM(faces, jnp.int32),
            pltpu.VMEM(faces, jnp.int32),
            pltpu.VMEM(faces, jnp.float32),
            pltpu.SemaphoreType.DMA((7,)),
        ),
        in_specs=[pl.BlockSpec(memory_space=pl.ANY)] * 7,
    )(
        *[
            pltpu.with_memory_space_constraint(x, pltpu.HBM)
            for x in (conc, kappa, velocity, cell_type, target_row, target_col, mortar_weight)
        ]
    )
    got_b = swap(msg, "stream", 1)
    got_a = swap(msg, "stream", 0)
    msg_a, msg_b, edge_u, m = call(
        edge_kernel,
        (
            shape(PLANES + 1, *tile),
            shape(PLANES + 1, *tile),
            shape(2, 2, 2, *wide_tile),
            shape(11, *wide_tile),
        ),
    )(*fields, offsets, got_a, got_b)
    side_b = swap(msg_b, "slab", 1)
    side_a = swap(msg_a, "slab", 0)
    u3, coef, av = call(
        block_kernel,
        (
            shape(2, DEPTH, *tile),
            shape(2, 2, 10, *wide_tile),
            shape(2, 5, *wide_tile),
        ),
        (
            pltpu.VMEM((G_FACE,) + tile, jnp.float32),
            pltpu.VMEM((2, 2, DEPTH + 2) + wide_tile, jnp.float32),
            pltpu.VMEM((2, DEPTH) + wide_tile, jnp.float32),
            pltpu.VMEM((2, DEPTH) + wide_tile, jnp.float32),
            pltpu.VMEM((2, DEPTH + 1) + wide_tile, jnp.float32),
            pltpu.VMEM((DEPTH,) + wide_tile, jnp.float32),
        ),
    )(*fields, m, got_a, got_b)
    return call(
        join_kernel,
        shape(2, DEPTH, *tile),
        (
            pltpu.VMEM((2, PLANES) + wide_tile, jnp.float32),
            pltpu.VMEM((2, DEPTH) + tile, jnp.float32),
            pltpu.SemaphoreType.DMA((6,)),
        ),
        out_specs=pl.BlockSpec(memory_space=pl.ANY),
    )(coef, av, edge_u, m, u3, side_a, side_b)


def solution(mesh):
    return jax.shard_map(
        per_device,
        mesh=mesh,
        in_specs=(
            P(None, "slab", None, "stream"),
            P(None, "slab", None, "stream"),
            P("slab", None, "stream"),
            P("slab", None, "stream"),
            P(None, None, "stream"),
            P(None, None, "stream"),
            P(None, None, "stream"),
        ),
        out_specs=P(None, "slab", None, "stream"),
        check_vma=False,
    )
```

time: 44.9 us -> 33.9 us (0.76)
  waiting for transfers between devices: 14.8 us -> 7.92 us
  local copies, waits for them, and re-layouts: 6.5 us -> 0 us
  Pallas kernels: 11.8 us -> 14.5 us
    ppermute x4, waiting for transfers between devices: 14.8 us -> 7.92 us  [swap(): return lax.ppermute(value, axis, pairs)]
    unnamed x14 -> x0, local copies, waits for them, and re-layouts: 6.5 us -> none
    pallas_call x2 -> x3, Pallas kernels: 7.61 us -> 10.9 us  [the longest x1 6.92 us: per_device(): call(block_kernel, (shape(2, DEPTH, *tile), shape(2, 2, 10, *wide_tile),...]
    pallas_call x1, Pallas kernels: 4.21 us -> 3.6 us  [per_device(): call(join_kernel, shape(2, DEPTH, *tile), (pltpu.VMEM((2, PLANES) + wide_...]
  transfers between devices with their start and end apart: 4 -> 4, of which waited for: 3 -> 2; matrix products, arithmetic and copies ran while one was open for 0% -> 0% of each run, Pallas kernels for 0% -> 20%
where the time goes in v2:
time: 33.9 us; the launch traced here: 33.8 us
  Pallas kernels  14.5 us (43%)
  starting transfers between devices  11.3 us (33%)
  waiting for transfers between devices  7.92 us (23%)
    ppermute x4, starting transfers between devices, swap(): return lax.ppermute(value, axis, pairs)  11.3 us
    ppermute x4, waiting for transfers between devices, swap(): return lax.ppermute(value, axis, pairs)  7.92 us
    pallas_call x1, Pallas kernels, per_device(): call(block_kernel, (shape(2, DEPTH, *tile), shape(2, 2, 10, *wide_tile),...  6.92 us
    pallas_call x1, Pallas kernels, per_device(): call(join_kernel, shape(2, DEPTH, *tile), (pltpu.VMEM((2, PLANES) + wide_...  3.6 us
    pallas_call x1, Pallas kernels, per_device(): call(edge_kernel, (shape(PLANES + 1, *tile), shape(PLANES + 1, *tile), sh...  2.17 us
    pallas_call x1, Pallas kernels, per_device(): call(pack_kernel, (shape(TILES, *tile), shape(2, DEPTH, *tile), shape(2,...  1.83 us
  transfers between devices with their start and end apart: 4, of which 2 were waited for; matrix products, arithmetic and copies ran while one was open for 0% of the time, Pallas kernels for 20%

profile of v2, /device:TPU:121, one launch (start us, length us, event | category | flops | bytes accessed | tf_op | source)
XLA Modules:
  0.0 33.8 jit_solution(14760085456145743166)
XLA Ops:
  0.0 1.8 %shard_map.73 = (f32[3,64,128]{2,1,0:T(8,128)S(1)}, f32[2,8,64,128]{3,2,1,0:T(8,128)S(1)}, f32[2,8,64,128]{3,2,1,0:T(8,128)S(1)}, f32[8,64,128]{2,1,0:T(8,128)S(...) custom-call(f32[2,8,64,128]{3,2,1,0:T(8,128)} %conc_in.1, f32[2,8,64,128]{3,2,1,0:T(8,128)} %kappa_in.1, ...), custom_call_target="tpu_custom_call" | custom-call | flops 2097152 | bytes 2097152 | tf_op jit(solution)/shard_map/pallas_call | solution.py:387
  1.8 5.5 %collective-permute-start.1 = (f32[3,64,128]{2,1,0:T(8,128)S(1)}, f32[3,64,128]{2,1,0:T(8,128)S(1)}, u32[]{:S(2)}, u32[]{:S(2)}) collective-permute-start(f32[3,64,128]{2,1,0:T(8,128)S(1)} %get-tuple-element.23), channel_id=1, source_target_pairs={{8,16},{16,8},{24,32},{32,24},{40,48},{48,40},{56,64},{64,56},{72,... | collective-permute-start | bytes 294920 | tf_op jit(solution)/shard_map/ppermute | solution.py:365
  7.3 0.1 collective-permute-start
  7.4 2.4 %collective-permute-done.1.got_b = f32[3,64,128]{2,1,0:T(8,128)S(1)} collective-permute-done((f32[3,64,128]{2,1,0:T(8,128)S(1)}, f32[3,64,128]{2,1,0:T(8,128)S(1)}, u32[]{:S(2)}, u32[]{:S(2)}) %collective-permute-start.1) | collective-permute-done | bytes 98336 | tf_op jit(solution)/shard_map/ppermute | solution.py:365
  9.9 0.0 collective-permute-done.got_a
  9.9 2.2 %shard_map.74 = (f32[13,64,128]{2,1,0:T(8,128)S(1)}, f32[13,64,128]{2,1,0:T(8,128)S(1)}, f32[2,2,2,64,256]{4,3,2,1,0:T(8,128)S(1)}, f32[11,64,256]{2,1,0:T(8,128)S(1)}) custom-call(f32[2,8,64,128]{3,2,1,0:T(8,128)S(1)} %get-tuple-element.18.conc, f32[2,8,64,128]{3,2,1,0:T(8,128)S(1)} %get-tuple-element.19.kappa, f32[8,64,128]{2,1,0:T(8,128)S(1)} %get-tuple-element.20.vel, ...), custom_call_target="tpu_custom_call" | custom-call | flops 2097152 | bytes 2097152 | tf_op jit(solution)/shard_map/pallas_call | solution.py:413
  12.1 1.3 %collective-permute-start.2 = (f32[13,64,128]{2,1,0:T(8,128)S(1)}, f32[13,64,128]{2,1,0:T(8,128)S(1)}, u32[]{:S(2)}, u32[]{:S(2)}) collective-permute-start(f32[13,64,128]{2,1,0:T(8,128)S(1)} %get-tuple-element.29), channel_id=1, source_target_pairs={{0,1},{1,0},{2,3},{3,2},{4,5},{5,4},{6,7},{7,6},{8,9},{9,8},{10,11... | collective-permute-start | bytes 1277960 | tf_op jit(solution)/shard_map/ppermute | solution.py:365
  13.4 4.4 %collective-permute-start.3 = (f32[13,64,128]{2,1,0:T(8,128)S(1)}, f32[13,64,128]{2,1,0:T(8,128)S(1)}, u32[]{:S(2)}, u32[]{:S(2)}) collective-permute-start(f32[13,64,128]{2,1,0:T(8,128)S(1)} %get-tuple-element.30), channel_id=1, source_target_pairs={{1,2},{2,1},{3,4},{4,3},{5,6},{6,5},{9,10},{10,9},{11,12},{12,11},... | collective-permute-start | bytes 1277960 | tf_op jit(solution)/shard_map/ppermute | solution.py:365
  17.8 6.9 %shard_map.75 = (f32[2,8,64,128]{3,2,1,0:T(8,128)S(1)}, f32[2,2,10,64,256]{4,3,2,1,0:T(8,128)S(1)}, f32[2,5,64,256]{3,2,1,0:T(8,128)S(1)}) custom-call(f32[2,8,64,128]{3,2,1,0:T(8,128)S(1)} %get-tuple-element.18.conc, f32[2,8,64,128]{3,2,1,0:T(8,128)S(1)} %get-tuple-element.19.kappa, f32[8,64,128]{2,1,0:T(8,128)S(1)} %get-tuple-element.20.vel, ...), custom_call_target="tpu_custom_call" | custom-call | flops 2097152 | bytes 2097152 | tf_op jit(solution)/shard_map/pallas_call | solution.py:424
  24.7 0.0 collective-permute-done.2.got_a
  24.7 5.5 %collective-permute-done.3.got_b = f32[13,64,128]{2,1,0:T(8,128)S(1)} collective-permute-done((f32[13,64,128]{2,1,0:T(8,128)S(1)}, f32[13,64,128]{2,1,0:T(8,128)S(1)}, u32[]{:S(2)}, u32[]{:S(2)}) %collective-permute-start.3) | collective-permute-done | bytes 426016 | tf_op jit(solution)/shard_map/ppermute | solution.py:365
  30.2 3.6 %shard_map.76 = f32[2,8,64,128]{3,2,1,0:T(8,128)} custom-call(f32[2,2,10,64,256]{4,3,2,1,0:T(8,128)S(1)} %get-tuple-element.25.coef, f32[2,5,64,256]{3,2,1,0:T(8,128)S(1)} %get-tuple-element.26.av, f32[2,2,2,64,256]{4,3,2,1,0:T(8,128)S(1)} %get-tuple-element.27.edge_u, f32[11,64,256]{2,1,0:T(8,128)S(1)} %get-tuple-element.24.m_ref, ...), custom_call_target="tpu_custom_call" | custom-call | flops 2097152 | bytes 2097152 | tf_op jit(solution)/shard_map/pallas_call | solution.py:440
Async XLA Ops:
  1.8 8.0 %collective-permute-start.1 = (f32[3,64,128]{2,1,0:T(8,128)S(1)}, f32[3,64,128]{2,1,0:T(8,128)S(1)}, u32[]{:S(2)}, u32[]{:S(2)}) collective-permute-start(f32[3,64,128]{2,1,0:T(8,128)S(1)} %get-tuple-element.23), channel_id=1, source_target_pairs={{8,16},{16,8},{24,32},{32,24},{40,48},{48,40},{56,64},{64,56},{72,... | collective-permute-start | bytes 294920 | tf_op jit(solution)/shard_map/ppermute | solution.py:365
  7.3 2.5 %collective-permute-start = (f32[3,64,128]{2,1,0:T(8,128)S(1)}, f32[3,64,128]{2,1,0:T(8,128)S(1)}, u32[]{:S(2)}, u32[]{:S(2)}) collective-permute-start(f32[3,64,128]{2,1,0:T(8,128)S(1)} %get-tuple-element.23), channel_id=1, source_target_pairs={{0,8},{8,0},{16,24},{24,16},{32,40},{40,32},{48,56},{56,48},{64,72... | collective-permute-start | bytes 294920 | tf_op jit(solution)/shard_map/ppermute | solution.py:365
  12.1 12.6 %collective-permute-start.2 = (f32[13,64,128]{2,1,0:T(8,128)S(1)}, f32[13,64,128]{2,1,0:T(8,128)S(1)}, u32[]{:S(2)}, u32[]{:S(2)}) collective-permute-start(f32[13,64,128]{2,1,0:T(8,128)S(1)} %get-tuple-element.29), channel_id=1, source_target_pairs={{0,1},{1,0},{2,3},{3,2},{4,5},{5,4},{6,7},{7,6},{8,9},{9,8},{10,11... | collective-permute-start | bytes 1277960 | tf_op jit(solution)/shard_map/ppermute | solution.py:365
  13.4 16.8 %collective-permute-start.3 = (f32[13,64,128]{2,1,0:T(8,128)S(1)}, f32[13,64,128]{2,1,0:T(8,128)S(1)}, u32[]{:S(2)}, u32[]{:S(2)}) collective-permute-start(f32[13,64,128]{2,1,0:T(8,128)S(1)} %get-tuple-element.30), channel_id=1, source_target_pairs={{1,2},{2,1},{3,4},{4,3},{5,6},{6,5},{9,10},{10,9},{11,12},{12,11},... | collective-permute-start | bytes 1277960 | tf_op jit(solution)/shard_map/ppermute | solution.py:365

commit v3 on v2

--- a/solution.py
+++ b/solution.py
@@ -11,7 +11,7 @@
 HALO = 3
 GROUP = 2 * HALO
 SLOTS = COLS // GROUP
-PLANES = 12
+PLANES, RAW, LATE = 12, 8, 4
 G_CONC, G_KAPPA, G_VEL, G_TYPE, G_FACE, GROUPS = 0, 16, 32, 40, 48, 54
 TILES = -(-GROUPS // SLOTS)
 
@@ -100,11 +100,17 @@
 
 def pack_kernel(
     conc_in, kappa_in, vel_in, kind_in, row_in, col_in, w_in,
-    msg, conc, kappa, vel, active, faces,
+    msg, raw_a, raw_b, conc, kappa, vel, active, faces,
     kind, row, col, w, sems,
 ):
     moves = [(conc_in, conc), (kappa_in, kappa), (vel_in, vel), (kind_in, kind)]
     moves += [(row_in, row), (col_in, col), (w_in, w)]
+    slab_even, _, _ = slab_flags()
+    for raw, lower in ((raw_a, slab_even), (raw_b, jnp.logical_not(slab_even))):
+        first = jnp.where(lower, DEPTH - 1, 0)
+        second = jnp.where(lower, DEPTH - 2, 1)
+        moves += [(conc_in.at[:, first], raw.at[0:2]), (kappa_in.at[:, first], raw.at[2:4])]
+        moves += [(kappa_in.at[:, second], raw.at[4:6]), (vel_in.at[first], raw.at[6])]
     copies = [pltpu.make_async_copy(*move, sems.at[i]) for i, move in enumerate(moves)]
     for copy in copies:
         copy.start()
@@ -130,6 +136,8 @@
         on = kind[z].astype(jnp.float32)
         active[z] = on
         put(G_TYPE + z, on)
+    for raw, lower in ((raw_a, slab_even), (raw_b, jnp.logical_not(slab_even))):
+        raw[7] = jnp.where(lower, active[DEPTH - 1], active[0])
     for copy in copies[4:]:
         copy.wait()
     for i, plane in enumerate(face_planes(row, col, w)):
@@ -195,21 +203,22 @@
             )
             w0 = u0 + a0 * (in_plane(u0, kx0, ky0, v0) + k01 * (u1 - u0) - hold * u0)
             edge_u[side, 1, q] = w0
-            rows[q], rows[2 + q], rows[4 + q] = c0, u0, w0
-            rows[6 + q], rows[8 + q] = k0, k1
-        rows[10], rows[11] = v0, a0
+            rows[q], rows[2 + q], rows[4 + q] = c0, k0, k1
+            rows[RAW + q], rows[RAW + 2 + q] = u0, w0
+        rows[6], rows[7] = v0, a0
         sent.append(rows)
 
     strip_a = jnp.zeros((ROWS, COLS), jnp.float32)
     strip_b = strip_a
     for i, (top, bottom) in enumerate(zip(*sent)):
         to_a, to_b = jnp.where(slab_even, bottom, top), jnp.where(slab_even, top, bottom)
-        msg_a[i] = to_a[:, :COLS]
-        msg_b[i] = to_b[:, :COLS]
+        if i >= RAW:
+            msg_a[i - RAW] = to_a[:, :COLS]
+            msg_b[i - RAW] = to_b[:, :COLS]
         strip_a = place_group(strip_a, to_a[:, COLS:], i)
         strip_b = place_group(strip_b, to_b[:, COLS:], i)
-    msg_a[PLANES] = strip_a
-    msg_b[PLANES] = strip_b
+    msg_a[LATE] = strip_a
+    msg_b[LATE] = strip_b
 
 
 def block_kernel(
@@ -290,7 +299,7 @@
         lax.fori_loop(0, DEPTH, advance, 0)
 
 
-def join_kernel(coef, av, edge_u, m_ref, u3, got_a, got_b, out, ghost, result, sems):
+def join_kernel(coef, av, edge_u, m_ref, u3, raw_a, raw_b, got_a, got_b, out, ghost, result, sems):
     copies = []
 
     def send(q, z, count):
@@ -306,23 +315,24 @@
     slab_even, _, _ = slab_flags()
     for side in range(2):
         first = slab_even if side == 1 else jnp.logical_not(slab_even)
-        strip = jnp.where(first, got_a[PLANES], got_b[PLANES])
+        strip = jnp.where(first, got_a[LATE], got_b[LATE])
         for i in range(PLANES):
-            ghost[side, i] = wide(jnp.where(first, got_a[i], got_b[i]), take_group(strip, i))
+            from_a, from_b = (raw_a[i], raw_b[i]) if i < RAW else (got_a[i - RAW], got_b[i - RAW])
+            ghost[side, i] = wide(jnp.where(first, from_a, from_b), take_group(strip, i))
 
     for side in range(2):
         z0, z1, z2 = layers_of(side)
         a0, a1, a2, v0, v1 = [av[side, i] for i in range(5)]
-        vg, ag = ghost[side, 10], ghost[side, 11]
+        vg, ag = ghost[side, 6], ghost[side, 7]
         for q in range(2):
             h = RATES[q]
             kx0, ky0, kx1, ky1, k01, k12, hold, first_to_g, k0, first_c = [
                 coef[side, q, i] for i in range(10)
             ]
-            kg, kgg = ghost[side, 6 + q], ghost[side, 8 + q]
+            kg, kgg = ghost[side, 2 + q], ghost[side, 4 + q]
             k_face, kg2 = 0.5 * (kg + k0), 0.5 * (kg + kgg)
             own_c = [first_c, edge_u[side, 0, q], edge_u[side, 1, q]]
-            ghost_c = [ghost[side, 2 * t + q] for t in range(3)]
+            ghost_c = [ghost[side, i + q] for i in (0, RAW, RAW + 2)]
             to_lower, to_upper = (gather, scatter) if side == 0 else (scatter, gather)
 
             g, e = ghost_c[0], own_c[0]
@@ -384,10 +394,12 @@
     tile = (ROWS, COLS)
     wide_tile = (ROWS, WIDE)
     faces = (2,) + tile
-    msg, *fields, offsets = call(
+    msg, raw_a, raw_b, *fields, offsets = call(
         pack_kernel,
         (
             shape(TILES, *tile),
+            shape(RAW, *tile),
+            shape(RAW, *tile),
             shape(2, DEPTH, *tile),
             shape(2, DEPTH, *tile),
             shape(DEPTH, *tile),
@@ -399,7 +411,7 @@
             pltpu.VMEM(faces, jnp.int32),
             pltpu.VMEM(faces, jnp.int32),
             pltpu.VMEM(faces, jnp.float32),
-            pltpu.SemaphoreType.DMA((7,)),
+            pltpu.SemaphoreType.DMA((15,)),
         ),
         in_specs=[pl.BlockSpec(memory_space=pl.ANY)] * 7,
     )(
@@ -410,11 +422,13 @@
     )
     got_b = swap(msg, "stream", 1)
     got_a = swap(msg, "stream", 0)
+    raw_b = swap(raw_b, "slab", 1)
+    raw_a = swap(raw_a, "slab", 0)
     msg_a, msg_b, edge_u, m = call(
         edge_kernel,
         (
-            shape(PLANES + 1, *tile),
-            shape(PLANES + 1, *tile),
+            shape(LATE + 1, *tile),
+            shape(LATE + 1, *tile),
             shape(2, 2, 2, *wide_tile),
             shape(11, *wide_tile),
         ),
@@ -446,7 +460,7 @@
             pltpu.SemaphoreType.DMA((6,)),
         ),
         out_specs=pl.BlockSpec(memory_space=pl.ANY),
-    )(coef, av, edge_u, m, u3, side_a, side_b)
+    )(coef, av, edge_u, m, u3, raw_a, raw_b, side_a, side_b)
 
 
 def solution(mesh):

time: 33.9 us -> 31.4 us (0.926)
  the two profiles are of different devices: /device:TPU:121 before, /device:TPU:120 now
where the time goes in v3:
time: 31.4 us; the launch traced here: 31.2 us
  starting transfers between devices  16.5 us (53%)
  Pallas kernels  14.6 us (46%)
    ppermute x6, starting transfers between devices, swap(): return lax.ppermute(value, axis, pairs)  16.5 us
    pallas_call x1, Pallas kernels, per_device(): call(block_kernel, (shape(2, DEPTH, *tile), shape(2, 2, 10, *wide_tile),...  6.92 us
    pallas_call x1, Pallas kernels, per_device(): call(join_kernel, shape(2, DEPTH, *tile), (pltpu.VMEM((2, PLANES) + wide_...  3.62 us
    pallas_call x1, Pallas kernels, per_device(): call(edge_kernel, (shape(LATE + 1, *tile), shape(LATE + 1, *tile), shape(...  2.17 us
    pallas_call x1, Pallas kernels, per_device(): call(pack_kernel, (shape(TILES, *tile), shape(RAW, *tile), shape(RAW, *ti...  1.92 us
  transfers between devices with their start and end apart: 6, of which 0 were waited for; matrix products, arithmetic and copies ran while one was open for 0% of the time, Pallas kernels for 29%

profile of v3, /device:TPU:120, one launch (start us, length us, event | category | flops | bytes accessed | tf_op | source)
XLA Modules:
  0.0 31.2 jit_solution(17166605662262569732)
XLA Ops:
  0.0 1.9 %shard_map.73 = (f32[3,64,128]{2,1,0:T(8,128)S(1)}, f32[8,64,128]{2,1,0:T(8,128)S(1)}, f32[8,64,128]{2,1,0:T(8,128)S(1)}, f32[2,8,64,128]{3,2,1,0:T(8,128)S(1)},...) custom-call(f32[2,8,64,128]{3,2,1,0:T(8,128)} %conc_in.1, ...), custom_call_target="tpu_custom_call" | custom-call | flops 2097152 | bytes 2097152 | tf_op jit(solution)/shard_map/pallas_call | solution.py:397
  1.9 2.1 %collective-permute-start.1 = (f32[3,64,128]{2,1,0:T(8,128)S(1)}, f32[3,64,128]{2,1,0:T(8,128)S(1)}, u32[]{:S(2)}, u32[]{:S(2)}) collective-permute-start(f32[3,64,128]{2,1,0:T(8,128)S(1)} %get-tuple-element.25), channel_id=1, source_target_pairs={{8,16},{16,8},{24,32},{32,24},{40,48},{48,40},{56,64},{64,56},{72,... | collective-permute-start | bytes 294920 | tf_op jit(solution)/shard_map/ppermute | solution.py:375
  4.0 3.3 %collective-permute-start = (f32[3,64,128]{2,1,0:T(8,128)S(1)}, f32[3,64,128]{2,1,0:T(8,128)S(1)}, u32[]{:S(2)}, u32[]{:S(2)}) collective-permute-start(f32[3,64,128]{2,1,0:T(8,128)S(1)} %get-tuple-element.25), channel_id=1, source_target_pairs={{0,8},{8,0},{16,24},{24,16},{32,40},{40,32},{48,56},{56,48},{64,72... | collective-permute-start | bytes 294920 | tf_op jit(solution)/shard_map/ppermute | solution.py:375
  7.4 1.5 %collective-permute-start.2 = (f32[8,64,128]{2,1,0:T(8,128)S(1)}, f32[8,64,128]{2,1,0:T(8,128)S(1)}, u32[]{:S(2)}, u32[]{:S(2)}) collective-permute-start(f32[8,64,128]{2,1,0:T(8,128)S(1)} %get-tuple-element.31), channel_id=1, source_target_pairs={{0,1},{1,0},{2,3},{3,2},{4,5},{5,4},{6,7},{7,6},{8,9},{9,8},{10,11... | collective-permute-start | bytes 786440 | tf_op jit(solution)/shard_map/ppermute | solution.py:375
  8.8 4.4 %collective-permute-start.3 = (f32[8,64,128]{2,1,0:T(8,128)S(1)}, f32[8,64,128]{2,1,0:T(8,128)S(1)}, u32[]{:S(2)}, u32[]{:S(2)}) collective-permute-start(f32[8,64,128]{2,1,0:T(8,128)S(1)} %get-tuple-element.32), channel_id=1, source_target_pairs={{1,2},{2,1},{3,4},{4,3},{5,6},{6,5},{9,10},{10,9},{11,12},{12,11},... | collective-permute-start | bytes 786440 | tf_op jit(solution)/shard_map/ppermute | solution.py:375
  13.2 0.0 collective-permute-done.1.got_b
  13.2 0.0 collective-permute-done.got_a
  13.2 2.2 %shard_map.74 = (f32[5,64,128]{2,1,0:T(8,128)S(1)}, f32[5,64,128]{2,1,0:T(8,128)S(1)}, f32[2,2,2,64,256]{4,3,2,1,0:T(8,128)S(1)}, f32[11,64,256]{2,1,0:T(8,128)S(1)}) custom-call(f32[2,8,64,128]{3,2,1,0:T(8,128)S(1)} %get-tuple-element.20.conc, f32[2,8,64,128]{3,2,1,0:T(8,128)S(1)} %get-tuple-element.21.kappa, f32[8,64,128]{2,1,0:T(8,128)S(1)} %get-tuple-element.22.vel, ...), custom_call_target="tpu_custom_call" | custom-call | flops 2097152 | bytes 2097152 | tf_op jit(solution)/shard_map/pallas_call | solution.py:427
  15.4 0.3 collective-permute-start.4
  15.7 4.9 %collective-permute-start.5 = (f32[5,64,128]{2,1,0:T(8,128)S(1)}, f32[5,64,128]{2,1,0:T(8,128)S(1)}, u32[]{:S(2)}, u32[]{:S(2)}) collective-permute-start(f32[5,64,128]{2,1,0:T(8,128)S(1)} %get-tuple-element.34), channel_id=1, source_target_pairs={{1,2},{2,1},{3,4},{4,3},{5,6},{6,5},{9,10},{10,9},{11,12},{12,11},... | collective-permute-start | bytes 491528 | tf_op jit(solution)/shard_map/ppermute | solution.py:375
  20.6 6.9 %shard_map.75 = (f32[2,8,64,128]{3,2,1,0:T(8,128)S(1)}, f32[2,2,10,64,256]{4,3,2,1,0:T(8,128)S(1)}, f32[2,5,64,256]{3,2,1,0:T(8,128)S(1)}) custom-call(f32[2,8,64,128]{3,2,1,0:T(8,128)S(1)} %get-tuple-element.20.conc, f32[2,8,64,128]{3,2,1,0:T(8,128)S(1)} %get-tuple-element.21.kappa, f32[8,64,128]{2,1,0:T(8,128)S(1)} %get-tuple-element.22.vel, ...), custom_call_target="tpu_custom_call" | custom-call | flops 2097152 | bytes 2097152 | tf_op jit(solution)/shard_map/pallas_call | solution.py:438
  27.5 0.0 collective-permute-done.2.raw_a
  27.5 0.0 collective-permute-done.3.raw_b
  27.6 0.0 collective-permute-done.4.got_a
  27.6 0.0 collective-permute-done.5.got_b
  27.6 3.6 %shard_map.76 = f32[2,8,64,128]{3,2,1,0:T(8,128)} custom-call(f32[2,2,10,64,256]{4,3,2,1,0:T(8,128)S(1)} %get-tuple-element.27.coef, f32[2,5,64,256]{3,2,1,0:T(8,128)S(1)} %get-tuple-element.28.av, f32[2,2,2,64,256]{4,3,2,1,0:T(8,128)S(1)} %get-tuple-element.29.edge_u, f32[11,64,256]{2,1,0:T(8,128)S(1)} %get-tuple-element.26.m_ref, ...), custom_call_target="tpu_custom_call" | custom-call | flops 2097152 | bytes 2097152 | tf_op jit(solution)/shard_map/pallas_call | solution.py:454
Async XLA Ops:
  1.9 11.3 %collective-permute-start.1 = (f32[3,64,128]{2,1,0:T(8,128)S(1)}, f32[3,64,128]{2,1,0:T(8,128)S(1)}, u32[]{:S(2)}, u32[]{:S(2)}) collective-permute-start(f32[3,64,128]{2,1,0:T(8,128)S(1)} %get-tuple-element.25), channel_id=1, source_target_pairs={{8,16},{16,8},{24,32},{32,24},{40,48},{48,40},{56,64},{64,56},{72,... | collective-permute-start | bytes 294920 | tf_op jit(solution)/shard_map/ppermute | solution.py:375
  4.0 9.2 %collective-permute-start = (f32[3,64,128]{2,1,0:T(8,128)S(1)}, f32[3,64,128]{2,1,0:T(8,128)S(1)}, u32[]{:S(2)}, u32[]{:S(2)}) collective-permute-start(f32[3,64,128]{2,1,0:T(8,128)S(1)} %get-tuple-element.25), channel_id=1, source_target_pairs={{0,8},{8,0},{16,24},{24,16},{32,40},{40,32},{48,56},{56,48},{64,72... | collective-permute-start | bytes 294920 | tf_op jit(solution)/shard_map/ppermute | solution.py:375
  7.4 20.2 %collective-permute-start.2 = (f32[8,64,128]{2,1,0:T(8,128)S(1)}, f32[8,64,128]{2,1,0:T(8,128)S(1)}, u32[]{:S(2)}, u32[]{:S(2)}) collective-permute-start(f32[8,64,128]{2,1,0:T(8,128)S(1)} %get-tuple-element.31), channel_id=1, source_target_pairs={{0,1},{1,0},{2,3},{3,2},{4,5},{5,4},{6,7},{7,6},{8,9},{9,8},{10,11... | collective-permute-start | bytes 786440 | tf_op jit(solution)/shard_map/ppermute | solution.py:375
  8.8 18.7 %collective-permute-start.3 = (f32[8,64,128]{2,1,0:T(8,128)S(1)}, f32[8,64,128]{2,1,0:T(8,128)S(1)}, u32[]{:S(2)}, u32[]{:S(2)}) collective-permute-start(f32[8,64,128]{2,1,0:T(8,128)S(1)} %get-tuple-element.32), channel_id=1, source_target_pairs={{1,2},{2,1},{3,4},{4,3},{5,6},{6,5},{9,10},{10,9},{11,12},{12,11},... | collective-permute-start | bytes 786440 | tf_op jit(solution)/shard_map/ppermute | solution.py:375
  15.4 12.1 %collective-permute-start.4 = (f32[5,64,128]{2,1,0:T(8,128)S(1)}, f32[5,64,128]{2,1,0:T(8,128)S(1)}, u32[]{:S(2)}, u32[]{:S(2)}) collective-permute-start(f32[5,64,128]{2,1,0:T(8,128)S(1)} %get-tuple-element.33), channel_id=1, source_target_pairs={{0,1},{1,0},{2,3},{3,2},{4,5},{5,4},{6,7},{7,6},{8,9},{9,8},{10,11... | collective-permute-start | bytes 491528 | tf_op jit(solution)/shard_map/ppermute | solution.py:375
  15.7 11.8 %collective-permute-start.5 = (f32[5,64,128]{2,1,0:T(8,128)S(1)}, f32[5,64,128]{2,1,0:T(8,128)S(1)}, u32[]{:S(2)}, u32[]{:S(2)}) collective-permute-start(f32[5,64,128]{2,1,0:T(8,128)S(1)} %get-tuple-element.34), channel_id=1, source_target_pairs={{1,2},{2,1},{3,4},{4,3},{5,6},{6,5},{9,10},{10,9},{11,12},{12,11},... | collective-permute-start | bytes 491528 | tf_op jit(solution)/shard_map/ppermute | solution.py:375

commit v4 on v0

v4 whole, which is shorter than its diff:
```python
import jax
import jax.numpy as jnp
from jax import lax
from jax.experimental import pallas as pl
from jax.experimental.pallas import tpu as pltpu
from jax.sharding import PartitionSpec as P

RATES = (0.08, 0.12)
DEPTH, ROWS, COLS = 8, 64, 128
LANES = 2 * ROWS
EDGE = 8
TALL = COLS + 2 * EDGE
G_CONC, G_KAPPA, G_VT, G_FACE, GROUPS = 0, 8, 16, 24, 27
RAW = 4
LATE = 2 * TALL + RAW * 2 * EDGE


def first_half(shape):
    return lax.broadcasted_iota(jnp.int32, shape, 1) < ROWS


def halves(x, y):
    return jnp.where(first_half(x.shape), x, y)


def doubled(x):
    other = pltpu.roll(x, ROWS, 1)
    return halves(x, other), halves(other, x)


def shift_cols(x, by):
    return pltpu.roll(x, (-by) % x.shape[0], 0)


def shift_rows(x, by):
    return pltpu.roll(x, (-by) % LANES, 1)


def in_plane(c, kx, ky, v):
    s = kx * (shift_cols(c, 1) - c) - v * c
    f = ky * (shift_rows(c, 1) - c)
    return (s - shift_cols(s, -1)) + (f - shift_rows(f, -1))


def face_x(k):
    return 0.5 * (k + shift_cols(k, 1))


def face_y(k):
    row = lax.rem(lax.broadcasted_iota(jnp.int32, k.shape, 1), ROWS)
    return jnp.where(row < ROWS - 1, 0.5 * (k + shift_rows(k, 1)), 0.0)


def gather(m_ref, bed):
    total = None
    for a in (-1, 0, 1):
        at_a = shift_rows(bed, a) if a else bed
        for b in (-1, 0, 1):
            term = m_ref[3 * (a + 1) + b + 1] * (shift_cols(at_a, b) if b else at_a)
            total = term if total is None else total + term
    return total


def scatter(m_ref, water):
    total = None
    for a in (-1, 0, 1):
        part = None
        for b in (-1, 0, 1):
            term = m_ref[3 * (a + 1) + b + 1]
            if water is not None:
                term = term * water
            term = shift_cols(term, -b) if b else term
            part = term if part is None else part + term
        part = shift_rows(part, -a) if a else part
        total = part if total is None else total + part
    return total


def slab_flags():
    slab = lax.axis_index("slab")
    upper = (slab > 0).astype(jnp.float32)
    lower = (slab < lax.axis_size("slab") - 1).astype(jnp.float32)
    return slab % 2 == 0, upper, lower


def stream_even():
    return lax.axis_index("stream") % 2 == 0


def layers_of(side):
    return (0, 1, 2) if side == 0 else (DEPTH - 1, DEPTH - 2, DEPTH - 3)


def pack_kernel(
    conc_in, kappa_in, vel_in, kind_in, row_in, col_in, w_in,
    msg_a, msg_b, raw_a, raw_b, conc, kappa, vel, active, faces,
    conc_s, kappa_s, vel_s, kind_s, row_s, col_s, w_s, sems,
):
    moves = [(conc_in, conc_s), (kappa_in, kappa_s), (vel_in, vel_s), (kind_in, kind_s)]
    moves += [(row_in, row_s), (col_in, col_s), (w_in, w_s)]
    copies = [pltpu.make_async_copy(*move, sems.at[i]) for i, move in enumerate(moves)]
    for copy in copies:
        copy.start()
    even = stream_even()
    slab_even, _, _ = slab_flags()

    def turned(first, second):
        return jnp.concatenate([first, second], axis=0).T

    def put(group, plane):
        head, tail = plane[:EDGE], plane[COLS - EDGE :]
        msg_a[group] = jnp.where(even, tail, head)
        msg_b[group] = jnp.where(even, head, tail)

    def put_raw(i, top, bottom):
        raw_a[i] = jnp.where(slab_even, bottom, top)
        raw_b[i] = jnp.where(slab_even, top, bottom)

    copies[0].wait()
    for z in range(DEPTH):
        conc[z] = turned(conc_s[0, z], conc_s[1, z])
        put(G_CONC + z, conc[z])
    copies[1].wait()
    for z in range(DEPTH):
        kappa[z] = turned(kappa_s[0, z], kappa_s[1, z])
        put(G_KAPPA + z, kappa[z])
    copies[2].wait()
    copies[3].wait()
    for z in range(DEPTH):
        on = kind_s[z].astype(jnp.float32)
        vel[z] = turned(vel_s[z], vel_s[z])
        active[z] = turned(on, on)
        put(G_VT + z, halves(vel[z], active[z]))
    for copy in copies[4:]:
        copy.wait()
    row = lax.broadcasted_iota(jnp.int32, (ROWS, COLS), 0)
    col = lax.broadcasted_iota(jnp.int32, (ROWS, COLS), 1) + lax.axis_index("stream") * COLS
    for k in range(2):
        offsets = (row_s[k] - row).astype(jnp.float32), (col_s[k] - col).astype(jnp.float32)
        for i, item in enumerate(offsets + (w_s[k],)):
            faces[2 * i + k] = turned(item, item)
    for i in range(3):
        put(G_FACE + i, halves(faces[2 * i], faces[2 * i + 1]))
    last = DEPTH - 1
    put_raw(0, conc[0], conc[last])
    put_raw(1, kappa[0], kappa[last])
    put_raw(2, kappa[1], kappa[last - 1])
    put_raw(3, halves(vel[0], active[0]), halves(vel[last], active[last]))


class Halo:
    def __init__(self, got_a, got_b):
        self.got = got_a, got_b
        self.even = stream_even()

    def sides(self, group):
        a, b = self.got[0][group], self.got[1][group]
        return jnp.where(self.even, b, a), jnp.where(self.even, a, b)

    def plane(self, ref, z, group):
        left, right = self.sides(group + z)
        return jnp.concatenate([left, ref[z], right], axis=0)

    def pair(self, refs, places, group):
        left, right = [doubled(x) for x in self.sides(group)]
        return [
            jnp.concatenate([left[i], refs[i][places[i]], right[i]], axis=0) for i in range(2)
        ]

    def motion(self, vel, active, z):
        return self.pair((vel, active), (z, z), G_VT + z)


def edge_kernel(conc, kappa, vel, active, faces, got_a, got_b, msg_a, msg_b, edge_u, m_out):
    halo = Halo(got_a, got_b)
    planes = [halo.pair((faces, faces), (2 * i, 2 * i + 1), G_FACE + i) for i in range(3)]
    rate = jnp.where(first_half((TALL, LANES)), RATES[0], RATES[1])
    weights = [rate * planes[2][k] for k in range(2)]
    for a in (-1, 0, 1):
        parts = [jnp.where(planes[0][k] == a, weights[k], 0.0) for k in range(2)]
        for b in (-1, 0, 1):
            hits = [jnp.where(planes[1][k] == b, parts[k], 0.0) for k in range(2)]
            m_out[3 * (a + 1) + b + 1] = hits[0] + hits[1]
    m_out[9] = scatter(m_out, None)
    m_out[10] = weights[0] + weights[1]
    slab_even, upper, lower = slab_flags()

    sent = []
    for side in range(2):
        z0, z1, z2 = layers_of(side)
        hold = m_out[9] * upper if side == 0 else m_out[10] * lower
        (v0, a0), (v1, a1) = [halo.motion(vel, active, z) for z in (z0, z1)]
        k0, k1, k2 = [halo.plane(kappa, z, G_KAPPA) for z in (z0, z1, z2)]
        c0, c1, c2 = [halo.plane(conc, z, G_CONC) for z in (z0, z1, z2)]
        kx0, ky0 = face_x(k0), face_y(k0)
        k01, k12 = 0.5 * (k0 + k1), 0.5 * (k1 + k2)
        flow = k01 * (c1 - c0)
        u0 = c0 + a0 * (in_plane(c0, kx0, ky0, v0) + flow - hold * c0)
        edge_u[side, 0] = u0
        u1 = c1 + a1 * (in_plane(c1, face_x(k1), face_y(k1), v1) + k12 * (c2 - c1) - flow)
        w0 = u0 + a0 * (in_plane(u0, kx0, ky0, v0) + k01 * (u1 - u0) - hold * u0)
        edge_u[side, 1] = w0
        sent.append((u0, w0, c0, k0, k1, halves(v0, a0)))

    for i, (top, bottom) in enumerate(zip(*sent)):
        for msg, low in ((msg_a, slab_even), (msg_b, jnp.logical_not(slab_even))):
            if i < 2:
                msg[pl.ds(i * TALL, TALL)] = jnp.where(low, bottom, top)
            else:
                start = 2 * TALL + (i - 2) * 2 * EDGE
                msg[pl.ds(start, EDGE)] = jnp.where(low, bottom[:EDGE], top[:EDGE])
                msg[pl.ds(start + EDGE, EDGE)] = jnp.where(
                    low, bottom[TALL - EDGE :], top[TALL - EDGE :]
                )


def block_kernel(
    conc, kappa, vel, active, m_ref, got_a, got_b,
    u3, middle, coef, av,
    cells, kx, ky, kz, own, move, on,
):
    halo = Halo(got_a, got_b)
    _, upper, lower = slab_flags()
    zeros = jnp.zeros((TALL, LANES), jnp.float32)
    for z in range(1, DEPTH - 1):
        own[z] = zeros
    own[0] = m_ref[9] * upper
    own[DEPTH - 1] = m_ref[10] * lower
    above = None
    for z in range(DEPTH):
        k = halo.plane(kappa, z, G_KAPPA)
        kx[z] = face_x(k)
        ky[z] = face_y(k)
        kz[z] = zeros if above is None else 0.5 * (above + k)
        above = k
        cells[0, z + 1] = halo.plane(conc, z, G_CONC)
        move[z], on[z] = halo.motion(vel, active, z)
    kz[DEPTH] = zeros
    for t in range(2):
        cells[t, 0] = zeros
        cells[t, DEPTH + 1] = zeros

    for side in range(2):
        z0, z1, z2 = layers_of(side)
        f01, f12 = (1, 2) if side == 0 else (DEPTH - 1, DEPTH - 2)
        for i, z in enumerate((z0, z1, z2)):
            av[side, i] = on[z]
        for i, z in enumerate((z0, z1)):
            av[side, 3 + i] = move[z]
        c0 = cells[0, z0 + 1]
        items = [kx[z0], ky[z0], kx[z1], ky[z1], kz[f01], kz[f12], kz[f01] + own[z0]]
        items.append(gather(m_ref, c0) if side == 0 else scatter(m_ref, c0))
        items += [halo.plane(kappa, z0, G_KAPPA), c0]
        for i, item in enumerate(items):
            coef[side, i] = item

    for step in range(3):
        now, later = step % 2, (step + 1) % 2

        def advance(z, _):
            c = cells[now, z + 1]
            r = in_plane(c, kx[z], ky[z], move[z])
            r += kz[z + 1] * (cells[now, z + 2] - c) - kz[z] * (c - cells[now, z]) - own[z] * c
            new = c + on[z] * r
            if step == 2:
                u3[z] = new[EDGE : EDGE + COLS]
            else:
                cells[later, z + 1] = new
            return 0

        lax.fori_loop(0, DEPTH, advance, 0)
    for z in range(3, DEPTH - 3):
        back = u3[z].T
        middle[0, z - 3] = back[:ROWS]
        middle[1, z - 3] = back[ROWS:]


def join_kernel(
    coef, av, edge_u, m_ref, u3, middle, raw_a, raw_b, got_a, got_b, out, ghost, result, sems
):
    copies = []

    def send(source, z, count):
        target = out.at[:, pl.ds(z, count)]
        copies.append(pltpu.make_async_copy(source, target, sems.at[len(copies)]))
        copies[-1].start()

    send(middle, 3, DEPTH - 6)
    slab_even, _, _ = slab_flags()
    for side in range(2):
        first = slab_even if side == 1 else jnp.logical_not(slab_even)
        for i in range(2):
            part = pl.ds(i * TALL, TALL)
            ghost[side, i] = jnp.where(first, got_a[part], got_b[part])
        for i in range(RAW):
            left = pl.ds(2 * TALL + i * 2 * EDGE, EDGE)
            right = pl.ds(2 * TALL + i * 2 * EDGE + EDGE, EDGE)
            ghost[side, 2 + i, pl.ds(0, EDGE)] = jnp.where(first, got_a[left], got_b[left])
            ghost[side, 2 + i, pl.ds(EDGE, COLS)] = jnp.where(first, raw_a[i], raw_b[i])
            ghost[side, 2 + i, pl.ds(EDGE + COLS, EDGE)] = jnp.where(
                first, got_a[right], got_b[right]
            )

    for side in range(2):
        z0, z1, z2 = layers_of(side)
        a0, a1, a2, v0, v1 = [av[side, i] for i in range(5)]
        kx0, ky0, kx1, ky1, k01, k12, hold, first_to_g, k0, first_c = [
            coef[side, i] for i in range(10)
        ]
        kg, kgg = ghost[side, 3], ghost[side, 4]
        vg, ag = doubled(ghost[side, 5])
        k_face, kg2 = 0.5 * (kg + k0), 0.5 * (kg + kgg)
        own_c = [first_c, edge_u[side, 0], edge_u[side, 1]]
        ghost_c = [ghost[side, i] for i in (2, 0, 1)]
        to_lower, to_upper = (gather, scatter) if side == 0 else (scatter, gather)

        g, e = ghost_c[0], own_c[0]
        flow = k_face * (g - e)
        e1 = a0 * (flow + to_upper(m_ref, g))
        d1 = ag * (first_to_g - flow)
        g, e = ghost_c[1] + d1, own_c[1] + e1
        flow = k_face * (g - e)
        ghost_self = m_ref[10] if side == 0 else m_ref[9]
        d2 = d1 + ag * (
            in_plane(d1, face_x(kg), face_y(kg), vg)
            - (kg2 + ghost_self) * d1
            + (to_lower(m_ref, e) - flow)
        )
        e2 = e1 + a0 * (in_plane(e1, kx0, ky0, v0) - hold * e1 + (flow + to_upper(m_ref, g)))
        n2 = a1 * (k01 * e1)
        g, e = ghost_c[2] + d2, own_c[2] + e2
        flow = k_face * (g - e)
        e3 = e2 + a0 * (
            in_plane(e2, kx0, ky0, v0) - hold * e2 + k01 * n2 + (flow + to_upper(m_ref, g))
        )
        n3 = n2 + a1 * (in_plane(n2, kx1, ky1, v1) - (k01 + k12) * n2 + k01 * e2)
        m3 = a2 * (k12 * n2)
        low = min(z0, z2)
        for z, x in ((z0, e3), (z1, n3), (z2, m3)):
            back = (u3[z] + x[EDGE : EDGE + COLS]).T
            result[side, 0, z - low] = back[:ROWS]
            result[side, 1, z - low] = back[ROWS:]
        send(result.at[side], low, 3)
    for copy in copies:
        copy.wait()


def swap(value, axis, parity):
    count = lax.axis_size(axis)
    pairs = []
    for i in range(parity, count - 1, 2):
        pairs += [(i, i + 1), (i + 1, i)]
    return lax.ppermute(value, axis, pairs)


def shape(*dims):
    return jax.ShapeDtypeStruct(dims, jnp.float32)


def call(kernel, outs, scratch=(), **specs):
    return pl.pallas_call(
        kernel,
        out_shape=outs,
        scratch_shapes=list(scratch),
        cost_estimate=pl.CostEstimate(flops=2**21, bytes_accessed=2**21, transcendentals=0),
        compiler_params=pltpu.CompilerParams(vmem_limit_bytes=40 * 2**20),
        **specs,
    )


def per_device(conc, kappa, velocity, cell_type, target_row, target_col, mortar_weight):
    tile = (ROWS, COLS)
    plane = (COLS, LANES)
    tall = (TALL, LANES)
    messages = [shape(GROUPS, EDGE, LANES)] * 2 + [shape(RAW, *plane)] * 2
    msg_a, msg_b, raw_a, raw_b, *fields, faces = call(
        pack_kernel,
        messages + [shape(DEPTH, *plane)] * 4 + [shape(6, *plane)],
        (
            pltpu.VMEM((2, DEPTH) + tile, jnp.float32),
            pltpu.VMEM((2, DEPTH) + tile, jnp.float32),
            pltpu.VMEM((DEPTH,) + tile, jnp.float32),
            pltpu.VMEM((DEPTH,) + tile, jnp.int32),
            pltpu.VMEM((2,) + tile, jnp.int32),
            pltpu.VMEM((2,) + tile, jnp.int32),
            pltpu.VMEM((2,) + tile, jnp.float32),
            pltpu.SemaphoreType.DMA((7,)),
        ),
        in_specs=[pl.BlockSpec(memory_space=pl.ANY)] * 7,
    )(
        *[
            pltpu.with_memory_space_constraint(x, pltpu.HBM)
            for x in (conc, kappa, velocity, cell_type, target_row, target_col, mortar_weight)
        ]
    )
    got_b = swap(msg_b, "stream", 1)
    got_a = swap(msg_a, "stream", 0)
    raw_b = swap(raw_b, "slab", 1)
    raw_a = swap(raw_a, "slab", 0)
    late_a, late_b, edge_u, m = call(
        edge_kernel,
        (shape(LATE, LANES), shape(LATE, LANES), shape(2, 2, *tall), shape(11, *tall)),
    )(*fields, faces, got_a, got_b)
    late_b = swap(late_b, "slab", 1)
    late_a = swap(late_a, "slab", 0)
    u3, middle, coef, av = call(
        block_kernel,
        (
            shape(DEPTH, *plane),
            shape(2, DEPTH - 6, *tile),
            shape(2, 10, *tall),
            shape(2, 5, *tall),
        ),
        (
            pltpu.VMEM((2, DEPTH + 2) + tall, jnp.float32),
            pltpu.VMEM((DEPTH,) + tall, jnp.float32),
            pltpu.VMEM((DEPTH,) + tall, jnp.float32),
            pltpu.VMEM((DEPTH + 1,) + tall, jnp.float32),
            pltpu.VMEM((DEPTH,) + tall, jnp.float32),
            pltpu.VMEM((DEPTH,) + tall, jnp.float32),
            pltpu.VMEM((DEPTH,) + tall, jnp.float32),
        ),
    )(*fields, m, got_a, got_b)
    return call(
        join_kernel,
        shape(2, DEPTH, *tile),
        (
            pltpu.VMEM((2, 2 + RAW) + tall, jnp.float32),
            pltpu.VMEM((2, 2, 3) + tile, jnp.float32),
            pltpu.SemaphoreType.DMA((3,)),
        ),
        out_specs=pl.BlockSpec(memory_space=pl.ANY),
    )(coef, av, edge_u, m, u3, middle, raw_a, raw_b, late_a, late_b)


def solution(mesh):
    return jax.shard_map(
        per_device,
        mesh=mesh,
        in_specs=(
            P(None, "slab", None, "stream"),
            P(None, "slab", None, "stream"),
            P("slab", None, "stream"),
            P("slab", None, "stream"),
            P(None, None, "stream"),
            P(None, None, "stream"),
            P(None, None, "stream"),
        ),
        out_specs=P(None, "slab", None, "stream"),
        check_vma=False,
    )
```

time: 197 us -> 27.9 us (0.14)
  starting transfers between devices: 103 us -> 15.9 us
  waiting for transfers between devices: 41.1 us -> 1.46 us
  other arithmetic: 36.6 us -> 0 us
  local copies, waits for them, and re-layouts: 13.6 us -> 0 us
  Pallas kernels: 0 us -> 9.99 us
    ppermute x25 -> x6, starting transfers between devices: 103 us -> 15.9 us  [swap(): return lax.ppermute(value, axis, pairs)]
    ppermute x25 -> x6, waiting for transfers between devices: 41.1 us -> 1.46 us  [swap(): return lax.ppermute(value, axis, pairs)]
    mul x20 -> x0, other arithmetic: 16.6 us -> none  [the longest x3 5.39 us: transport(): fz = 0.5 * (kz[:, 1:] + kz[:, :-1]) * (cz[:, 1:] - cz[:, :-1])]
    pallas_call x0 -> x4, Pallas kernels: none -> 9.99 us  [the longest x1 4.68 us: per_device(): call(block_kernel, (shape(DEPTH, *plane), shape(2, DEPTH - 6, *tile), sha...]
    add x18 -> x0, other arithmetic: 9.69 us -> none  [the longest x6 3.42 us: spread(): part = part + hit * flux[:, intersection]]
    scatter-add x6 -> x0, other arithmetic: 5.98 us -> none  [per_device(): delta = delta.at[:, depth - 1].add(-loss).at[:, 0].add(gain)]
    ppermute x4 -> x0, local copies, waits for them, and re-layouts: 4.51 us -> none  [the longest x2 2.94 us: extended(): lax.ppermute(tail, axis, [(i, (i + 1) % count) for i in range(ends)])]
    slice x32 -> x0, local copies, waits for them, and re-layouts: 3.71 us -> none  [the longest x4 1.81 us: extended(): lax.slice_in_dim(cells, cells.shape[dim] - width, cells.shape[dim], axis=...]
  transfers between devices with their start and end apart: 25 -> 6, of which waited for: 12 -> 1; matrix products, arithmetic and copies ran while one was open for 16% -> 0% of each run, Pallas kernels for 0% -> 20%
where the time goes in v4:
time: 27.9 us; the launch traced here: 27.4 us
  starting transfers between devices  15.9 us (57%)
  Pallas kernels  9.99 us (36%)
  waiting for transfers between devices  1.46 us (5%)
    ppermute x6, starting transfers between devices, swap(): return lax.ppermute(value, axis, pairs)  15.9 us
    pallas_call x1, Pallas kernels, per_device(): call(block_kernel, (shape(DEPTH, *plane), shape(2, DEPTH - 6, *tile), sha...  4.68 us
    pallas_call x1, Pallas kernels, per_device(): call(join_kernel, shape(2, DEPTH, *tile), (pltpu.VMEM((2, 2 + RAW) + tall...  2.39 us
    pallas_call x1, Pallas kernels, per_device(): call(pack_kernel, messages + [shape(DEPTH, *plane)] * 4 + [shape(6, *plan...  2.07 us
    ppermute x6, waiting for transfers between devices, swap(): return lax.ppermute(value, axis, pairs)  1.46 us
    pallas_call x1, Pallas kernels, per_device(): call(edge_kernel, (shape(LATE, LANES), shape(LATE, LANES), shape(2, 2, *t...  0.85 us
  transfers between devices with their start and end apart: 6, of which 1 were waited for; matrix products, arithmetic and copies ran while one was open for 0% of the time, Pallas kernels for 20%

profile of v4, /device:TPU:121, one launch (start us, length us, event | category | flops | bytes accessed | tf_op | source)
XLA Modules:
  0.0 27.4 jit_solution(10226762167656067317)
XLA Ops:
  0.0 2.1 %shard_map.73 = (f32[27,8,128]{2,1,0:T(8,128)S(1)}, f32[27,8,128]{2,1,0:T(8,128)S(1)}, f32[4,128,128]{2,1,0:T(8,128)S(1)}, f32[4,128,128]{2,1,0:T(8,128)S(1)}, f...) custom-call(f32[2,8,64,128]{3,2,1,0:T(8,128)} %conc_in.1, ...), custom_call_target="tpu_custom_call" | custom-call | flops 2097152 | bytes 2097152 | tf_op jit(solution)/shard_map/pallas_call | solution.py:376
  2.1 0.8 %collective-permute-start = (f32[27,8,128]{2,1,0:T(8,128)S(1)}, f32[27,8,128]{2,1,0:T(8,128)S(1)}, u32[]{:S(2)}, u32[]{:S(2)}) collective-permute-start(f32[27,8,128]{2,1,0:T(8,128)S(1)} %get-tuple-element.27), channel_id=1, source_target_pairs={{0,8},{8,0},{16,24},{24,16},{32,40},{40,32},{48,56},{56,48},{64,72... | collective-permute-start | bytes 331784 | tf_op jit(solution)/shard_map/ppermute | solution.py:353
  2.8 4.8 %collective-permute-start.1 = (f32[27,8,128]{2,1,0:T(8,128)S(1)}, f32[27,8,128]{2,1,0:T(8,128)S(1)}, u32[]{:S(2)}, u32[]{:S(2)}) collective-permute-start(f32[27,8,128]{2,1,0:T(8,128)S(1)} %get-tuple-element.28), channel_id=1, source_target_pairs={{8,16},{16,8},{24,32},{32,24},{40,48},{48,40},{56,64},{64,56},{72,... | collective-permute-start | bytes 331784 | tf_op jit(solution)/shard_map/ppermute | solution.py:353
  7.7 1.3 %collective-permute-start.2 = (f32[4,128,128]{2,1,0:T(8,128)S(1)}, f32[4,128,128]{2,1,0:T(8,128)S(1)}, u32[]{:S(2)}, u32[]{:S(2)}) collective-permute-start(f32[4,128,128]{2,1,0:T(8,128)S(1)} %get-tuple-element.35), channel_id=1, source_target_pairs={{0,1},{1,0},{2,3},{3,2},{4,5},{5,4},{6,7},{7,6},{8,9},{9,8},{10,11... | collective-permute-start | bytes 786440 | tf_op jit(solution)/shard_map/ppermute | solution.py:353
  9.0 4.1 %collective-permute-start.3 = (f32[4,128,128]{2,1,0:T(8,128)S(1)}, f32[4,128,128]{2,1,0:T(8,128)S(1)}, u32[]{:S(2)}, u32[]{:S(2)}) collective-permute-start(f32[4,128,128]{2,1,0:T(8,128)S(1)} %get-tuple-element.36), channel_id=1, source_target_pairs={{1,2},{2,1},{3,4},{4,3},{5,6},{6,5},{9,10},{10,9},{11,12},{12,11},... | collective-permute-start | bytes 786440 | tf_op jit(solution)/shard_map/ppermute | solution.py:353
  13.1 0.0 collective-permute-done.got_a
  13.1 0.0 collective-permute-done.1.got_b
  13.1 0.8 %shard_map.74 = (f32[352,128]{1,0:T(8,128)S(1)}, f32[352,128]{1,0:T(8,128)S(1)}, f32[2,2,144,128]{3,2,1,0:T(8,128)S(1)}, f32[11,144,128]{2,1,0:T(8,128)S(1)}) custom-call(f32[8,128,128]{2,1,0:T(8,128)S(1)} %get-tuple-element.22.conc, f32[8,128,128]{2,1,0:T(8,128)S(1)} %get-tuple-element.23.kappa, f32[8,128,128]{2,1,0:T(8,128)S(1)} %get-tuple-element.24.vel, ...), custom_call_target="tpu_custom_call" | custom-call | flops 2097152 | bytes 2097152 | tf_op jit(solution)/shard_map/pallas_call | solution.py:400
  14.0 0.1 collective-permute-start.4
  14.1 4.8 %collective-permute-start.5 = (f32[352,128]{1,0:T(8,128)S(1)}, f32[352,128]{1,0:T(8,128)S(1)}, u32[]{:S(2)}, u32[]{:S(2)}) collective-permute-start(f32[352,128]{1,0:T(8,128)S(1)} %get-tuple-element.38), channel_id=1, source_target_pairs={{1,2},{2,1},{3,4},{4,3},{5,6},{6,5},{9,10},{10,9},{11,12},{12,11},... | collective-permute-start | bytes 540680 | tf_op jit(solution)/shard_map/ppermute | solution.py:353
  18.9 4.7 %shard_map.75 = (f32[8,128,128]{2,1,0:T(8,128)S(1)}, f32[2,2,64,128]{3,2,1,0:T(8,128)S(1)}, f32[2,10,144,128]{3,2,1,0:T(8,128)S(1)}, f32[2,5,144,128]{3,2,1,0:T(8,128)S(1)}) custom-call(f32[8,128,128]{2,1,0:T(8,128)S(1)} %get-tuple-element.22.conc, f32[8,128,128]{2,1,0:T(8,128)S(1)} %get-tuple-element.23.kappa, f32[8,128,128]{2,1,0:T(8,128)S(1)} %get-tuple-element.24.vel, ...), custom_call_target="tpu_custom_call" | custom-call | flops 2097152 | bytes 2097152 | tf_op jit(solution)/shard_map/pallas_call | solution.py:406
  23.6 0.0 collective-permute-done.2.raw_a
  23.6 0.0 collective-permute-done.3.raw_b
  23.6 0.0 collective-permute-done.4.got_a
  23.6 1.4 %collective-permute-done.5.got_b = f32[352,128]{1,0:T(8,128)S(1)} collective-permute-done((f32[352,128]{1,0:T(8,128)S(1)}, f32[352,128]{1,0:T(8,128)S(1)}, u32[]{:S(2)}, u32[]{:S(2)}) %collective-permute-start.5) | collective-permute-done | bytes 180256 | tf_op jit(solution)/shard_map/ppermute | solution.py:353
  25.0 2.4 %shard_map.76 = f32[2,8,64,128]{3,2,1,0:T(8,128)} custom-call(f32[2,10,144,128]{3,2,1,0:T(8,128)S(1)} %get-tuple-element.30.coef, f32[2,5,144,128]{3,2,1,0:T(8,128)S(1)} %get-tuple-element.31.av, f32[2,2,144,128]{3,2,1,0:T(8,128)S(1)} %get-tuple-element.32.edge_u, f32[11,144,128]{2,1,0:T(8,128)S(1)} %get-tuple-element.29.m_ref, ...), custom_call_target="tpu_custom_call" | custom-call | flops 2097152 | bytes 2097152 | tf_op jit(solution)/shard_map/pallas_call | solution.py:424
Async XLA Ops:
  2.1 11.0 %collective-permute-start = (f32[27,8,128]{2,1,0:T(8,128)S(1)}, f32[27,8,128]{2,1,0:T(8,128)S(1)}, u32[]{:S(2)}, u32[]{:S(2)}) collective-permute-start(f32[27,8,128]{2,1,0:T(8,128)S(1)} %get-tuple-element.27), channel_id=1, source_target_pairs={{0,8},{8,0},{16,24},{24,16},{32,40},{40,32},{48,56},{56,48},{64,72... | collective-permute-start | bytes 331784 | tf_op jit(solution)/shard_map/ppermute | solution.py:353
  2.8 10.3 %collective-permute-start.1 = (f32[27,8,128]{2,1,0:T(8,128)S(1)}, f32[27,8,128]{2,1,0:T(8,128)S(1)}, u32[]{:S(2)}, u32[]{:S(2)}) collective-permute-start(f32[27,8,128]{2,1,0:T(8,128)S(1)} %get-tuple-element.28), channel_id=1, source_target_pairs={{8,16},{16,8},{24,32},{32,24},{40,48},{48,40},{56,64},{64,56},{72,... | collective-permute-start | bytes 331784 | tf_op jit(solution)/shard_map/ppermute | solution.py:353
  7.7 15.9 %collective-permute-start.2 = (f32[4,128,128]{2,1,0:T(8,128)S(1)}, f32[4,128,128]{2,1,0:T(8,128)S(1)}, u32[]{:S(2)}, u32[]{:S(2)}) collective-permute-start(f32[4,128,128]{2,1,0:T(8,128)S(1)} %get-tuple-element.35), channel_id=1, source_target_pairs={{0,1},{1,0},{2,3},{3,2},{4,5},{5,4},{6,7},{7,6},{8,9},{9,8},{10,11... | collective-permute-start | bytes 786440 | tf_op jit(solution)/shard_map/ppermute | solution.py:353
  9.0 14.6 %collective-permute-start.3 = (f32[4,128,128]{2,1,0:T(8,128)S(1)}, f32[4,128,128]{2,1,0:T(8,128)S(1)}, u32[]{:S(2)}, u32[]{:S(2)}) collective-permute-start(f32[4,128,128]{2,1,0:T(8,128)S(1)} %get-tuple-element.36), channel_id=1, source_target_pairs={{1,2},{2,1},{3,4},{4,3},{5,6},{6,5},{9,10},{10,9},{11,12},{12,11},... | collective-permute-start | bytes 786440 | tf_op jit(solution)/shard_map/ppermute | solution.py:353
  14.0 9.6 %collective-permute-start.4 = (f32[352,128]{1,0:T(8,128)S(1)}, f32[352,128]{1,0:T(8,128)S(1)}, u32[]{:S(2)}, u32[]{:S(2)}) collective-permute-start(f32[352,128]{1,0:T(8,128)S(1)} %get-tuple-element.37), channel_id=1, source_target_pairs={{0,1},{1,0},{2,3},{3,2},{4,5},{5,4},{6,7},{7,6},{8,9},{9,8},{10,11... | collective-permute-start | bytes 540680 | tf_op jit(solution)/shard_map/ppermute | solution.py:353
  14.1 11.0 %collective-permute-start.5 = (f32[352,128]{1,0:T(8,128)S(1)}, f32[352,128]{1,0:T(8,128)S(1)}, u32[]{:S(2)}, u32[]{:S(2)}) collective-permute-start(f32[352,128]{1,0:T(8,128)S(1)} %get-tuple-element.38), channel_id=1, source_target_pairs={{1,2},{2,1},{3,4},{4,3},{5,6},{6,5},{9,10},{10,9},{11,12},{12,11},... | collective-permute-start | bytes 540680 | tf_op jit(solution)/shard_map/ppermute | solution.py:353

commit v5 on v4

v5 whole, which is shorter than its diff:
```python
import functools

import jax
import jax.numpy as jnp
from jax import lax
from jax.experimental import pallas as pl
from jax.experimental.pallas import tpu as pltpu
from jax.sharding import PartitionSpec as P

RATES = (0.08, 0.12)
DEPTH, ROWS, COLS = 8, 64, 128
LANES = 2 * ROWS
EDGE = 8
TALL = COLS + 2 * EDGE
G_CONC, G_KAPPA, G_VT, G_FACE, GROUPS = 0, 8, 16, 24, 27
RAW = 4
LATE = 2 * COLS + (RAW + 2) * EDGE


def first_half(shape):
    return lax.broadcasted_iota(jnp.int32, shape, 1) < ROWS


def halves(x, y):
    return jnp.where(first_half(x.shape), x, y)


def doubled(x):
    other = pltpu.roll(x, ROWS, 1)
    return halves(x, other), halves(other, x)


def shift_cols(x, by):
    return pltpu.roll(x, (-by) % x.shape[0], 0)


def shift_rows(x, by):
    return pltpu.roll(x, (-by) % LANES, 1)


def in_plane(c, kx, ky, v):
    s = kx * (shift_cols(c, 1) - c) - v * c
    f = ky * (shift_rows(c, 1) - c)
    return (s - shift_cols(s, -1)) + (f - shift_rows(f, -1))


def face_x(k):
    return 0.5 * (k + shift_cols(k, 1))


def face_y(k):
    row = lax.rem(lax.broadcasted_iota(jnp.int32, k.shape, 1), ROWS)
    return jnp.where(row < ROWS - 1, 0.5 * (k + shift_rows(k, 1)), 0.0)


def couple(m_ref, kind, other):
    total = None
    for a in (-1, 0, 1):
        at_a = shift_rows(other, a) if a else other
        for b in (-1, 0, 1):
            term = m_ref[kind, 3 * (a + 1) + b + 1] * (shift_cols(at_a, b) if b else at_a)
            total = term if total is None else total + term
    return total


def slab_flags():
    slab = lax.axis_index("slab")
    upper = (slab > 0).astype(jnp.float32)
    lower = (slab < lax.axis_size("slab") - 1).astype(jnp.float32)
    return slab % 2 == 0, upper, lower


def faces_down(parity):
    return lax.axis_index("slab") % 2 == parity


def layer(down, i):
    return jnp.where(down, DEPTH - 1 - i, i)


def stream_even():
    return lax.axis_index("stream") % 2 == 0


def turned(first, second):
    return jnp.concatenate([first, second], axis=0).T


def pack_kernel(
    conc_in, kappa_in, vel_in, kind_in, row_in, col_in, w_in,
    msg_a, msg_b, raw_a, raw_b, conc, kappa, vel, active, faces,
    conc_s, kappa_s, vel_s, kind_s, row_s, col_s, w_s, sems,
):
    moves = [(conc_in, conc_s), (kappa_in, kappa_s), (vel_in, vel_s), (kind_in, kind_s)]
    moves += [(row_in, row_s), (col_in, col_s), (w_in, w_s)]
    copies = [pltpu.make_async_copy(*move, sems.at[i]) for i, move in enumerate(moves)]
    for copy in copies:
        copy.start()
    even = stream_even()

    def put(group, plane):
        head, tail = plane[:EDGE], plane[COLS - EDGE :]
        msg_a[group] = jnp.where(even, tail, head)
        msg_b[group] = jnp.where(even, head, tail)

    copies[0].wait()
    for z in range(DEPTH):
        conc[z] = turned(conc_s[0, z], conc_s[1, z])
        put(G_CONC + z, conc[z])
    copies[1].wait()
    for z in range(DEPTH):
        kappa[z] = turned(kappa_s[0, z], kappa_s[1, z])
        put(G_KAPPA + z, kappa[z])
    for copy in copies[2:]:
        copy.wait()
    row = lax.broadcasted_iota(jnp.int32, (ROWS, COLS), 0)
    col = lax.broadcasted_iota(jnp.int32, (ROWS, COLS), 1) + lax.axis_index("stream") * COLS
    for k in range(2):
        offsets = (row_s[k] - row).astype(jnp.float32), (col_s[k] - col).astype(jnp.float32)
        for i, item in enumerate(offsets + (w_s[k],)):
            faces[2 * i + k] = turned(item, item)
    for z in range(DEPTH):
        on = kind_s[z].astype(jnp.float32)
        vel[z] = turned(vel_s[z], vel_s[z])
        active[z] = turned(on, on)
        put(G_VT + z, halves(vel[z], active[z]))
    for i in range(3):
        put(G_FACE + i, halves(faces[2 * i], faces[2 * i + 1]))
    for parity, raw in enumerate((raw_a, raw_b)):
        down = faces_down(parity)
        z0, z1 = layer(down, 0), layer(down, 1)
        raw[0], raw[1], raw[2] = conc[z0], kappa[z0], kappa[z1]
        raw[3] = halves(vel[z0], active[z0])


class Halo:
    def __init__(self, got_a, got_b):
        self.got = got_a, got_b
        self.even = stream_even()

    def sides(self, group):
        a, b = self.got[0][group], self.got[1][group]
        return jnp.where(self.even, b, a), jnp.where(self.even, a, b)

    def plane(self, ref, z, group):
        left, right = self.sides(group + z)
        return jnp.concatenate([left, ref[z], right], axis=0)

    def pair(self, refs, places, group):
        left, right = [doubled(x) for x in self.sides(group)]
        return [
            jnp.concatenate([left[i], refs[i][places[i]], right[i]], axis=0) for i in range(2)
        ]

    def motion(self, vel, active, z):
        return self.pair((vel, active), (z, z), G_VT + z)


def edge_kernel(parity, conc, kappa, vel, active, got_a, got_b, faces, msg, edge_u, *made):
    halo = Halo(got_a, got_b)
    if made:
        m_out, = made
        planes = [halo.pair((faces, faces), (2 * i, 2 * i + 1), G_FACE + i) for i in range(3)]
        rate = jnp.where(first_half((TALL, LANES)), RATES[0], RATES[1])
        weights = [rate * planes[2][k] for k in range(2)]
        landed = None
        for a in (-1, 0, 1):
            parts = [jnp.where(planes[0][k] == a, weights[k], 0.0) for k in range(2)]
            here = None
            for b in (-1, 0, 1):
                hits = [jnp.where(planes[1][k] == b, parts[k], 0.0) for k in range(2)]
                total = hits[0] + hits[1]
                m_out[3 * (a + 1) + b + 1] = total
                total = shift_cols(total, -b) if b else total
                here = total if here is None else here + total
            here = shift_rows(here, -a) if a else here
            landed = here if landed is None else landed + here
        m_out[9] = landed
        m_out[10] = weights[0] + weights[1]
    else:
        m_out = faces

    down = faces_down(parity)
    _, upper, lower = slab_flags()
    z0, z1, z2 = [layer(down, i) for i in range(3)]
    hold = m_out[jnp.where(down, 10, 9)] * jnp.where(down, lower, upper)
    (v0, a0), (v1, a1) = [halo.motion(vel, active, z) for z in (z0, z1)]
    k0, k1, k2 = [halo.plane(kappa, z, G_KAPPA) for z in (z0, z1, z2)]
    c0, c1, c2 = [halo.plane(conc, z, G_CONC) for z in (z0, z1, z2)]
    kx0, ky0 = face_x(k0), face_y(k0)
    k01, k12 = 0.5 * (k0 + k1), 0.5 * (k1 + k2)
    flow = k01 * (c1 - c0)
    u0 = c0 + a0 * (in_plane(c0, kx0, ky0, v0) + flow - hold * c0)
    u1 = c1 + a1 * (in_plane(c1, face_x(k1), face_y(k1), v1) + k12 * (c2 - c1) - flow)
    w0 = u0 + a0 * (in_plane(u0, kx0, ky0, v0) + k01 * (u1 - u0) - hold * u0)
    edge_u[0] = u0
    edge_u[1] = w0
    upper_half = lax.broadcasted_iota(jnp.int32, (EDGE, LANES), 0) < EDGE // 2
    for i, x in enumerate((u0, w0, c0, k0, k1, halves(v0, a0))):
        if i < 2:
            msg[pl.ds(i * COLS, COLS)] = x[EDGE : EDGE + COLS]
        msg[pl.ds(2 * COLS + i * EDGE, EDGE)] = jnp.where(upper_half, x[EDGE + COLS :], x[:EDGE])
    if msg.shape[0] > LATE:
        msg[pl.ds(LATE, EDGE)] = jnp.zeros((EDGE, LANES), jnp.float32)


def block_kernel(
    conc, kappa, vel, active, got_a, got_b, m_ref,
    u3, middle, coef, av, both_m,
    cells, kx, ky, kz, own, move, on,
):
    halo = Halo(got_a, got_b)
    _, upper, lower = slab_flags()
    for a in (-1, 0, 1):
        for b in (-1, 0, 1):
            i = 3 * (a + 1) + b + 1
            both_m[0, i] = m_ref[i]
            there = shift_cols(m_ref[8 - i], b) if b else m_ref[8 - i]
            both_m[1, i] = shift_rows(there, a) if a else there
    both_m[0, 9] = m_ref[10]
    both_m[1, 9] = m_ref[9]
    zeros = jnp.zeros((TALL, LANES), jnp.float32)
    own[0] = m_ref[9] * upper
    own[1] = m_ref[10] * lower
    above = None
    for z in range(DEPTH):
        k = halo.plane(kappa, z, G_KAPPA)
        kx[z] = face_x(k)
        ky[z] = face_y(k)
        if z:
            kz[z] = 0.5 * (above + k)
        above = k
        cells[0, z] = halo.plane(conc, z, G_CONC)
        move[z], on[z] = halo.motion(vel, active, z)

    for parity in range(2):
        down = faces_down(parity)
        z0, z1, z2 = [layer(down, i) for i in range(3)]
        f01, f12 = jnp.where(down, DEPTH - 1, 1), jnp.where(down, DEPTH - 2, 2)
        for i, z in enumerate((z0, z1, z2)):
            av[parity, i] = on[z]
        for i, z in enumerate((z0, z1)):
            av[parity, 3 + i] = move[z]
        c0 = cells[0, z0]
        k01 = kz[f01]
        items = [kx[z0], ky[z0], kx[z1], ky[z1], k01, kz[f12]]
        items.append(k01 + own[jnp.where(down, 1, 0)])
        items.append(couple(both_m, jnp.where(down, 1, 0), c0))
        items += [halo.plane(kappa, z0, G_KAPPA), c0]
        for i, item in enumerate(items):
            coef[parity, i] = item

    for step in range(3):
        now, later = step % 2, (step + 1) % 2
        for z in range(DEPTH):
            c = cells[now, z]
            r = in_plane(c, kx[z], ky[z], move[z])
            if z < DEPTH - 1:
                r += kz[z + 1] * (cells[now, z + 1] - c)
            else:
                r -= own[1] * c
            if z:
                r -= kz[z] * (c - cells[now, z - 1])
            else:
                r -= own[0] * c
            new = c + on[z] * r
            if step == 2:
                u3[z] = new[EDGE : EDGE + COLS]
            else:
                cells[later, z] = new
    for z in range(3, DEPTH - 3):
        back = u3[z].T
        middle[0, z - 3] = back[:ROWS]
        middle[1, z - 3] = back[ROWS:]


def join_kernel(
    parity, coef, av, edge_u, m_ref, u3, middle, raw, late, *rest
):
    if parity == 0:
        raw_b, out, moved, result, sems = rest
        moved[0], moved[1] = doubled(raw_b[3])
        motion = doubled(raw[3])
    else:
        moved, _, out, result, sems = rest
        motion = moved[0], moved[1]
    down = faces_down(parity)
    start = jnp.where(down, DEPTH - 3, 0)
    copies = []
    if parity == 0:
        copies.append(pltpu.make_async_copy(middle, out.at[:, pl.ds(3, DEPTH - 6)], sems.at[0]))
        copies[-1].start()

    def ghost(i, main):
        edges = late[pl.ds(2 * COLS + i * EDGE, EDGE)]
        return jnp.concatenate([edges, main, edges], axis=0)

    ghost_c = [ghost(2, raw[0]), ghost(0, late[pl.ds(0, COLS)]), ghost(1, late[pl.ds(COLS, COLS)])]
    kg, kgg = ghost(3, raw[1]), ghost(4, raw[2])
    pads = doubled(late[pl.ds(2 * COLS + 5 * EDGE, EDGE)])
    vg, ag = [jnp.concatenate([pad, x, pad], axis=0) for pad, x in zip(pads, motion)]
    a0, a1, a2, v0, v1 = [av[parity, i] for i in range(5)]
    kx0, ky0, kx1, ky1, k01, k12, hold, first_to_g, k0, first_c = [
        coef[parity, i] for i in range(10)
    ]
    k_face, kg2 = 0.5 * (kg + k0), 0.5 * (kg + kgg)
    own_c = [first_c, edge_u[0], edge_u[1]]
    to_own, to_ghost = jnp.where(down, 0, 1), jnp.where(down, 1, 0)

    g, e = ghost_c[0], own_c[0]
    flow = k_face * (g - e)
    e1 = a0 * (flow + couple(m_ref, to_own, g))
    d1 = ag * (first_to_g - flow)
    g, e = ghost_c[1] + d1, own_c[1] + e1
    flow = k_face * (g - e)
    d2 = d1 + ag * (
        in_plane(d1, face_x(kg), face_y(kg), vg)
        - (kg2 + m_ref[to_ghost, 9]) * d1
        + (couple(m_ref, to_ghost, e) - flow)
    )
    e2 = e1 + a0 * (in_plane(e1, kx0, ky0, v0) - hold * e1 + (flow + couple(m_ref, to_own, g)))
    n2 = a1 * (k01 * e1)
    g, e = ghost_c[2] + d2, own_c[2] + e2
    flow = k_face * (g - e)
    e3 = e2 + a0 * (
        in_plane(e2, kx0, ky0, v0) - hold * e2 + k01 * n2 + (flow + couple(m_ref, to_own, g))
    )
    n3 = n2 + a1 * (in_plane(n2, kx1, ky1, v1) - (k01 + k12) * n2 + k01 * e2)
    m3 = a2 * (k12 * n2)
    for i, x in enumerate((e3, n3, m3)):
        z = layer(down, i)
        back = (u3[z] + x[EDGE : EDGE + COLS]).T
        result[0, z - start] = back[:ROWS]
        result[1, z - start] = back[ROWS:]
    copies.append(pltpu.make_async_copy(result, out.at[:, pl.ds(start, 3)], sems.at[1]))
    copies[-1].start()
    for copy in copies:
        copy.wait()


def swap(value, axis, parity):
    count = lax.axis_size(axis)
    pairs = []
    for i in range(parity, count - 1, 2):
        pairs += [(i, i + 1), (i + 1, i)]
    return lax.ppermute(value, axis, pairs)


def shape(*dims):
    return jax.ShapeDtypeStruct(dims, jnp.float32)


def call(kernel, outs, scratch=(), **specs):
    return pl.pallas_call(
        kernel,
        out_shape=outs,
        scratch_shapes=list(scratch),
        cost_estimate=pl.CostEstimate(flops=1024, bytes_accessed=1024, transcendentals=0),
        compiler_params=pltpu.CompilerParams(vmem_limit_bytes=40 * 2**20),
        **specs,
    )


def per_device(conc, kappa, velocity, cell_type, target_row, target_col, mortar_weight):
    tile = (ROWS, COLS)
    plane = (COLS, LANES)
    tall = (TALL, LANES)
    given = (conc, kappa, velocity, cell_type, target_row, target_col, mortar_weight)
    anywhere = pl.BlockSpec(memory_space=pl.ANY)
    whole = pl.BlockSpec(memory_space=pltpu.VMEM)

    msg_a, msg_b, raw_a, raw_b, *fields, faces = call(
        pack_kernel,
        [shape(GROUPS, EDGE, LANES)] * 2
        + [shape(RAW, *plane)] * 2
        + [shape(DEPTH, *plane)] * 4
        + [shape(6, *plane)],
        [pltpu.VMEM(x.shape, x.dtype) for x in given] + [pltpu.SemaphoreType.DMA((7,))],
        in_specs=[anywhere] * 7,
    )(*[pltpu.with_memory_space_constraint(x, pltpu.HBM) for x in given])
    got_b = swap(msg_b, "stream", 1)
    got_a = swap(msg_a, "stream", 0)
    raw_b = swap(raw_b, "slab", 1)
    raw_a = swap(raw_a, "slab", 0)
    fields += [got_a, got_b]
    late_b, edge_b, m = call(
        functools.partial(edge_kernel, 1),
        (shape(LATE + EDGE, LANES), shape(2, *tall), shape(11, *tall)),
    )(*fields, faces)
    late_b = swap(late_b, "slab", 1)
    late_a, edge_a = call(
        functools.partial(edge_kernel, 0), (shape(LATE, LANES), shape(2, *tall))
    )(*fields, m)
    late_a = swap(late_a, "slab", 0)
    u3, middle, coef, av, both_m = call(
        block_kernel,
        (
            shape(DEPTH, *plane),
            shape(2, DEPTH - 6, *tile),
            shape(2, 10, *tall),
            shape(2, 5, *tall),
            shape(2, 10, *tall),
        ),
        (
            pltpu.VMEM((2, DEPTH) + tall, jnp.float32),
            pltpu.VMEM((DEPTH,) + tall, jnp.float32),
            pltpu.VMEM((DEPTH,) + tall, jnp.float32),
            pltpu.VMEM((DEPTH,) + tall, jnp.float32),
            pltpu.VMEM((2,) + tall, jnp.float32),
            pltpu.VMEM((DEPTH,) + tall, jnp.float32),
            pltpu.VMEM((DEPTH,) + tall, jnp.float32),
        ),
    )(*fields, m)

    def join(parity, outs, out_specs, edge_u, raw, late, *more, aliases={}):
        return call(
            functools.partial(join_kernel, parity),
            outs,
            (pltpu.VMEM((2, 3) + tile, jnp.float32), pltpu.SemaphoreType.DMA((2,))),
            in_specs=[whole] * 9 + [anywhere] * (len(more) - 1),
            out_specs=out_specs,
            input_output_aliases=aliases,
        )(coef, av, edge_u, both_m, u3, middle, raw, late, *more)

    final = shape(2, DEPTH, *tile)
    out, moved = join(
        0, (final, shape(2, *plane)), (anywhere, whole), edge_a, raw_a, late_a, raw_b
    )
    return join(1, final, anywhere, edge_b, raw_b, late_b, moved, out, aliases={9: 0})


def solution(mesh):
    return jax.shard_map(
        per_device,
        mesh=mesh,
        in_specs=(
            P(None, "slab", None, "stream"),
            P(None, "slab", None, "stream"),
            P("slab", None, "stream"),
            P("slab", None, "stream"),
            P(None, None, "stream"),
            P(None, None, "stream"),
            P(None, None, "stream"),
        ),
        out_specs=P(None, "slab", None, "stream"),
        check_vma=False,
    )
```

time: 27.9 us -> 26 us (0.932)
  starting transfers between devices: 15.9 us -> 14.7 us
  Pallas kernels: 9.99 us -> 8.84 us
  waiting for transfers between devices: 1.46 us -> 1.92 us
    pallas_call x1, Pallas kernels: 4.68 us -> 2.93 us  [per_device(): call(block_kernel, (shape(DEPTH, *plane), shape(2, DEPTH - 6, *tile), sha...]
    ppermute x6, starting transfers between devices: 15.9 us -> 14.7 us  [swap(): return lax.ppermute(value, axis, pairs)]
    pallas_call x3 -> x5, Pallas kernels: 5.3 us -> 5.91 us  [the longest x2 3.05 us: join(): call(functools.partial(join_kernel, parity), outs, (pltpu.VMEM((2, 3) + t...]
    ppermute x6, waiting for transfers between devices: 1.46 us -> 1.92 us  [swap(): return lax.ppermute(value, axis, pairs)]
  transfers between devices with their start and end apart: 6 -> 6, of which waited for: 1 -> 1; matrix products, arithmetic and copies ran while one was open for 0% -> 0% of each run, Pallas kernels for 20% -> 21%
where the time goes in v5:
time: 26 us; the launch traced here: 25.6 us
  starting transfers between devices  14.7 us (57%)
  Pallas kernels  8.84 us (34%)
  waiting for transfers between devices  1.92 us (7%)
    ppermute x6, starting transfers between devices, swap(): return lax.ppermute(value, axis, pairs)  14.7 us
    pallas_call x2, Pallas kernels, join(): call(functools.partial(join_kernel, parity), outs, (pltpu.VMEM((2, 3) + t...  3.05 us
    pallas_call x1, Pallas kernels, per_device(): call(block_kernel, (shape(DEPTH, *plane), shape(2, DEPTH - 6, *tile), sha...  2.93 us
    pallas_call x1, Pallas kernels, per_device(): call(pack_kernel, [shape(GROUPS, EDGE, LANES)] * 2 + [shape(RAW, *plane)]...  1.99 us
    ppermute x6, waiting for transfers between devices, swap(): return lax.ppermute(value, axis, pairs)  1.92 us
  transfers between devices with their start and end apart: 6, of which 1 were waited for; matrix products, arithmetic and copies ran while one was open for 0% of the time, Pallas kernels for 21%

profile of v5, /device:TPU:121, one launch (start us, length us, event | category | flops | bytes accessed | tf_op | source)
XLA Modules:
  0.0 25.6 jit_solution(14586748141579957514)
XLA Ops:
  0.0 2.0 %shard_map.73 = (f32[27,8,128]{2,1,0:T(8,128)S(1)}, f32[27,8,128]{2,1,0:T(8,128)S(1)}, f32[4,128,128]{2,1,0:T(8,128)S(1)}, f32[4,128,128]{2,1,0:T(8,128)S(1)}, f...) custom-call(f32[2,8,64,128]{3,2,1,0:T(8,128)} %conc_in.1, ...), custom_call_target="tpu_custom_call" | custom-call | flops 1024 | bytes 1024 | tf_op jit(solution)/shard_map/pallas_call | solution.py:372
  2.0 0.8 %collective-permute-start = (f32[27,8,128]{2,1,0:T(8,128)S(1)}, f32[27,8,128]{2,1,0:T(8,128)S(1)}, u32[]{:S(2)}, u32[]{:S(2)}) collective-permute-start(f32[27,8,128]{2,1,0:T(8,128)S(1)} %get-tuple-element.30), channel_id=1, source_target_pairs={{0,8},{8,0},{16,24},{24,16},{32,40},{40,32},{48,56},{56,48},{64,72... | collective-permute-start | bytes 331784 | tf_op jit(solution)/shard_map/ppermute | solution.py:346
  2.8 4.8 %collective-permute-start.1 = (f32[27,8,128]{2,1,0:T(8,128)S(1)}, f32[27,8,128]{2,1,0:T(8,128)S(1)}, u32[]{:S(2)}, u32[]{:S(2)}) collective-permute-start(f32[27,8,128]{2,1,0:T(8,128)S(1)} %get-tuple-element.31), channel_id=1, source_target_pairs={{8,16},{16,8},{24,32},{32,24},{40,48},{48,40},{56,64},{64,56},{72,... | collective-permute-start | bytes 331784 | tf_op jit(solution)/shard_map/ppermute | solution.py:346
  7.6 4.8 %collective-permute-start.2 = (f32[4,128,128]{2,1,0:T(8,128)S(1)}, f32[4,128,128]{2,1,0:T(8,128)S(1)}, u32[]{:S(2)}, u32[]{:S(2)}) collective-permute-start(f32[4,128,128]{2,1,0:T(8,128)S(1)} %get-tuple-element.40), channel_id=1, source_target_pairs={{1,2},{2,1},{3,4},{4,3},{5,6},{6,5},{9,10},{10,9},{11,12},{12,11},... | collective-permute-start | bytes 786440 | tf_op jit(solution)/shard_map/ppermute | solution.py:346
  12.4 0.1 collective-permute-start.4
  12.5 0.0 collective-permute-done.got_a
  12.5 0.0 collective-permute-done.1.got_b
  12.5 0.5 %shard_map.74 = (f32[312,128]{1,0:T(8,128)S(1)}, f32[2,144,128]{2,1,0:T(8,128)S(1)}, f32[11,144,128]{2,1,0:T(8,128)S(1)}) custom-call(f32[8,128,128]{2,1,0:T(8,128)S(1)} %get-tuple-element.26.conc, f32[8,128,128]{2,1,0:T(8,128)S(1)} %get-tuple-element.27.kappa, f32[8,128,128]{2,1,0:T(8,128)S(1)} %get-tuple-element.28.vel, ...), custom_call_target="tpu_custom_call" | custom-call | flops 1024 | bytes 1024 | tf_op jit(solution)/shard_map/pallas_call | solution.py:386
  13.0 4.1 %collective-permute-start.3 = (f32[312,128]{1,0:T(8,128)S(1)}, f32[312,128]{1,0:T(8,128)S(1)}, u32[]{:S(2)}, u32[]{:S(2)}) collective-permute-start(f32[312,128]{1,0:T(8,128)S(1)} %get-tuple-element.41), channel_id=1, source_target_pairs={{1,2},{2,1},{3,4},{4,3},{5,6},{6,5},{9,10},{10,9},{11,12},{12,11},... | collective-permute-start | bytes 479240 | tf_op jit(solution)/shard_map/ppermute | solution.py:346
  17.1 0.4 %shard_map.76 = (f32[304,128]{1,0:T(8,128)S(1)}, f32[2,144,128]{2,1,0:T(8,128)S(1)}) custom-call(f32[8,128,128]{2,1,0:T(8,128)S(1)} %get-tuple-element.26.conc, f32[8,128,128]{2,1,0:T(8,128)S(1)} %get-tuple-element.27.kappa, f32[8,128,128]{2,1,0:T(8,128)S(1)} %get-tuple-element.28.vel, f32[8,128,128]{2,1,0:T(8,128)S(1)} %get-tuple-element.29.active, ...), custom_call_target="tpu_custom_call" | custom-call | flops 1024 | bytes 1024 | tf_op jit(solution)/shard_map/pallas_call | solution.py:391
  17.5 0.1 collective-permute-start.5
  17.6 2.9 %shard_map.75 = (f32[8,128,128]{2,1,0:T(8,128)S(1)}, f32[2,2,64,128]{3,2,1,0:T(8,128)S(1)}, f32[2,10,144,128]{3,2,1,0:T(8,128)S(1)}, f32[2,5,144,128]{3,2,1,0:T(8,128)S(1)}, f32[2,10,144,128]{3,2,1,0:T(8,128)S(1)}) custom-call(f32[8,128,128]{2,1,0:T(8,128)S(1)} %get-tuple-element.26.conc, f32[8,128,128]{2,1,0:T(8,128)S(1)} %get-tuple-element.27.kappa, ...), custom_call_target="tpu_custom_call" | custom-call | flops 1024 | bytes 1024 | tf_op jit(solution)/shard_map/pallas_call | solution.py:395
  20.6 0.0 collective-permute-done.2.rest_0_.raw
  20.6 0.0 collective-permute-done.4.raw
  20.6 1.9 %collective-permute-done.5.late = f32[304,128]{1,0:T(8,128)S(1)} collective-permute-done((f32[304,128]{1,0:T(8,128)S(1)}, f32[304,128]{1,0:T(8,128)S(1)}, u32[]{:S(2)}, u32[]{:S(2)}) %collective-permute-start.5) | collective-permute-done | bytes 155680 | tf_op jit(solution)/shard_map/ppermute | solution.py:346
  22.5 1.6 %shard_map.77 = (f32[2,8,64,128]{3,2,1,0:T(8,128)}, f32[2,128,128]{2,1,0:T(8,128)S(1)}) custom-call(f32[2,10,144,128]{3,2,1,0:T(8,128)S(1)} %get-tuple-element.34.coef, f32[2,5,144,128]{3,2,1,0:T(8,128)S(1)} %get-tuple-element.35.av, f32[2,144,128]{2,1,0:T(8,128)S(1)} %get-tuple-element.42.edge_u, f32[2,10,144,128]{3,2,1,0:T(8,128)S(1)} %get-tuple-element.37.m_ref, ...), custom_call_target="tpu_custom_call" | custom-call | flops 1024 | bytes 1024 | tf_op jit(solution)/shard_map/pallas_call | solution.py:416
  24.0 0.0 collective-permute-done.3.late
  24.1 1.5 %shard_map.78 = f32[2,8,64,128]{3,2,1,0:T(8,128)} custom-call(f32[2,10,144,128]{3,2,1,0:T(8,128)S(1)} %get-tuple-element.34.coef, f32[2,5,144,128]{3,2,1,0:T(8,128)S(1)} %get-tuple-element.35.av, f32[2,144,128]{2,1,0:T(8,128)S(1)} %get-tuple-element.36.edge_u, f32[2,10,144,128]{3,2,1,0:T(8,128)S(1)} %get-tuple-element.37.m_ref, ...), custom_call_target="tpu_custom_call", output_to_operand_aliasing={{}: (9, {})} | custom-call | flops 1024 | bytes 1024 | tf_op jit(solution)/shard_map/pallas_call | solution.py:416
Async XLA Ops:
  2.0 10.5 %collective-permute-start = (f32[27,8,128]{2,1,0:T(8,128)S(1)}, f32[27,8,128]{2,1,0:T(8,128)S(1)}, u32[]{:S(2)}, u32[]{:S(2)}) collective-permute-start(f32[27,8,128]{2,1,0:T(8,128)S(1)} %get-tuple-element.30), channel_id=1, source_target_pairs={{0,8},{8,0},{16,24},{24,16},{32,40},{40,32},{48,56},{56,48},{64,72... | collective-permute-start | bytes 331784 | tf_op jit(solution)/shard_map/ppermute | solution.py:346
  2.8 9.7 %collective-permute-start.1 = (f32[27,8,128]{2,1,0:T(8,128)S(1)}, f32[27,8,128]{2,1,0:T(8,128)S(1)}, u32[]{:S(2)}, u32[]{:S(2)}) collective-permute-start(f32[27,8,128]{2,1,0:T(8,128)S(1)} %get-tuple-element.31), channel_id=1, source_target_pairs={{8,16},{16,8},{24,32},{32,24},{40,48},{48,40},{56,64},{64,56},{72,... | collective-permute-start | bytes 331784 | tf_op jit(solution)/shard_map/ppermute | solution.py:346
  7.6 13.0 %collective-permute-start.2 = (f32[4,128,128]{2,1,0:T(8,128)S(1)}, f32[4,128,128]{2,1,0:T(8,128)S(1)}, u32[]{:S(2)}, u32[]{:S(2)}) collective-permute-start(f32[4,128,128]{2,1,0:T(8,128)S(1)} %get-tuple-element.40), channel_id=1, source_target_pairs={{1,2},{2,1},{3,4},{4,3},{5,6},{6,5},{9,10},{10,9},{11,12},{12,11},... | collective-permute-start | bytes 786440 | tf_op jit(solution)/shard_map/ppermute | solution.py:346
  12.4 8.2 %collective-permute-start.4 = (f32[4,128,128]{2,1,0:T(8,128)S(1)}, f32[4,128,128]{2,1,0:T(8,128)S(1)}, u32[]{:S(2)}, u32[]{:S(2)}) collective-permute-start(f32[4,128,128]{2,1,0:T(8,128)S(1)} %get-tuple-element.43), channel_id=1, source_target_pairs={{0,1},{1,0},{2,3},{3,2},{4,5},{5,4},{6,7},{7,6},{8,9},{9,8},{10,11... | collective-permute-start | bytes 786440 | tf_op jit(solution)/shard_map/ppermute | solution.py:346
  13.0 11.0 %collective-permute-start.3 = (f32[312,128]{1,0:T(8,128)S(1)}, f32[312,128]{1,0:T(8,128)S(1)}, u32[]{:S(2)}, u32[]{:S(2)}) collective-permute-start(f32[312,128]{1,0:T(8,128)S(1)} %get-tuple-element.41), channel_id=1, source_target_pairs={{1,2},{2,1},{3,4},{4,3},{5,6},{6,5},{9,10},{10,9},{11,12},{12,11},... | collective-permute-start | bytes 479240 | tf_op jit(solution)/shard_map/ppermute | solution.py:346
  17.5 5.0 %collective-permute-start.5 = (f32[304,128]{1,0:T(8,128)S(1)}, f32[304,128]{1,0:T(8,128)S(1)}, u32[]{:S(2)}, u32[]{:S(2)}) collective-permute-start(f32[304,128]{1,0:T(8,128)S(1)} %get-tuple-element.44), channel_id=1, source_target_pairs={{0,1},{1,0},{2,3},{3,2},{4,5},{5,4},{6,7},{7,6},{8,9},{9,8},{10,11... | collective-permute-start | bytes 466952 | tf_op jit(solution)/shard_map/ppermute | solution.py:346

commit v6 on v5

--- a/solution.py
+++ b/solution.py
@@ -54,12 +54,15 @@
 
 
 def couple(m_ref, kind, other):
+    rows = [shift_rows(other, -1), other, shift_rows(other, 1)]
     total = None
-    for a in (-1, 0, 1):
-        at_a = shift_rows(other, a) if a else other
-        for b in (-1, 0, 1):
-            term = m_ref[kind, 3 * (a + 1) + b + 1] * (shift_cols(at_a, b) if b else at_a)
-            total = term if total is None else total + term
+    for b in (-1, 0, 1):
+        part = None
+        for a in (-1, 0, 1):
+            term = m_ref[kind, 3 * (a + 1) + b + 1] * rows[a + 1]
+            part = term if part is None else part + term
+        part = shift_cols(part, b) if b else part
+        total = part if total is None else total + part
     return total
 
 
@@ -88,7 +91,7 @@
 
 def pack_kernel(
     conc_in, kappa_in, vel_in, kind_in, row_in, col_in, w_in,
-    msg_a, msg_b, raw_a, raw_b, conc, kappa, vel, active, faces,
+    msg_a, msg_b, raw_a, raw_b, conc, kappa, mixed, faces,
     conc_s, kappa_s, vel_s, kind_s, row_s, col_s, w_s, sems,
 ):
     moves = [(conc_in, conc_s), (kappa_in, kappa_s), (vel_in, vel_s), (kind_in, kind_s)]
@@ -120,17 +123,14 @@
         for i, item in enumerate(offsets + (w_s[k],)):
             faces[2 * i + k] = turned(item, item)
     for z in range(DEPTH):
-        on = kind_s[z].astype(jnp.float32)
-        vel[z] = turned(vel_s[z], vel_s[z])
-        active[z] = turned(on, on)
-        put(G_VT + z, halves(vel[z], active[z]))
+        mixed[z] = turned(vel_s[z], kind_s[z].astype(jnp.float32))
+        put(G_VT + z, mixed[z])
     for i in range(3):
         put(G_FACE + i, halves(faces[2 * i], faces[2 * i + 1]))
     for parity, raw in enumerate((raw_a, raw_b)):
         down = faces_down(parity)
         z0, z1 = layer(down, 0), layer(down, 1)
-        raw[0], raw[1], raw[2] = conc[z0], kappa[z0], kappa[z1]
-        raw[3] = halves(vel[z0], active[z0])
+        raw[0], raw[1], raw[2], raw[3] = conc[z0], kappa[z0], kappa[z1], mixed[z0]
 
 
 class Halo:
@@ -152,11 +152,11 @@
             jnp.concatenate([left[i], refs[i][places[i]], right[i]], axis=0) for i in range(2)
         ]
 
-    def motion(self, vel, active, z):
-        return self.pair((vel, active), (z, z), G_VT + z)
-
-
-def edge_kernel(parity, conc, kappa, vel, active, got_a, got_b, faces, msg, edge_u, *made):
+    def motion(self, mixed, z):
+        return doubled(self.plane(mixed, z, G_VT))
+
+
+def edge_kernel(parity, conc, kappa, mixed, got_a, got_b, faces, msg, edge_u, *made):
     halo = Halo(got_a, got_b)
     if made:
         m_out, = made
@@ -184,7 +184,7 @@
     _, upper, lower = slab_flags()
     z0, z1, z2 = [layer(down, i) for i in range(3)]
     hold = m_out[jnp.where(down, 10, 9)] * jnp.where(down, lower, upper)
-    (v0, a0), (v1, a1) = [halo.motion(vel, active, z) for z in (z0, z1)]
+    (v0, a0), (v1, a1) = [halo.motion(mixed, z) for z in (z0, z1)]
     k0, k1, k2 = [halo.plane(kappa, z, G_KAPPA) for z in (z0, z1, z2)]
     c0, c1, c2 = [halo.plane(conc, z, G_CONC) for z in (z0, z1, z2)]
     kx0, ky0 = face_x(k0), face_y(k0)
@@ -205,7 +205,7 @@
 
 
 def block_kernel(
-    conc, kappa, vel, active, got_a, got_b, m_ref,
+    conc, kappa, mixed, got_a, got_b, m_ref,
     u3, middle, coef, av, both_m,
     cells, kx, ky, kz, own, move, on,
 ):
@@ -214,9 +214,8 @@
     for a in (-1, 0, 1):
         for b in (-1, 0, 1):
             i = 3 * (a + 1) + b + 1
-            both_m[0, i] = m_ref[i]
-            there = shift_cols(m_ref[8 - i], b) if b else m_ref[8 - i]
-            both_m[1, i] = shift_rows(there, a) if a else there
+            both_m[0, i] = shift_cols(m_ref[i], -b) if b else m_ref[i]
+            both_m[1, i] = shift_rows(m_ref[8 - i], a) if a else m_ref[8 - i]
     both_m[0, 9] = m_ref[10]
     both_m[1, 9] = m_ref[9]
     zeros = jnp.zeros((TALL, LANES), jnp.float32)
@@ -231,7 +230,7 @@
             kz[z] = 0.5 * (above + k)
         above = k
         cells[0, z] = halo.plane(conc, z, G_CONC)
-        move[z], on[z] = halo.motion(vel, active, z)
+        move[z], on[z] = halo.motion(mixed, z)
 
     for parity in range(2):
         down = faces_down(parity)
@@ -275,21 +274,22 @@
 
 
 def join_kernel(
-    parity, coef, av, edge_u, m_ref, u3, middle, raw, late, *rest
+    parity, coef, av, edge_u, m_ref, u3, raw, late, *rest
 ):
+    down = faces_down(parity)
+    copies = []
+
+    def send(source, target):
+        copies.append(pltpu.make_async_copy(source, target, sems.at[len(copies)]))
+        copies[-1].start()
+
     if parity == 0:
-        raw_b, out, moved, result, sems = rest
-        moved[0], moved[1] = doubled(raw_b[3])
-        motion = doubled(raw[3])
+        _, result = rest
     else:
-        moved, _, out, result, sems = rest
-        motion = moved[0], moved[1]
-    down = faces_down(parity)
-    start = jnp.where(down, DEPTH - 3, 0)
-    copies = []
-    if parity == 0:
-        copies.append(pltpu.make_async_copy(middle, out.at[:, pl.ds(3, DEPTH - 6)], sems.at[0]))
-        copies[-1].start()
+        joined, middle, out, result, sems = rest
+        send(middle, out.at[:, pl.ds(3, DEPTH - 6)])
+        for i in range(3):
+            send(joined.at[:, i], out.at[:, layer(faces_down(0), i)])
 
     def ghost(i, main):
         edges = late[pl.ds(2 * COLS + i * EDGE, EDGE)]
@@ -297,8 +297,7 @@
 
     ghost_c = [ghost(2, raw[0]), ghost(0, late[pl.ds(0, COLS)]), ghost(1, late[pl.ds(COLS, COLS)])]
     kg, kgg = ghost(3, raw[1]), ghost(4, raw[2])
-    pads = doubled(late[pl.ds(2 * COLS + 5 * EDGE, EDGE)])
-    vg, ag = [jnp.concatenate([pad, x, pad], axis=0) for pad, x in zip(pads, motion)]
+    vg, ag = doubled(ghost(5, raw[3]))
     a0, a1, a2, v0, v1 = [av[parity, i] for i in range(5)]
     kx0, ky0, kx1, ky1, k01, k12, hold, first_to_g, k0, first_c = [
         coef[parity, i] for i in range(10)
@@ -320,20 +319,28 @@
     )
     e2 = e1 + a0 * (in_plane(e1, kx0, ky0, v0) - hold * e1 + (flow + couple(m_ref, to_own, g)))
     n2 = a1 * (k01 * e1)
+
+    def finish(i, x):
+        z = layer(down, i)
+        back = (u3[z] + x[EDGE : EDGE + COLS]).T
+        result[0, i] = back[:ROWS]
+        result[1, i] = back[ROWS:]
+        if parity:
+            send(result.at[:, i], out.at[:, z])
+
+    finish(2, a2 * (k12 * n2))
+    finish(1, n2 + a1 * (in_plane(n2, kx1, ky1, v1) - (k01 + k12) * n2 + k01 * e2))
     g, e = ghost_c[2] + d2, own_c[2] + e2
     flow = k_face * (g - e)
-    e3 = e2 + a0 * (
-        in_plane(e2, kx0, ky0, v0) - hold * e2 + k01 * n2 + (flow + couple(m_ref, to_own, g))
+    finish(
+        0,
+        e2
+        + a0
+        * (
+            in_plane(e2, kx0, ky0, v0) - hold * e2 + k01 * n2
+            + (flow + couple(m_ref, to_own, g))
+        ),
     )
-    n3 = n2 + a1 * (in_plane(n2, kx1, ky1, v1) - (k01 + k12) * n2 + k01 * e2)
-    m3 = a2 * (k12 * n2)
-    for i, x in enumerate((e3, n3, m3)):
-        z = layer(down, i)
-        back = (u3[z] + x[EDGE : EDGE + COLS]).T
-        result[0, z - start] = back[:ROWS]
-        result[1, z - start] = back[ROWS:]
-    copies.append(pltpu.make_async_copy(result, out.at[:, pl.ds(start, 3)], sems.at[1]))
-    copies[-1].start()
     for copy in copies:
         copy.wait()
 
@@ -373,7 +380,7 @@
         pack_kernel,
         [shape(GROUPS, EDGE, LANES)] * 2
         + [shape(RAW, *plane)] * 2
-        + [shape(DEPTH, *plane)] * 4
+        + [shape(DEPTH, *plane)] * 3
         + [shape(6, *plane)],
         [pltpu.VMEM(x.shape, x.dtype) for x in given] + [pltpu.SemaphoreType.DMA((7,))],
         in_specs=[anywhere] * 7,
@@ -412,21 +419,23 @@
         ),
     )(*fields, m)
 
-    def join(parity, outs, out_specs, edge_u, raw, late, *more, aliases={}):
+    def join(parity, operands, extra, outs, **specs):
         return call(
             functools.partial(join_kernel, parity),
             outs,
-            (pltpu.VMEM((2, 3) + tile, jnp.float32), pltpu.SemaphoreType.DMA((2,))),
-            in_specs=[whole] * 9 + [anywhere] * (len(more) - 1),
-            out_specs=out_specs,
-            input_output_aliases=aliases,
-        )(coef, av, edge_u, both_m, u3, middle, raw, late, *more)
-
-    final = shape(2, DEPTH, *tile)
-    out, moved = join(
-        0, (final, shape(2, *plane)), (anywhere, whole), edge_a, raw_a, late_a, raw_b
+            in_specs=[whole] * (4 + len(operands)) + [anywhere] * len(extra),
+            **specs,
+        )(coef, av, operands[0], both_m, u3, *operands[1:], *extra)
+
+    joined = join(0, (edge_a, raw_a, late_a), (raw_b,), shape(2, 3, *tile))
+    return join(
+        1,
+        (edge_b, raw_b, late_b, joined, middle),
+        (),
+        shape(2, DEPTH, *tile),
+        scratch=(pltpu.VMEM((2, 3) + tile, jnp.float32), pltpu.SemaphoreType.DMA((7,))),
+        out_specs=anywhere,
     )
-    return join(1, final, anywhere, edge_b, raw_b, late_b, moved, out, aliases={9: 0})
 
 
 def solution(mesh):

time: 26 us -> 25.2 us (0.969)
  Pallas kernels: 8.84 us -> 8.22 us
    pallas_call x2, Pallas kernels: 3.05 us -> 2.33 us  [join(): call(functools.partial(join_kernel, parity), outs, in_specs=[whole] * (4...]
  transfers between devices with their start and end apart: 6 -> 6, of which waited for: 1 -> 1; matrix products, arithmetic and copies ran while one was open for 0% -> 0% of each run, Pallas kernels for 21% -> 20%
where the time goes in v6:
time: 25.2 us; the launch traced here: 24.7 us
  starting transfers between devices  14.7 us (58%)
  Pallas kernels  8.22 us (33%)
  waiting for transfers between devices  1.7 us (7%)
    ppermute x6, starting transfers between devices, swap(): return lax.ppermute(value, axis, pairs)  14.7 us
    pallas_call x1, Pallas kernels, per_device(): call(block_kernel, (shape(DEPTH, *plane), shape(2, DEPTH - 6, *tile), sha...  3.06 us
    pallas_call x2, Pallas kernels, join(): call(functools.partial(join_kernel, parity), outs, in_specs=[whole] * (4...  2.33 us
    pallas_call x1, Pallas kernels, per_device(): call(pack_kernel, [shape(GROUPS, EDGE, LANES)] * 2 + [shape(RAW, *plane)]...  1.86 us
    ppermute x6, waiting for transfers between devices, swap(): return lax.ppermute(value, axis, pairs)  1.7 us
    pallas_call x1, Pallas kernels, per_device(): call(functools.partial(edge_kernel, 1), (shape(LATE + EDGE, LANES), shape...  0.55 us
  transfers between devices with their start and end apart: 6, of which 1 were waited for; matrix products, arithmetic and copies ran while one was open for 0% of the time, Pallas kernels for 20%

profile of v6, /device:TPU:121, one launch (start us, length us, event | category | flops | bytes accessed | tf_op | source)
XLA Modules:
  0.0 24.7 jit_solution(13036646604241299178)
XLA Ops:
  0.0 1.9 %shard_map.73 = (f32[27,8,128]{2,1,0:T(8,128)S(1)}, f32[27,8,128]{2,1,0:T(8,128)S(1)}, f32[4,128,128]{2,1,0:T(8,128)S(1)}, f32[4,128,128]{2,1,0:T(8,128)S(1)}, f...) custom-call(f32[2,8,64,128]{3,2,1,0:T(8,128)} %conc_in.1, ...), custom_call_target="tpu_custom_call" | custom-call | flops 1024 | bytes 1024 | tf_op jit(solution)/shard_map/pallas_call | solution.py:379
  1.9 0.8 %collective-permute-start = (f32[27,8,128]{2,1,0:T(8,128)S(1)}, f32[27,8,128]{2,1,0:T(8,128)S(1)}, u32[]{:S(2)}, u32[]{:S(2)}) collective-permute-start(f32[27,8,128]{2,1,0:T(8,128)S(1)} %get-tuple-element.26), channel_id=1, source_target_pairs={{0,8},{8,0},{16,24},{24,16},{32,40},{40,32},{48,56},{56,48},{64,72... | collective-permute-start | bytes 331784 | tf_op jit(solution)/shard_map/ppermute | solution.py:353
  2.6 4.8 %collective-permute-start.1 = (f32[27,8,128]{2,1,0:T(8,128)S(1)}, f32[27,8,128]{2,1,0:T(8,128)S(1)}, u32[]{:S(2)}, u32[]{:S(2)}) collective-permute-start(f32[27,8,128]{2,1,0:T(8,128)S(1)} %get-tuple-element.27), channel_id=1, source_target_pairs={{8,16},{16,8},{24,32},{32,24},{40,48},{48,40},{56,64},{64,56},{72,... | collective-permute-start | bytes 331784 | tf_op jit(solution)/shard_map/ppermute | solution.py:353
  7.5 4.8 %collective-permute-start.2 = (f32[4,128,128]{2,1,0:T(8,128)S(1)}, f32[4,128,128]{2,1,0:T(8,128)S(1)}, u32[]{:S(2)}, u32[]{:S(2)}) collective-permute-start(f32[4,128,128]{2,1,0:T(8,128)S(1)} %get-tuple-element.35), channel_id=1, source_target_pairs={{1,2},{2,1},{3,4},{4,3},{5,6},{6,5},{9,10},{10,9},{11,12},{12,11},... | collective-permute-start | bytes 786440 | tf_op jit(solution)/shard_map/ppermute | solution.py:353
  12.2 0.1 collective-permute-start.4
  12.3 0.0 collective-permute-done.got_a
  12.4 0.0 collective-permute-done.1.got_b
  12.4 0.6 %shard_map.74 = (f32[312,128]{1,0:T(8,128)S(1)}, f32[2,144,128]{2,1,0:T(8,128)S(1)}, f32[11,144,128]{2,1,0:T(8,128)S(1)}) custom-call(f32[8,128,128]{2,1,0:T(8,128)S(1)} %get-tuple-element.23.conc, f32[8,128,128]{2,1,0:T(8,128)S(1)} %get-tuple-element.24.kappa, f32[8,128,128]{2,1,0:T(8,128)S(1)} %get-tuple-element.25.mixed, ...), custom_call_target="tpu_custom_call" | custom-call | flops 1024 | bytes 1024 | tf_op jit(solution)/shard_map/pallas_call | solution.py:393
  12.9 4.1 %collective-permute-start.3 = (f32[312,128]{1,0:T(8,128)S(1)}, f32[312,128]{1,0:T(8,128)S(1)}, u32[]{:S(2)}, u32[]{:S(2)}) collective-permute-start(f32[312,128]{1,0:T(8,128)S(1)} %get-tuple-element.36), channel_id=1, source_target_pairs={{1,2},{2,1},{3,4},{4,3},{5,6},{6,5},{9,10},{10,9},{11,12},{12,11},... | collective-permute-start | bytes 479240 | tf_op jit(solution)/shard_map/ppermute | solution.py:353
  17.1 0.4 %shard_map.76 = (f32[304,128]{1,0:T(8,128)S(1)}, f32[2,144,128]{2,1,0:T(8,128)S(1)}) custom-call(f32[8,128,128]{2,1,0:T(8,128)S(1)} %get-tuple-element.23.conc, f32[8,128,128]{2,1,0:T(8,128)S(1)} %get-tuple-element.24.kappa, f32[8,128,128]{2,1,0:T(8,128)S(1)} %get-tuple-element.25.mixed, f32[27,8,128]{2,1,0:T(8,128)S(1)} %collective-permute-done.got_a, ...), custom_call_target="tpu_custom_call" | custom-call | flops 1024 | bytes 1024 | tf_op jit(solution)/shard_map/pallas_call | solution.py:398
  17.5 0.1 collective-permute-start.5
  17.6 3.1 %shard_map.75 = (f32[8,128,128]{2,1,0:T(8,128)S(1)}, f32[2,2,64,128]{3,2,1,0:T(8,128)S(1)}, f32[2,10,144,128]{3,2,1,0:T(8,128)S(1)}, f32[2,5,144,128]{3,2,1,0:T(8,128)S(1)}, f32[2,10,144,128]{3,2,1,0:T(8,128)S(1)}) custom-call(f32[8,128,128]{2,1,0:T(8,128)S(1)} %get-tuple-element.23.conc, f32[8,128,128]{2,1,0:T(8,128)S(1)} %get-tuple-element.24.kappa, ...), custom_call_target="tpu_custom_call" | custom-call | flops 1024 | bytes 1024 | tf_op jit(solution)/shard_map/pallas_call | solution.py:402
  20.7 0.0 collective-permute-done.2.rest_0_.raw
  20.7 0.0 collective-permute-done.4.raw
  20.7 1.7 %collective-permute-done.5.late = f32[304,128]{1,0:T(8,128)S(1)} collective-permute-done((f32[304,128]{1,0:T(8,128)S(1)}, f32[304,128]{1,0:T(8,128)S(1)}, u32[]{:S(2)}, u32[]{:S(2)}) %collective-permute-start.5) | collective-permute-done | bytes 155680 | tf_op jit(solution)/shard_map/ppermute | solution.py:353
  22.4 0.8 %shard_map.77.rest_0_ = f32[2,3,64,128]{3,2,1,0:T(8,128)S(1)} custom-call(f32[2,10,144,128]{3,2,1,0:T(8,128)S(1)} %get-tuple-element.30.coef, f32[2,5,144,128]{3,2,1,0:T(8,128)S(1)} %get-tuple-element.31.av, f32[2,144,128]{2,1,0:T(8,128)S(1)} %get-tuple-element.37.edge_u, f32[2,10,144,128]{3,2,1,0:T(8,128)S(1)} %get-tuple-element.33.m_ref, ...), custom_call_target="tpu_custom_call" | custom-call | flops 1024 | bytes 1024 | tf_op jit(solution)/shard_map/pallas_call | solution.py:423
  23.2 0.0 collective-permute-done.3.late
  23.2 1.5 %shard_map.78 = f32[2,8,64,128]{3,2,1,0:T(8,128)} custom-call(f32[2,10,144,128]{3,2,1,0:T(8,128)S(1)} %get-tuple-element.30.coef, f32[2,5,144,128]{3,2,1,0:T(8,128)S(1)} %get-tuple-element.31.av, f32[2,144,128]{2,1,0:T(8,128)S(1)} %get-tuple-element.32.edge_u, f32[2,10,144,128]{3,2,1,0:T(8,128)S(1)} %get-tuple-element.33.m_ref, ...), custom_call_target="tpu_custom_call" | custom-call | flops 1024 | bytes 1024 | tf_op jit(solution)/shard_map/pallas_call | solution.py:423
Async XLA Ops:
  1.9 10.5 %collective-permute-start = (f32[27,8,128]{2,1,0:T(8,128)S(1)}, f32[27,8,128]{2,1,0:T(8,128)S(1)}, u32[]{:S(2)}, u32[]{:S(2)}) collective-permute-start(f32[27,8,128]{2,1,0:T(8,128)S(1)} %get-tuple-element.26), channel_id=1, source_target_pairs={{0,8},{8,0},{16,24},{24,16},{32,40},{40,32},{48,56},{56,48},{64,72... | collective-permute-start | bytes 331784 | tf_op jit(solution)/shard_map/ppermute | solution.py:353
  2.6 9.7 %collective-permute-start.1 = (f32[27,8,128]{2,1,0:T(8,128)S(1)}, f32[27,8,128]{2,1,0:T(8,128)S(1)}, u32[]{:S(2)}, u32[]{:S(2)}) collective-permute-start(f32[27,8,128]{2,1,0:T(8,128)S(1)} %get-tuple-element.27), channel_id=1, source_target_pairs={{8,16},{16,8},{24,32},{32,24},{40,48},{48,40},{56,64},{64,56},{72,... | collective-permute-start | bytes 331784 | tf_op jit(solution)/shard_map/ppermute | solution.py:353
  7.5 13.2 %collective-permute-start.2 = (f32[4,128,128]{2,1,0:T(8,128)S(1)}, f32[4,128,128]{2,1,0:T(8,128)S(1)}, u32[]{:S(2)}, u32[]{:S(2)}) collective-permute-start(f32[4,128,128]{2,1,0:T(8,128)S(1)} %get-tuple-element.35), channel_id=1, source_target_pairs={{1,2},{2,1},{3,4},{4,3},{5,6},{6,5},{9,10},{10,9},{11,12},{12,11},... | collective-permute-start | bytes 786440 | tf_op jit(solution)/shard_map/ppermute | solution.py:353
  12.2 8.4 %collective-permute-start.4 = (f32[4,128,128]{2,1,0:T(8,128)S(1)}, f32[4,128,128]{2,1,0:T(8,128)S(1)}, u32[]{:S(2)}, u32[]{:S(2)}) collective-permute-start(f32[4,128,128]{2,1,0:T(8,128)S(1)} %get-tuple-element.38), channel_id=1, source_target_pairs={{0,1},{1,0},{2,3},{3,2},{4,5},{5,4},{6,7},{7,6},{8,9},{9,8},{10,11... | collective-permute-start | bytes 786440 | tf_op jit(solution)/shard_map/ppermute | solution.py:353
  12.9 10.3 %collective-permute-start.3 = (f32[312,128]{1,0:T(8,128)S(1)}, f32[312,128]{1,0:T(8,128)S(1)}, u32[]{:S(2)}, u32[]{:S(2)}) collective-permute-start(f32[312,128]{1,0:T(8,128)S(1)} %get-tuple-element.36), channel_id=1, source_target_pairs={{1,2},{2,1},{3,4},{4,3},{5,6},{6,5},{9,10},{10,9},{11,12},{12,11},... | collective-permute-start | bytes 479240 | tf_op jit(solution)/shard_map/ppermute | solution.py:353
  17.5 4.9 %collective-permute-start.5 = (f32[304,128]{1,0:T(8,128)S(1)}, f32[304,128]{1,0:T(8,128)S(1)}, u32[]{:S(2)}, u32[]{:S(2)}) collective-permute-start(f32[304,128]{1,0:T(8,128)S(1)} %get-tuple-element.39), channel_id=1, source_target_pairs={{0,1},{1,0},{2,3},{3,2},{4,5},{5,4},{6,7},{7,6},{8,9},{9,8},{10,11... | collective-permute-start | bytes 466952 | tf_op jit(solution)/shard_map/ppermute | solution.py:353

commit v7 on v6

--- a/solution.py
+++ b/solution.py
@@ -14,7 +14,7 @@
 TALL = COLS + 2 * EDGE
 G_CONC, G_KAPPA, G_VT, G_FACE, GROUPS = 0, 8, 16, 24, 27
 RAW = 4
-LATE = 2 * COLS + (RAW + 2) * EDGE
+LATE = 2 * COLS + (RAW + 1) * EDGE
 
 
 def first_half(shape):
@@ -199,7 +199,15 @@
     for i, x in enumerate((u0, w0, c0, k0, k1, halves(v0, a0))):
         if i < 2:
             msg[pl.ds(i * COLS, COLS)] = x[EDGE : EDGE + COLS]
-        msg[pl.ds(2 * COLS + i * EDGE, EDGE)] = jnp.where(upper_half, x[EDGE + COLS :], x[:EDGE])
+        edges = jnp.where(upper_half, x[EDGE + COLS :], x[:EDGE])
+        if i == 0:
+            outer = edges
+        elif i == 1:
+            at = lax.broadcasted_iota(jnp.int32, (EDGE, LANES), 0)
+            inner = jnp.where(upper_half, pltpu.roll(edges, 2, 0), pltpu.roll(edges, EDGE - 2, 0))
+            msg[pl.ds(2 * COLS, EDGE)] = jnp.where((at < 2) | (at >= EDGE - 2), outer, inner)
+        else:
+            msg[pl.ds(2 * COLS + (i - 1) * EDGE, EDGE)] = edges
     if msg.shape[0] > LATE:
         msg[pl.ds(LATE, EDGE)] = jnp.zeros((EDGE, LANES), jnp.float32)
 
@@ -292,7 +300,10 @@
             send(joined.at[:, i], out.at[:, layer(faces_down(0), i)])
 
     def ghost(i, main):
-        edges = late[pl.ds(2 * COLS + i * EDGE, EDGE)]
+        edges = late[pl.ds(2 * COLS + max(i - 1, 0) * EDGE, EDGE)]
+        if i == 1:
+            at = lax.broadcasted_iota(jnp.int32, (EDGE, LANES), 0)
+            edges = jnp.where(at < EDGE // 2, pltpu.roll(edges, EDGE - 2, 0), pltpu.roll(edges, 2, 0))
         return jnp.concatenate([edges, main, edges], axis=0)
 
     ghost_c = [ghost(2, raw[0]), ghost(0, late[pl.ds(0, COLS)]), ghost(1, late[pl.ds(COLS, COLS)])]

time: 25.2 us -> 25.1 us (level)
  no operation moved by 1% of the time
where the time goes in v7:
time: 25.1 us; the launch traced here: 24.6 us
  starting transfers between devices  14.7 us (59%)
  Pallas kernels  8.23 us (33%)
  waiting for transfers between devices  1.61 us (6%)
    ppermute x6, starting transfers between devices, swap(): return lax.ppermute(value, axis, pairs)  14.7 us
    pallas_call x1, Pallas kernels, per_device(): call(block_kernel, (shape(DEPTH, *plane), shape(2, DEPTH - 6, *tile), sha...  3.05 us
    pallas_call x2, Pallas kernels, join(): call(functools.partial(join_kernel, parity), outs, in_specs=[whole] * (4...  2.34 us
    pallas_call x1, Pallas kernels, per_device(): call(pack_kernel, [shape(GROUPS, EDGE, LANES)] * 2 + [shape(RAW, *plane)]...  1.86 us
    ppermute x6, waiting for transfers between devices, swap(): return lax.ppermute(value, axis, pairs)  1.61 us
    pallas_call x1, Pallas kernels, per_device(): call(functools.partial(edge_kernel, 1), (shape(LATE + EDGE, LANES), shape...  0.55 us
  transfers between devices with their start and end apart: 6, of which 1 were waited for; matrix products, arithmetic and copies ran while one was open for 0% of the time, Pallas kernels for 20%

profile of v7, /device:TPU:121, one launch (start us, length us, event | category | flops | bytes accessed | tf_op | source)
XLA Modules:
  0.0 24.6 jit_solution(18102856512762257987)
XLA Ops:
  0.0 1.9 %shard_map.73 = (f32[27,8,128]{2,1,0:T(8,128)S(1)}, f32[27,8,128]{2,1,0:T(8,128)S(1)}, f32[4,128,128]{2,1,0:T(8,128)S(1)}, f32[4,128,128]{2,1,0:T(8,128)S(1)}, f...) custom-call(f32[2,8,64,128]{3,2,1,0:T(8,128)} %conc_in.1, ...), custom_call_target="tpu_custom_call" | custom-call | flops 1024 | bytes 1024 | tf_op jit(solution)/shard_map/pallas_call | solution.py:390
  1.9 0.8 %collective-permute-start = (f32[27,8,128]{2,1,0:T(8,128)S(1)}, f32[27,8,128]{2,1,0:T(8,128)S(1)}, u32[]{:S(2)}, u32[]{:S(2)}) collective-permute-start(f32[27,8,128]{2,1,0:T(8,128)S(1)} %get-tuple-element.26), channel_id=1, source_target_pairs={{0,8},{8,0},{16,24},{24,16},{32,40},{40,32},{48,56},{56,48},{64,72... | collective-permute-start | bytes 331784 | tf_op jit(solution)/shard_map/ppermute | solution.py:364
  2.6 4.8 %collective-permute-start.1 = (f32[27,8,128]{2,1,0:T(8,128)S(1)}, f32[27,8,128]{2,1,0:T(8,128)S(1)}, u32[]{:S(2)}, u32[]{:S(2)}) collective-permute-start(f32[27,8,128]{2,1,0:T(8,128)S(1)} %get-tuple-element.27), channel_id=1, source_target_pairs={{8,16},{16,8},{24,32},{32,24},{40,48},{48,40},{56,64},{64,56},{72,... | collective-permute-start | bytes 331784 | tf_op jit(solution)/shard_map/ppermute | solution.py:364
  7.5 4.8 %collective-permute-start.2 = (f32[4,128,128]{2,1,0:T(8,128)S(1)}, f32[4,128,128]{2,1,0:T(8,128)S(1)}, u32[]{:S(2)}, u32[]{:S(2)}) collective-permute-start(f32[4,128,128]{2,1,0:T(8,128)S(1)} %get-tuple-element.35), channel_id=1, source_target_pairs={{1,2},{2,1},{3,4},{4,3},{5,6},{6,5},{9,10},{10,9},{11,12},{12,11},... | collective-permute-start | bytes 786440 | tf_op jit(solution)/shard_map/ppermute | solution.py:364
  12.2 0.1 collective-permute-start.4
  12.3 0.0 collective-permute-done.got_a
  12.4 0.0 collective-permute-done.1.got_b
  12.4 0.6 %shard_map.74 = (f32[304,128]{1,0:T(8,128)S(1)}, f32[2,144,128]{2,1,0:T(8,128)S(1)}, f32[11,144,128]{2,1,0:T(8,128)S(1)}) custom-call(f32[8,128,128]{2,1,0:T(8,128)S(1)} %get-tuple-element.23.conc, f32[8,128,128]{2,1,0:T(8,128)S(1)} %get-tuple-element.24.kappa, f32[8,128,128]{2,1,0:T(8,128)S(1)} %get-tuple-element.25.mixed, ...), custom_call_target="tpu_custom_call" | custom-call | flops 1024 | bytes 1024 | tf_op jit(solution)/shard_map/pallas_call | solution.py:404
  12.9 4.1 %collective-permute-start.3 = (f32[304,128]{1,0:T(8,128)S(1)}, f32[304,128]{1,0:T(8,128)S(1)}, u32[]{:S(2)}, u32[]{:S(2)}) collective-permute-start(f32[304,128]{1,0:T(8,128)S(1)} %get-tuple-element.36), channel_id=1, source_target_pairs={{1,2},{2,1},{3,4},{4,3},{5,6},{6,5},{9,10},{10,9},{11,12},{12,11},... | collective-permute-start | bytes 466952 | tf_op jit(solution)/shard_map/ppermute | solution.py:364
  17.1 0.4 %shard_map.76 = (f32[296,128]{1,0:T(8,128)S(1)}, f32[2,144,128]{2,1,0:T(8,128)S(1)}) custom-call(f32[8,128,128]{2,1,0:T(8,128)S(1)} %get-tuple-element.23.conc, f32[8,128,128]{2,1,0:T(8,128)S(1)} %get-tuple-element.24.kappa, f32[8,128,128]{2,1,0:T(8,128)S(1)} %get-tuple-element.25.mixed, f32[27,8,128]{2,1,0:T(8,128)S(1)} %collective-permute-done.got_a, ...), custom_call_target="tpu_custom_call" | custom-call | flops 1024 | bytes 1024 | tf_op jit(solution)/shard_map/pallas_call | solution.py:409
  17.5 0.1 collective-permute-start.5
  17.6 3.1 %shard_map.75 = (f32[8,128,128]{2,1,0:T(8,128)S(1)}, f32[2,2,64,128]{3,2,1,0:T(8,128)S(1)}, f32[2,10,144,128]{3,2,1,0:T(8,128)S(1)}, f32[2,5,144,128]{3,2,1,0:T(8,128)S(1)}, f32[2,10,144,128]{3,2,1,0:T(8,128)S(1)}) custom-call(f32[8,128,128]{2,1,0:T(8,128)S(1)} %get-tuple-element.23.conc, f32[8,128,128]{2,1,0:T(8,128)S(1)} %get-tuple-element.24.kappa, ...), custom_call_target="tpu_custom_call" | custom-call | flops 1024 | bytes 1024 | tf_op jit(solution)/shard_map/pallas_call | solution.py:413
  20.6 0.0 collective-permute-done.2.rest_0_.raw
  20.7 0.0 collective-permute-done.4.raw
  20.7 1.6 %collective-permute-done.5.late = f32[296,128]{1,0:T(8,128)S(1)} collective-permute-done((f32[296,128]{1,0:T(8,128)S(1)}, f32[296,128]{1,0:T(8,128)S(1)}, u32[]{:S(2)}, u32[]{:S(2)}) %collective-permute-start.5) | collective-permute-done | bytes 151584 | tf_op jit(solution)/shard_map/ppermute | solution.py:364
  22.3 0.8 %shard_map.77.rest_0_ = f32[2,3,64,128]{3,2,1,0:T(8,128)S(1)} custom-call(f32[2,10,144,128]{3,2,1,0:T(8,128)S(1)} %get-tuple-element.30.coef, f32[2,5,144,128]{3,2,1,0:T(8,128)S(1)} %get-tuple-element.31.av, f32[2,144,128]{2,1,0:T(8,128)S(1)} %get-tuple-element.37.edge_u, f32[2,10,144,128]{3,2,1,0:T(8,128)S(1)} %get-tuple-element.33.m_ref, ...), custom_call_target="tpu_custom_call" | custom-call | flops 1024 | bytes 1024 | tf_op jit(solution)/shard_map/pallas_call | solution.py:434
  23.1 0.0 collective-permute-done.3.late
  23.1 1.5 %shard_map.78 = f32[2,8,64,128]{3,2,1,0:T(8,128)} custom-call(f32[2,10,144,128]{3,2,1,0:T(8,128)S(1)} %get-tuple-element.30.coef, f32[2,5,144,128]{3,2,1,0:T(8,128)S(1)} %get-tuple-element.31.av, f32[2,144,128]{2,1,0:T(8,128)S(1)} %get-tuple-element.32.edge_u, f32[2,10,144,128]{3,2,1,0:T(8,128)S(1)} %get-tuple-element.33.m_ref, ...), custom_call_target="tpu_custom_call" | custom-call | flops 1024 | bytes 1024 | tf_op jit(solution)/shard_map/pallas_call | solution.py:434
Async XLA Ops:
  1.9 10.5 %collective-permute-start = (f32[27,8,128]{2,1,0:T(8,128)S(1)}, f32[27,8,128]{2,1,0:T(8,128)S(1)}, u32[]{:S(2)}, u32[]{:S(2)}) collective-permute-start(f32[27,8,128]{2,1,0:T(8,128)S(1)} %get-tuple-element.26), channel_id=1, source_target_pairs={{0,8},{8,0},{16,24},{24,16},{32,40},{40,32},{48,56},{56,48},{64,72... | collective-permute-start | bytes 331784 | tf_op jit(solution)/shard_map/ppermute | solution.py:364
  2.6 9.7 %collective-permute-start.1 = (f32[27,8,128]{2,1,0:T(8,128)S(1)}, f32[27,8,128]{2,1,0:T(8,128)S(1)}, u32[]{:S(2)}, u32[]{:S(2)}) collective-permute-start(f32[27,8,128]{2,1,0:T(8,128)S(1)} %get-tuple-element.27), channel_id=1, source_target_pairs={{8,16},{16,8},{24,32},{32,24},{40,48},{48,40},{56,64},{64,56},{72,... | collective-permute-start | bytes 331784 | tf_op jit(solution)/shard_map/ppermute | solution.py:364
  7.5 13.2 %collective-permute-start.2 = (f32[4,128,128]{2,1,0:T(8,128)S(1)}, f32[4,128,128]{2,1,0:T(8,128)S(1)}, u32[]{:S(2)}, u32[]{:S(2)}) collective-permute-start(f32[4,128,128]{2,1,0:T(8,128)S(1)} %get-tuple-element.35), channel_id=1, source_target_pairs={{1,2},{2,1},{3,4},{4,3},{5,6},{6,5},{9,10},{10,9},{11,12},{12,11},... | collective-permute-start | bytes 786440 | tf_op jit(solution)/shard_map/ppermute | solution.py:364
  12.2 8.4 %collective-permute-start.4 = (f32[4,128,128]{2,1,0:T(8,128)S(1)}, f32[4,128,128]{2,1,0:T(8,128)S(1)}, u32[]{:S(2)}, u32[]{:S(2)}) collective-permute-start(f32[4,128,128]{2,1,0:T(8,128)S(1)} %get-tuple-element.38), channel_id=1, source_target_pairs={{0,1},{1,0},{2,3},{3,2},{4,5},{5,4},{6,7},{7,6},{8,9},{9,8},{10,11... | collective-permute-start | bytes 786440 | tf_op jit(solution)/shard_map/ppermute | solution.py:364
  12.9 10.2 %collective-permute-start.3 = (f32[304,128]{1,0:T(8,128)S(1)}, f32[304,128]{1,0:T(8,128)S(1)}, u32[]{:S(2)}, u32[]{:S(2)}) collective-permute-start(f32[304,128]{1,0:T(8,128)S(1)} %get-tuple-element.36), channel_id=1, source_target_pairs={{1,2},{2,1},{3,4},{4,3},{5,6},{6,5},{9,10},{10,9},{11,12},{12,11},... | collective-permute-start | bytes 466952 | tf_op jit(solution)/shard_map/ppermute | solution.py:364
  17.5 4.8 %collective-permute-start.5 = (f32[296,128]{1,0:T(8,128)S(1)}, f32[296,128]{1,0:T(8,128)S(1)}, u32[]{:S(2)}, u32[]{:S(2)}) collective-permute-start(f32[296,128]{1,0:T(8,128)S(1)} %get-tuple-element.39), channel_id=1, source_target_pairs={{0,1},{1,0},{2,3},{3,2},{4,5},{5,4},{6,7},{7,6},{8,9},{9,8},{10,11... | collective-permute-start | bytes 454664 | tf_op jit(solution)/shard_map/ppermute | solution.py:364
